TPU v7x, 32 devices: a whole 2x2x4 slice. The times are simulated.
32 devices in a mesh: dp: 8 (over z, x), fsdp: 4 (over y, core).
Axes of the slice: x: 2, y: 2, z: 4, core: 2. Of those that a mesh axis runs over, the one named last changes fastest.
Arguments:
- inputs: bfloat16 [64, 8, 16, 1152], P(('dp', 'fsdp')), may hold values from -6 to 6
- out_cotangent: bfloat16 [64, 8, 16, 1152], P(('dp', 'fsdp')), may hold values from -6 to 6
- lengths: int32 [64], P(('dp', 'fsdp')), may hold values from 8 to 16, as said below
- timesteps: int32 [64], P(('dp', 'fsdp')), may hold values from 0 to 999
- labels: int32 [64], P(('dp', 'fsdp')), may hold values from 0 to 100
- time_table: bfloat16 [1000, 1152], replicated, may hold values from -6 to 6
- class_table: bfloat16 [101, 1152], replicated, may hold values from -6 to 6
- ada_weight: bfloat16 [1152, 6912], P('fsdp', 'dp'), may hold values from -0.1875 to 0.1875
- qkv_weight: bfloat16 [1152, 3456], P('fsdp', 'dp'), may hold values from -0.1875 to 0.1875
- proj_weight: bfloat16 [1152, 1152], P('fsdp', 'dp'), may hold values from -0.625 to 0.625
- up_weight: bfloat16 [1152, 4608], P('fsdp', 'dp'), may hold values from -0.1875 to 0.1875
- down_weight: bfloat16 [4608, 1152], P('fsdp', 'dp'), may hold values from -0.09375 to 0.09375
Outputs:
- activations: bfloat16 [64, 8, 16, 1152], P(('dp', 'fsdp'))
- input_grad: bfloat16 [64, 8, 16, 1152], P(('dp', 'fsdp'))
- ada_grad: float32 [1152, 6912], P('fsdp', 'dp')
- qkv_grad: float32 [1152, 3456], P('fsdp', 'dp')
- proj_grad: float32 [1152, 1152], P('fsdp', 'dp')
- up_grad: float32 [1152, 4608], P('fsdp', 'dp')
- down_grad: float32 [4608, 1152], P('fsdp', 'dp')
Inputs may be any that keep to these rules, and one draw needn't show every extreme that they name: `lengths`: every clip has 8 to 16 live frames; some clip has exactly 16 and some exactly 8.
All inputs are finite; a program needn't handle non-finite values.
Results may differ from a plain program's by a relative error of at most 0.019.
The roundings to bfloat16 on the way count: a program that leaves them out, or rounds other values in their place, can miss the bound.
Values may be sent and summed in bfloat16 or wider, within the bound.
No kernel may reach another device: no remote copies, remote signals or barrier semaphores. Data moves between devices by JAX's collectives and lax.ppermute only.
A program may use at most 256 MiB of HBM per device.

v0:
```python
import math

import jax
import jax.numpy as jnp
from jax import lax
from jax.sharding import PartitionSpec as P

HEADS = 16


def norm_mod(values, shift_add, scale_mul):
    center = values - jnp.mean(values, -1, keepdims=True)
    spread = jnp.mean(center * center, -1, keepdims=True)
    return center * lax.rsqrt(spread + 1e-06) * (1.0 + scale_mul) + shift_add


def gelu_tanh(values):
    return jax.nn.gelu(values, approximate=True)


def gather_five(shards):
    row_set = (
        lax.all_gather(shards[0], "fsdp", axis=0, tiled=True),
        lax.all_gather(shards[1], "fsdp", axis=0, tiled=True),
        lax.all_gather(shards[2], "fsdp", axis=0, tiled=True),
        lax.all_gather(shards[3], "fsdp", axis=0, tiled=True),
        lax.all_gather(shards[4], "fsdp", axis=0, tiled=True),
    )
    return (
        lax.all_gather(row_set[0], "dp", axis=1, tiled=True),
        lax.all_gather(row_set[1], "dp", axis=1, tiled=True),
        lax.all_gather(row_set[2], "dp", axis=1, tiled=True),
        lax.all_gather(row_set[3], "dp", axis=1, tiled=True),
        lax.all_gather(row_set[4], "dp", axis=1, tiled=True),
    )


def scatter_five(totals):
    row_set = (
        lax.psum_scatter(
            totals[0].astype(jnp.bfloat16), "fsdp", scatter_dimension=0, tiled=True
        ).astype(jnp.float32),
        lax.psum_scatter(
            totals[1].astype(jnp.bfloat16), "fsdp", scatter_dimension=0, tiled=True
        ).astype(jnp.float32),
        lax.psum_scatter(
            totals[2].astype(jnp.bfloat16), "fsdp", scatter_dimension=0, tiled=True
        ).astype(jnp.float32),
        lax.psum_scatter(
            totals[3].astype(jnp.bfloat16), "fsdp", scatter_dimension=0, tiled=True
        ).astype(jnp.float32),
        lax.psum_scatter(
            totals[4].astype(jnp.bfloat16), "fsdp", scatter_dimension=0, tiled=True
        ).astype(jnp.float32),
    )
    return (
        lax.psum_scatter(
            row_set[0].astype(jnp.bfloat16), "dp", scatter_dimension=1, tiled=True
        ).astype(jnp.float32),
        lax.psum_scatter(
            row_set[1].astype(jnp.bfloat16), "dp", scatter_dimension=1, tiled=True
        ).astype(jnp.float32),
        lax.psum_scatter(
            row_set[2].astype(jnp.bfloat16), "dp", scatter_dimension=1, tiled=True
        ).astype(jnp.float32),
        lax.psum_scatter(
            row_set[3].astype(jnp.bfloat16), "dp", scatter_dimension=1, tiled=True
        ).astype(jnp.float32),
        lax.psum_scatter(
            row_set[4].astype(jnp.bfloat16), "dp", scatter_dimension=1, tiled=True
        ).astype(jnp.float32),
    )


def fetch_weights(ada_weight, core_shards):
    return tuple(gather_five((ada_weight,) + tuple(core_shards)))


def matmul_tn(left, right):
    return lax.dot_general(
        left, right, (((0,), (0,)), ((), ())), preferred_element_type=jnp.float32
    )


def matmul_nt(left, right):
    return lax.dot_general(
        left, right, (((1,), (1,)), ((), ())), preferred_element_type=jnp.float32
    )


def body(
    inputs,
    out_cotangent,
    lengths,
    timesteps,
    labels,
    time_table,
    class_table,
    ada_weight,
    qkv_weight,
    proj_weight,
    up_weight,
    down_weight,
):
    core_shards = (qkv_weight, proj_weight, up_weight, down_weight)
    clip_count, positions, frames, model_width = inputs.shape
    row_count = clip_count * positions * frames
    seq_count = clip_count * positions
    span = positions * frames
    head_size = model_width // HEADS
    attn_scale = 1.0 / math.sqrt(head_size)
    ada_full, qkv_full, proj_full, up_full, down_full = fetch_weights(ada_weight, core_shards)
    time_onehot = (timesteps[:, None] == lax.iota(jnp.int32, time_table.shape[0])[None, :]).astype(
        jnp.bfloat16
    )
    class_onehot = (labels[:, None] == lax.iota(jnp.int32, class_table.shape[0])[None, :]).astype(
        jnp.bfloat16
    )
    embedded = jnp.dot(time_onehot, time_table, preferred_element_type=jnp.float32) + jnp.dot(
        class_onehot, class_table, preferred_element_type=jnp.float32
    )
    cond_low = jax.nn.silu(embedded).astype(jnp.bfloat16)
    modulation = jnp.dot(cond_low, ada_full, preferred_element_type=jnp.float32)
    pieces = [
        modulation[:, None, offset * model_width : (offset + 1) * model_width]
        for offset in range(6)
    ]
    shift_one, scale_one, gate_one, shift_two, scale_two, gate_two = pieces
    residual = inputs.astype(jnp.float32).reshape(clip_count, span, model_width)
    hidden_one = (
        norm_mod(residual, shift_one, scale_one)
        .astype(jnp.bfloat16)
        .reshape(row_count, model_width)
    )
    mixed = jnp.dot(hidden_one, qkv_full, preferred_element_type=jnp.float32).astype(jnp.bfloat16)
    shaped = mixed.reshape(seq_count, frames, 3, HEADS, head_size)
    queries = shaped[:, :, 0]
    key_part = shaped[:, :, 1]
    value_part = shaped[:, :, 2]
    clip_live = lax.iota(jnp.int32, frames)[None, :] < lengths[:, None]
    key_live = jnp.repeat(clip_live, positions, axis=0)
    scores = (
        jnp.einsum("sqhe,skhe->shqk", queries, key_part, preferred_element_type=jnp.float32)
        * attn_scale
    )
    scores = jnp.where(key_live[:, None, None, :], scores, -1e30)
    row_max = jnp.max(scores, -1, keepdims=True)
    exp_scores = jnp.exp(scores - row_max)
    attn_probs = exp_scores / jnp.sum(exp_scores, -1, keepdims=True)
    probs_low = attn_probs.astype(jnp.bfloat16)
    attended = jnp.einsum(
        "shqk,skhe->sqhe", probs_low, value_part, preferred_element_type=jnp.float32
    )
    attended_low = attended.astype(jnp.bfloat16).reshape(row_count, model_width)
    branch = jnp.dot(attended_low, proj_full, preferred_element_type=jnp.float32).reshape(
        clip_count, span, model_width
    )
    middle = residual + gate_one * branch
    hidden_two = (
        norm_mod(middle, shift_two, scale_two).astype(jnp.bfloat16).reshape(row_count, model_width)
    )
    up_proj = jnp.dot(hidden_two, up_full, preferred_element_type=jnp.float32)
    activ_low = gelu_tanh(up_proj).astype(jnp.bfloat16)
    ffn_out = jnp.dot(activ_low, down_full, preferred_element_type=jnp.float32).reshape(
        clip_count, span, model_width
    )
    result = (middle + gate_two * ffn_out).astype(jnp.bfloat16).reshape(inputs.shape)
    ada_full, qkv_full, proj_full, up_full, down_full = fetch_weights(ada_weight, core_shards)
    grad_out = out_cotangent.astype(jnp.float32).reshape(clip_count, span, model_width)
    d_gate_two = jnp.sum(grad_out * ffn_out, axis=1)
    d_ffn = (grad_out * gate_two).astype(jnp.bfloat16).reshape(row_count, model_width)
    d_activ = matmul_nt(d_ffn, down_full)
    down_total = matmul_tn(activ_low, d_ffn)
    gelu_value, gelu_pull = jax.vjp(gelu_tanh, up_proj)
    d_up = gelu_pull(d_activ)[0].astype(jnp.bfloat16)
    d_hidden_two = matmul_nt(d_up, up_full)
    up_total = matmul_tn(hidden_two, d_up)
    norm_value, norm_pull = jax.vjp(norm_mod, middle, shift_two, scale_two)
    d_middle_norm, d_shift_two, d_scale_two = norm_pull(
        d_hidden_two.reshape(clip_count, span, model_width)
    )
    d_middle = grad_out + d_middle_norm
    d_gate_one = jnp.sum(d_middle * branch, axis=1)
    d_branch = (d_middle * gate_one).astype(jnp.bfloat16).reshape(row_count, model_width)
    d_attended = (
        matmul_nt(d_branch, proj_full)
        .astype(jnp.bfloat16)
        .reshape(seq_count, frames, HEADS, head_size)
    )
    proj_total = matmul_tn(attended_low, d_branch)
    d_value = jnp.einsum(
        "shqk,sqhe->skhe", probs_low, d_attended, preferred_element_type=jnp.float32
    )
    d_probs = jnp.einsum(
        "sqhe,skhe->shqk", d_attended, value_part, preferred_element_type=jnp.float32
    )
    d_scores = attn_probs * (d_probs - jnp.sum(attn_probs * d_probs, -1, keepdims=True))
    d_scores_low = d_scores.astype(jnp.bfloat16)
    d_query = (
        jnp.einsum("shqk,skhe->sqhe", d_scores_low, key_part, preferred_element_type=jnp.float32)
        * attn_scale
    )
    d_key = (
        jnp.einsum("shqk,sqhe->skhe", d_scores_low, queries, preferred_element_type=jnp.float32)
        * attn_scale
    )
    d_mixed = (
        jnp.stack([d_query, d_key, d_value], axis=2)
        .astype(jnp.bfloat16)
        .reshape(row_count, 3 * model_width)
    )
    d_hidden_one = matmul_nt(d_mixed, qkv_full)
    qkv_total = matmul_tn(hidden_one, d_mixed)
    norm_first, first_pull = jax.vjp(norm_mod, residual, shift_one, scale_one)
    d_input_norm, d_shift_one, d_scale_one = first_pull(
        d_hidden_one.reshape(clip_count, span, model_width)
    )
    input_grad = (d_middle + d_input_norm).astype(jnp.bfloat16).reshape(inputs.shape)
    d_modulation = jnp.concatenate(
        [
            d_shift_one[:, 0],
            d_scale_one[:, 0],
            d_gate_one,
            d_shift_two[:, 0],
            d_scale_two[:, 0],
            d_gate_two,
        ],
        axis=-1,
    )
    ada_total = jnp.dot(
        cond_low.astype(jnp.float32).T, d_modulation, precision=lax.Precision.HIGHEST
    )
    ada_grad, qkv_grad, proj_grad, up_grad, down_grad = scatter_five(
        (ada_total, qkv_total, proj_total, up_total, down_total)
    )
    return (result, input_grad, ada_grad, qkv_grad, proj_grad, up_grad, down_grad)


def solution(mesh):
    return jax.shard_map(
        body,
        mesh=mesh,
        in_specs=(
            P(("dp", "fsdp"), None, None, None),
            P(("dp", "fsdp"), None, None, None),
            P(("dp", "fsdp")),
            P(("dp", "fsdp")),
            P(("dp", "fsdp")),
            P(),
            P(),
            P("fsdp", "dp"),
            P("fsdp", "dp"),
            P("fsdp", "dp"),
            P("fsdp", "dp"),
            P("fsdp", "dp"),
        ),
        out_specs=(
            P(("dp", "fsdp"), None, None, None),
            P(("dp", "fsdp"), None, None, None),
            P("fsdp", "dp"),
            P("fsdp", "dp"),
            P("fsdp", "dp"),
            P("fsdp", "dp"),
            P("fsdp", "dp"),
        ),
        check_vma=False,
    )
```

profile of v0, /device:TPU:0, one launch (start us, length us, event | category | flops | bytes accessed | tf_op | source)
XLA Modules:
  0.0 1629.2 jit_solution(7630973754781885323)
XLA Ops:
  9.4 25.3 %all-gather.10.cloned.1.call-done = bf16[1152,864]{1,0:T(8,128)(2,1)} async-done(((bf16[288,864]{1,0:T(8,128)(2,1)}), bf16[1152,864]{1,0:T(8,128)(2,1)}) %all-gather.10.cloned.1.call-update) | async-done | bytes 1990672 | tf_op jit(solution)/shard_map/all_gather | solution.py:23
  38.9 14.4 all_gather.40
  54.8 7.1 all-gather
  64.0 14.2 all-gather.18.cloned.1.call-done
  84.7 212.8 %all-gather.12.cloned.1.call-done = bf16[1152,6912]{0,1:T(8,128)(2,1)} async-done(((bf16[1152,864]{0,1:T(8,128)(2,1)}), bf16[1152,6912]{0,1:T(8,128)(2,1)}) %all-gather.12.cloned.1.call-update) | async-done | bytes 15925264 | tf_op jit(solution)/shard_map/all_gather | solution.py:30
  297.5 9.7 fusion.56
  308.2 109.7 %all-gather.14.cloned.1.call-done = bf16[1152,3456]{0,1:T(8,128)(2,1)} async-done(((bf16[1152,432]{0,1:T(8,128)(2,1)}), bf16[1152,3456]{0,1:T(8,128)(2,1)}) %all-gather.14.cloned.1.call-update) | async-done | bytes 7962640 | tf_op jit(solution)/shard_map/all_gather | solution.py:31
  444.2 29.5 %all-gather.16.cloned.1.call-done = bf16[1152,1152]{0,1:T(8,128)(2,1)} async-done(((bf16[1152,144]{0,1:T(8,128)(2,1)}), bf16[1152,1152]{0,1:T(8,128)(2,1)}) %all-gather.16.cloned.1.call-update) | async-done | bytes 2654224 | tf_op jit(solution)/shard_map/all_gather | solution.py:32
  478.2 148.8 %all-gather.24.cloned.1.call-done = bf16[4608,1152]{0,1:T(8,128)(2,1)} async-done(((bf16[4608,144]{0,1:T(8,128)(2,1)}), bf16[4608,1152]{0,1:T(8,128)(2,1)}) %all-gather.24.cloned.1.call-update) | async-done | bytes 10616848 | tf_op jit(solution)/shard_map/all_gather | solution.py:34
  627.0 8.9 fusion.57
  635.9 144.0 %all-gather.20.cloned.1.call-done = bf16[1152,4608]{0,1:T(8,128)(2,1)} async-done(((bf16[1152,576]{0,1:T(8,128)(2,1)}), bf16[1152,4608]{0,1:T(8,128)(2,1)}) %all-gather.20.cloned.1.call-update) | async-done | bytes 10616848 | tf_op jit(solution)/shard_map/all_gather | solution.py:33
  779.9 10.8 fusion.9
  795.0 10.1 multiply_reduce_fusion.1
  858.5 11.5 convolution_convert_fusion.1
  870.8 15.4 convolution_convert_fusion
  888.7 27.9 %reduce-scatter.23.cloned.1.call-done = bf16[288,3456]{1,0:T(8,128)(2,1)} async-done(((bf16[1152,3456]{1,0:T(8,128)(2,1)}), bf16[288,3456]{1,0:T(8,128)(2,1)}) %reduce-scatter.23.cloned.1.call-update) | async-done | bytes 1990672 | tf_op jit(solution)/shard_map/reduce_scatter | solution.py:43
  920.8 84.7 %reduce-scatter.27.cloned.1.call-done = bf16[288,4608]{1,0:T(8,128)(2,1)} async-done(((bf16[1152,4608]{1,0:T(8,128)(2,1)}), bf16[288,4608]{1,0:T(8,128)(2,1)}) %reduce-scatter.27.cloned.1.call-update) | async-done | bytes 2654224 | tf_op jit(solution)/shard_map/reduce_scatter | solution.py:49
  1010.4 84.0 %reduce-scatter.29.cloned.1.call-done = bf16[1152,1152]{1,0:T(8,128)(2,1)} async-done(((bf16[4608,1152]{1,0:T(8,128)(2,1)}), bf16[1152,1152]{1,0:T(8,128)(2,1)}) %reduce-scatter.29.cloned.1.call-update) | async-done | bytes 2654224 | tf_op jit(solution)/shard_map/reduce_scatter | solution.py:52
  1099.7 118.6 %reduce-scatter.21.cloned.1.call-done = bf16[288,6912]{1,0:T(8,128)(2,1)} async-done(((bf16[1152,6912]{1,0:T(8,128)(2,1)}), bf16[288,6912]{1,0:T(8,128)(2,1)}) %reduce-scatter.21.cloned.1.call-update) | async-done | bytes 3981328 | tf_op jit(solution)/shard_map/reduce_scatter | solution.py:40
  1224.9 58.2 %reduce-scatter.35.cloned.1.call-done = bf16[144,288]{1,0:T(8,128)(2,1)} async-done(((bf16[1152,288]{1,0:T(8,128)(2,1)}), bf16[144,288]{1,0:T(8,128)(2,1)}) %reduce-scatter.35.cloned.1.call-update) | async-done | bytes 82960
  1285.0 71.2 %reduce-scatter.33.cloned.1.call-done = bf16[432,288]{1,0:T(8,128)(2,1)} async-done(((bf16[3456,288]{1,0:T(8,128)(2,1)}), bf16[432,288]{1,0:T(8,128)(2,1)}) %reduce-scatter.33.cloned.1.call-update) | async-done | bytes 248848
  1358.2 80.1 %reduce-scatter.37.cloned.1.call-done = bf16[576,288]{1,0:T(8,128)(2,1)} async-done(((bf16[4608,288]{1,0:T(8,128)(2,1)}), bf16[576,288]{1,0:T(8,128)(2,1)}) %reduce-scatter.37.cloned.1.call-update) | async-done | bytes 331792
  1440.4 72.3 %reduce-scatter.39.cloned.1.call-done = bf16[144,1152]{1,0:T(8,128)(2,1)} async-done(((bf16[1152,1152]{1,0:T(8,128)(2,1)}), bf16[144,1152]{1,0:T(8,128)(2,1)}) %reduce-scatter.39.cloned.1.call-update) | async-done | bytes 331792
  1515.1 104.3 %reduce-scatter.31.cloned.1.call-done = bf16[864,288]{1,0:T(8,128)(2,1)} async-done(((bf16[6912,288]{1,0:T(8,128)(2,1)}), bf16[864,288]{1,0:T(8,128)(2,1)}) %reduce-scatter.31.cloned.1.call-update) | async-done | bytes 497680
  (200 shorter events, 140.3 us)
Async XLA Ops:
  7.2 27.5 %all-gather.10.cloned.1.call-start = ((), (), s32[]{:S(2)}) async-start(), calls=%async_computation.10 | async-start | bytes 2580480 | tf_op jit(solution)/shard_map/all_gather | solution.py:23
  7.9 55.3 %all-gather.22.cloned.1.call-start = ((), (), s32[]{:S(2)}) async-start(), calls=%async_computation.16 | async-start | bytes 1658880 | tf_op jit(solution)/shard_map/all_gather | solution.py:27
  8.7 69.6 %all-gather.18.cloned.1.call-start = ((), (), s32[]{:S(2)}) async-start(), calls=%async_computation.14 | async-start | bytes 1843200 | tf_op jit(solution)/shard_map/all_gather | solution.py:26
  9.4 288.1 %all-gather.12.cloned.1.call-start = ((), (), s32[]{:S(2)}) async-start(), calls=%async_computation.11 | async-start | bytes 17915904 | tf_op jit(solution)/shard_map/all_gather | solution.py:30
  38.8 379.1 %all-gather.14.cloned.1.call-start = ((), (), s32[]{:S(2)}) async-start(), calls=%async_computation.12 | async-start | bytes 8957952 | tf_op jit(solution)/shard_map/all_gather | solution.py:31
  54.8 419.0 %all-gather.16.cloned.1.call-start = ((), (), s32[]{:S(2)}) async-start(), calls=%async_computation.13 | async-start | bytes 2985984 | tf_op jit(solution)/shard_map/all_gather | solution.py:32
  63.2 563.9 %all-gather.24.cloned.1.call-start = ((), (), s32[]{:S(2)}) async-start(), calls=%async_computation.17 | async-start | bytes 11943936 | tf_op jit(solution)/shard_map/all_gather | solution.py:34
  63.9 715.9 %all-gather.20.cloned.1.call-start = ((), (), s32[]{:S(2)}) async-start(), calls=%async_computation.15 | async-start | bytes 11943936 | tf_op jit(solution)/shard_map/all_gather | solution.py:33
  80.9 805.4 %reduce-scatter.25.cloned.1.call-start = ((), (), s32[]{:S(2)}) async-start(), calls=%async_computation.20 | async-start | bytes 3317760 | tf_op jit(solution)/shard_map/reduce_scatter | solution.py:46
  84.6 222.6 %copy-start.30 = (bf16[2,1152]{1,0:T(2,128)(2,1)}, bf16[2,1152]{1,0:T(2,128)(2,1)S(1)}, u32[]{:S(2)}) copy-start(bf16[2,1152]{1,0:T(2,128)(2,1)S(1)} %fusion.41) | copy-start | bytes 13828
  84.6 223.2 %copy-start.33 = (f32[256]{0:T(256)S(1)}, f32[256]{0:T(256)}, u32[]{:S(2)}) copy-start(f32[256]{0:T(256)} %div.58) | copy-start | bytes 3076
  84.6 223.2 %copy-start.34 = (f32[256]{0:T(256)S(1)}, f32[256]{0:T(256)}, u32[]{:S(2)}) copy-start(f32[256]{0:T(256)} %rsqrt.29) | copy-start | bytes 3076
  477.6 149.4 %copy-start.22 = (bf16[256,1152]{1,0:T(8,128)(2,1)S(1)}, bf16[256,1152]{1,0:T(8,128)(2,1)}, u32[]{:S(2)}) copy-start(bf16[256,1152]{1,0:T(8,128)(2,1)} %fusion.14) | copy-start | bytes 1769476
  478.2 301.7 %copy-start.16 = (bf16[2,128,1152]{2,1,0:T(8,128)(2,1)}, bf16[2,128,1152]{2,1,0:T(8,128)(2,1)S(1)}, u32[]{:S(2)}) copy-start(bf16[2,128,1152]{2,1,0:T(8,128)(2,1)S(1)} %add_convert_fusion.2) | copy-start | bytes 1769476
  810.4 106.2 %reduce-scatter.23.cloned.1.call-start = ((), (), s32[]{:S(2)}) async-start(), calls=%async_computation.19 | async-start | bytes 9953280 | tf_op jit(solution)/shard_map/reduce_scatter | solution.py:43
  848.8 156.7 %reduce-scatter.27.cloned.1.call-start = ((), (), s32[]{:S(2)}) async-start(), calls=%async_computation.21 | async-start | bytes 13271040 | tf_op jit(solution)/shard_map/reduce_scatter | solution.py:49
  857.2 237.2 %reduce-scatter.29.cloned.1.call-start = ((), (), s32[]{:S(2)}) async-start(), calls=%async_computation.22 | async-start | bytes 13271040 | tf_op jit(solution)/shard_map/reduce_scatter | solution.py:52
  870.0 348.3 %reduce-scatter.21.cloned.1.call-start = ((), (), s32[]{:S(2)}) async-start(), calls=%async_computation.18 | async-start | bytes 19906560 | tf_op jit(solution)/shard_map/reduce_scatter | solution.py:40
  886.2 397.0 %reduce-scatter.35.cloned.1.call-start = ((), (), s32[]{:S(2)}) async-start(), calls=%async_computation.25 | async-start | bytes 995328
  888.6 467.6 %reduce-scatter.33.cloned.1.call-start = ((), (), s32[]{:S(2)}) async-start(), calls=%async_computation.24 | async-start | bytes 2985984
  920.8 517.5 %reduce-scatter.37.cloned.1.call-start = ((), (), s32[]{:S(2)}) async-start(), calls=%async_computation.26 | async-start | bytes 3981312
  1010.3 502.4 %reduce-scatter.39.cloned.1.call-start = ((), (), s32[]{:S(2)}) async-start(), calls=%async_computation.27 | async-start | bytes 2985984
  1099.6 519.8 %reduce-scatter.31.cloned.1.call-start = ((), (), s32[]{:S(2)}) async-start(), calls=%async_computation.23 | async-start | bytes 5971968
  1512.7 109.1 %copy-start.1 = (bf16[1000,1152]{1,0:T(8,128)(2,1)S(1)}, bf16[1000,1152]{1,0:T(8,128)(2,1)}, u32[]{:S(2)}) copy-start(bf16[1000,1152]{1,0:T(8,128)(2,1)} %param.17) | copy-start | bytes 6912004
  (35 other events, 220.2 us)
Sparse Core Ops, SparseCore 0:
  9.6 25.0 all-gather.9
  36.3 21.1 all-gather.21
  59.1 19.0 all-gather.17
  80.3 217.1 all-gather.11
  300.1 117.7 all-gather.13
  420.5 53.1 all-gather.15
  475.9 151.0 all-gather.23
  629.2 150.6 all-gather.19
  810.5 33.1 reduce-scatter.24
  848.9 67.5 reduce-scatter.22
  919.4 86.1 reduce-scatter.26
  1008.2 86.1 reduce-scatter.28
  1097.2 121.1 reduce-scatter.20
  1222.2 60.9 reduce-scatter.34
  1286.7 69.4 reduce-scatter.32
  1360.1 78.1 reduce-scatter.36
  1442.3 70.4 reduce-scatter.38
  1516.2 103.2 reduce-scatter.30
where the time goes:
time: 1640 us; the launch traced here: 1630 us
  waiting for transfers between devices  1390 us (85%)
  matrix products  113 us (7%)
  local copies, waits for them, and re-layouts  76.2 us (5%)
  blocking collectives  21.5 us (1%)
    unnamed x23, waiting for transfers between devices  389 us
    all_gather x1, waiting for transfers between devices, gather_five(): lax.all_gather(row_set[0], 'dp', axis=1, tiled=True)  213 us
    all_gather x1, waiting for transfers between devices, gather_five(): lax.all_gather(row_set[4], 'dp', axis=1, tiled=True)  149 us
    all_gather x1, waiting for transfers between devices, gather_five(): lax.all_gather(row_set[3], 'dp', axis=1, tiled=True)  144 us
    reduce_scatter x1, waiting for transfers between devices, scatter_five(): lax.psum_scatter(totals[0].astype(jnp.bfloat16), 'fsdp', scatter_dimensio...  119 us
    all_gather x1, waiting for transfers between devices, gather_five(): lax.all_gather(row_set[1], 'dp', axis=1, tiled=True)  110 us
    reduce_scatter x1, waiting for transfers between devices, scatter_five(): lax.psum_scatter(totals[3].astype(jnp.bfloat16), 'fsdp', scatter_dimensio...  84.7 us
    reduce_scatter x1, waiting for transfers between devices, scatter_five(): lax.psum_scatter(totals[4].astype(jnp.bfloat16), 'fsdp', scatter_dimensio...  84 us
  transfers between devices with their start and end apart: 18, of which 16 were waited for; matrix products, arithmetic and copies ran while one was open for 10% of the time, Pallas kernels for 0%

commit v1 on v0

--- a/solution.py
+++ b/solution.py
@@ -1,11 +1,17 @@
+import functools
 import math
 
 import jax
 import jax.numpy as jnp
 from jax import lax
+from jax.experimental import pallas as pl
+from jax.experimental.pallas import tpu as pltpu
 from jax.sharding import PartitionSpec as P
 
 HEADS = 16
+AXES = ("dp", "fsdp")
+EPS = 1e-06
+F32, LOW = jnp.float32, jnp.bfloat16
 
 
 def norm_mod(values, shift_add, scale_mul):
@@ -88,7 +94,7 @@
     )
 
 
-def body(
+def general_body(
     inputs,
     out_cotangent,
     lengths,
@@ -236,32 +242,680 @@
     return (result, input_grad, ada_grad, qkv_grad, proj_grad, up_grad, down_grad)
 
 
+def dot_nn(left, right):
+    return lax.dot_general(left, right, (((1,), (0,)), ((), ())), preferred_element_type=F32)
+
+
+def dot_nt(left, right):
+    return lax.dot_general(left, right, (((1,), (1,)), ((), ())), preferred_element_type=F32)
+
+
+def dot_tn(left, right):
+    return lax.dot_general(left, right, (((0,), (0,)), ((), ())), preferred_element_type=F32)
+
+
+def stats(values):
+    mean = jnp.mean(values, -1, keepdims=True)
+    center = values - mean
+    spread = jnp.mean(center * center, -1, keepdims=True)
+    inverse = lax.rsqrt(spread + EPS)
+    return center * inverse, inverse
+
+
+def here(names):
+    return lax.axis_index(names[0]), lax.axis_index(names[1])
+
+
+def start_blocks(half_refs, weight_ref, sems):
+    column, row = here(AXES)
+    row_parts = weight_ref.shape[1]
+    copies = {}
+    for relative, halves in enumerate(half_refs):
+        copies[relative] = []
+        for part, ref in enumerate(halves):
+            height = ref.shape[0]
+            copy = pltpu.make_async_copy(
+                ref,
+                weight_ref.at[
+                    column ^ (relative // row_parts),
+                    row ^ (relative % row_parts),
+                    pl.ds(part * height, height),
+                ],
+                sems.at[relative, part],
+            )
+            copy.start()
+            copies[relative].append(copy)
+    return copies
+
+
+def pair_mask(span, frames, live):
+    query = lax.broadcasted_iota(jnp.int32, (span, span), 0)
+    key = lax.broadcasted_iota(jnp.int32, (span, span), 1)
+    return ((query // frames) == (key // frames)) & ((key % frames) < live)
+
+
+def head_probs(queries, keys, live_mask, scale):
+    scores = dot_nt(queries, keys) * scale
+    scores = jnp.where(live_mask, scores, -1e30)
+    exp_scores = jnp.exp(scores - jnp.max(scores, -1, keepdims=True))
+    return exp_scores / jnp.sum(exp_scores, -1, keepdims=True)
+
+
+def head_slices(ref, which, head, rows, size):
+    per = ref.shape[2] // size
+    slot = which * HEADS + head
+    return ref[slot // per, rows, (slot % per) * size : (slot % per + 1) * size]
+
+
+def attn_forward_kernel(sizes, *refs):
+    clips, span, frames, width, qkv_cols, proj_cols, chunk = sizes
+    column_parts, row_parts = sizes_parts(refs[-2])
+    blocks = column_parts * row_parts
+    lengths, tokens, mod = refs[:3]
+    half_refs = [(refs[3 + i], refs[3 + blocks + i]) for i in range(blocks)]
+    hidden, mixed, attended, branch, middle, hidden_two = refs[3 + 2 * blocks : 9 + 2 * blocks]
+    weight, sems = refs[9 + 2 * blocks :]
+    copies = start_blocks(half_refs, weight, sems)
+    size = width // HEADS
+    part_width = width // row_parts
+    scale = 1.0 / math.sqrt(size)
+
+    def first_norm(step, carry):
+        rows = pl.ds(pl.multiple_of(step * chunk, chunk), chunk)
+        clip_mod = mod[step * chunk // span]
+        unit, _ = stats(tokens[rows, :].astype(F32))
+        value = (unit * (1.0 + clip_mod[1:2]) + clip_mod[0:1]).astype(LOW)
+        for part in range(row_parts):
+            hidden[part, rows, :] = value[:, part * part_width : (part + 1) * part_width]
+        return carry
+
+    lax.fori_loop(0, clips * span // chunk, first_norm, 0)
+    column, row = here(AXES)
+    for relative in range(column_parts):
+        for other in range(row_parts):
+            for copy in copies[relative * row_parts + other]:
+                copy.wait()
+        place = column ^ relative
+        total = dot_nn(hidden[0], weight[place, 0, :, 0:qkv_cols])
+        for part in range(1, row_parts):
+            total += dot_nn(hidden[part], weight[place, part, :, 0:qkv_cols])
+        mixed[place] = total.astype(LOW)
+
+    per = part_width // size
+    for clip in range(clips):
+        rows = slice(clip * span, (clip + 1) * span)
+        live_mask = pair_mask(span, frames, lengths[clip])
+        for head in range(HEADS):
+            probs = head_probs(
+                head_slices(mixed, 0, head, rows, size),
+                head_slices(mixed, 1, head, rows, size),
+                live_mask,
+                scale,
+            )
+            value = dot_nn(probs.astype(LOW), head_slices(mixed, 2, head, rows, size))
+            attended[head // per, rows, (head % per) * size : (head % per + 1) * size] = (
+                value.astype(LOW)
+            )
+
+    for place in range(column_parts):
+        total = dot_nn(attended[0], weight[place, 0, :, qkv_cols : qkv_cols + proj_cols])
+        for part in range(1, row_parts):
+            total += dot_nn(attended[part], weight[place, part, :, qkv_cols : qkv_cols + proj_cols])
+        branch[:, place * proj_cols : (place + 1) * proj_cols] = total
+
+    def second_norm(step, carry):
+        rows = pl.ds(pl.multiple_of(step * chunk, chunk), chunk)
+        clip_mod = mod[step * chunk // span]
+        value = tokens[rows, :].astype(F32) + clip_mod[2:3] * branch[rows, :]
+        middle[rows, :] = value
+        unit, _ = stats(value)
+        hidden_two[rows, :] = (unit * (1.0 + clip_mod[4:5]) + clip_mod[3:4]).astype(LOW)
+        return carry
+
+    lax.fori_loop(0, clips * span // chunk, second_norm, 0)
+
+
+def sizes_parts(weight_ref):
+    return weight_ref.shape[0], weight_ref.shape[1]
+
+
+def attn_backward_kernel(sizes, *refs):
+    clips, span, frames, width, qkv_cols, proj_cols, chunk = sizes
+    column_parts, row_parts = sizes_parts(refs[-5])
+    blocks = column_parts * row_parts
+    lengths, tokens, cotangent, mod, middle, branch, mixed, grad_own, grad_far = refs[:9]
+    half_refs = [(refs[9 + i], refs[9 + blocks + i]) for i in range(blocks)]
+    input_grad, d_both, d_mod = refs[9 + 2 * blocks : 12 + 2 * blocks]
+    weight, sems, d_middle, d_attended, d_hidden = refs[12 + 2 * blocks :]
+    copies = start_blocks(half_refs, weight, sems)
+    size = width // HEADS
+    part_width = width // row_parts
+    scale = 1.0 / math.sqrt(size)
+    steps = span // chunk
+    zero_row = jnp.zeros((1, width), F32)
+
+    for clip in range(clips):
+        clip_mod = mod[clip]
+
+        def second_back(step, carry, clip=clip, clip_mod=clip_mod):
+            d_shift, d_scale, d_gate = carry
+            rows = pl.ds(pl.multiple_of(clip * span + step * chunk, chunk), chunk)
+            grad = grad_own[rows, :] + grad_far[rows, :].astype(F32)
+            unit, inverse = stats(middle[rows, :])
+            d_unit = grad * (1.0 + clip_mod[4:5])
+            d_value = cotangent[rows, :].astype(F32) + inverse * (
+                d_unit
+                - jnp.mean(d_unit, -1, keepdims=True)
+                - unit * jnp.mean(d_unit * unit, -1, keepdims=True)
+            )
+            d_middle[rows, :] = d_value
+            d_branch = (d_value * clip_mod[2:3]).astype(LOW)
+            for place in range(column_parts):
+                d_both[place, rows, qkv_cols : qkv_cols + proj_cols] = d_branch[
+                    :, place * proj_cols : (place + 1) * proj_cols
+                ]
+            return (
+                d_shift + jnp.sum(grad, 0, keepdims=True),
+                d_scale + jnp.sum(grad * unit, 0, keepdims=True),
+                d_gate + jnp.sum(d_value * branch[rows, :], 0, keepdims=True),
+            )
+
+        sums = lax.fori_loop(0, steps, second_back, (zero_row, zero_row, zero_row))
+        d_mod[clip, 2:3, :] = sums[2]
+        d_mod[clip, 3:4, :] = sums[0]
+        d_mod[clip, 4:5, :] = sums[1]
+        d_mod[clip, 5:6, :] = zero_row
+
+    for group in copies.values():
+        for copy in group:
+            copy.wait()
+
+    proj = slice(qkv_cols, qkv_cols + proj_cols)
+    for part in range(row_parts):
+        total = dot_nt(d_both[0, :, proj], weight[0, part, :, proj])
+        for place in range(1, column_parts):
+            total += dot_nt(d_both[place, :, proj], weight[place, part, :, proj])
+        d_attended[part] = total.astype(LOW)
+
+    per = part_width // size
+    for clip in range(clips):
+        rows = slice(clip * span, (clip + 1) * span)
+        live_mask = pair_mask(span, frames, lengths[clip])
+        for head in range(HEADS):
+            queries = head_slices(mixed, 0, head, rows, size)
+            keys = head_slices(mixed, 1, head, rows, size)
+            values = head_slices(mixed, 2, head, rows, size)
+            probs = head_probs(queries, keys, live_mask, scale)
+            grad = d_attended[head // per, rows, (head % per) * size : (head % per + 1) * size]
+            d_value = dot_tn(probs.astype(LOW), grad)
+            d_probs = dot_nt(grad, values)
+            d_scores = (probs * (d_probs - jnp.sum(probs * d_probs, -1, keepdims=True))).astype(LOW)
+            d_query = dot_nn(d_scores, keys) * scale
+            d_key = dot_tn(d_scores, queries) * scale
+            cols = qkv_cols // size
+            for which, piece in enumerate((d_query, d_key, d_value)):
+                slot = which * HEADS + head
+                d_both[
+                    slot // cols, rows, (slot % cols) * size : (slot % cols + 1) * size
+                ] = piece.astype(LOW)
+
+    for part in range(row_parts):
+        total = dot_nt(d_both[0, :, 0:qkv_cols], weight[0, part, :, 0:qkv_cols])
+        for place in range(1, column_parts):
+            total += dot_nt(d_both[place, :, 0:qkv_cols], weight[place, part, :, 0:qkv_cols])
+        d_hidden[:, part * part_width : (part + 1) * part_width] = total
+
+    for clip in range(clips):
+        clip_mod = mod[clip]
+
+        def first_back(step, carry, clip=clip, clip_mod=clip_mod):
+            d_shift, d_scale = carry
+            rows = pl.ds(pl.multiple_of(clip * span + step * chunk, chunk), chunk)
+            grad = d_hidden[rows, :]
+            unit, inverse = stats(tokens[rows, :].astype(F32))
+            d_unit = grad * (1.0 + clip_mod[1:2])
+            input_grad[rows, :] = (
+                d_middle[rows, :]
+                + inverse
+                * (
+                    d_unit
+                    - jnp.mean(d_unit, -1, keepdims=True)
+                    - unit * jnp.mean(d_unit * unit, -1, keepdims=True)
+                )
+            ).astype(LOW)
+            return (
+                d_shift + jnp.sum(grad, 0, keepdims=True),
+                d_scale + jnp.sum(grad * unit, 0, keepdims=True),
+            )
+
+        sums = lax.fori_loop(0, steps, first_back, (zero_row, zero_row))
+        d_mod[clip, 0:1, :] = sums[0]
+        d_mod[clip, 1:2, :] = sums[1]
+
+
+def attn_weight_kernel(sizes, *refs):
+    qkv_cols, proj_cols, half = sizes
+    own, far = refs[:3], refs[3:6]
+    outs = refs[6:]
+    column_parts, row_parts = own[2].shape[0], own[0].shape[0]
+    column, row = here(AXES)
+    for other in range(row_parts // 2):
+        part = row ^ (2 * other)
+        for relative in range(column_parts):
+            place = column ^ relative
+            x_bit, z_bits = relative % 2, relative // 2
+            groups = column_parts // 2
+            first = outs[other * groups + z_bits]
+            second = outs[(2 + x_bit) * groups + z_bits]
+            total = dot_tn(own[0][part], own[2][place, :, 0:qkv_cols]) + dot_tn(
+                far[0][part], far[2][place, :, 0:qkv_cols]
+            )
+            first[x_bit, :, 0:qkv_cols] = total[:half].astype(LOW)
+            second[other, :, 0:qkv_cols] = total[half:].astype(LOW)
+            proj = slice(qkv_cols, qkv_cols + proj_cols)
+            total = dot_tn(own[1][part], own[2][place, :, proj]) + dot_tn(
+                far[1][part], far[2][place, :, proj]
+            )
+            first[x_bit, :, proj] = total[:half].astype(LOW)
+            second[other, :, proj] = total[half:].astype(LOW)
+
+
+def feed_kernel(chunk, *refs):
+    hidden, d_outs = refs[0:2], refs[2:4]
+    blocks = refs[4:-7]
+    outs, blocks = blocks[-8:], blocks[:-8]
+    up_weight, down_weight, sems, up_proj, d_activ, activ_s, d_up_s = refs[-7:]
+    activ, d_up, d_hidden, partial = outs[0:2], outs[2:4], outs[4:6], outs[6:8]
+    column, _ = here(AXES)
+    copies = []
+    for relative, ref in enumerate(blocks):
+        half = ref.shape[0] // 2
+        place = pl.ds(pl.multiple_of((column ^ relative) * half, 16), half)
+        for which, weight in enumerate((up_weight, down_weight)):
+            copy = pltpu.make_async_copy(
+                ref.at[pl.ds(which * half, half)], weight.at[place], sems.at[relative, which]
+            )
+            copy.start()
+            copies.append(copy)
+    for copy in copies:
+        copy.wait()
+    tilt = math.sqrt(2.0 / math.pi)
+    for index in range(2):
+        up_proj[...] = dot_nt(hidden[index][...], up_weight[...])
+        d_activ[...] = dot_nn(d_outs[index][...], down_weight[...])
+
+        def gelu(step, carry, index=index):
+            rows = pl.ds(pl.multiple_of(step * chunk, chunk), chunk)
+            value = up_proj[rows, :]
+            square = value * value
+            bend = jnp.tanh(tilt * value * (1.0 + 0.044715 * square))
+            activ_low = (0.5 * value * (1.0 + bend)).astype(LOW)
+            slope = 0.5 * (1.0 + bend) + 0.5 * value * (1.0 - bend * bend) * (
+                tilt * (1.0 + 3.0 * 0.044715 * square)
+            )
+            activ[index][rows, :] = activ_low
+            d_up[index][rows, :] = (d_activ[rows, :] * slope).astype(LOW)
+            return carry
+
+        lax.fori_loop(0, up_proj.shape[0] // chunk, gelu, 0)
+        d_hidden[index][...] = dot_nn(d_up[index][...], up_weight[...]).astype(
+            d_hidden[index].dtype
+        )
+        partial[index][...] = dot_nt(activ[index][...], down_weight[...]).astype(
+            partial[index].dtype
+        )
+
+
+def feed_weight_kernel(tile, *refs):
+    count = (len(refs) - 3) // 2
+    hidden, d_outs, activ, d_up = refs[0:4], refs[4:8], refs[8:12], refs[12:16]
+    outs = refs[16:-3]
+    up_grad, down_grad, sems = refs[-3:]
+    column, _ = here(AXES)
+
+    def product(step, carry):
+        cols = pl.ds(pl.multiple_of(step * tile, tile), tile)
+        for left, right, grad in ((d_up, hidden, up_grad), (d_outs, activ, down_grad)):
+            total = dot_tn(left[0][:, cols], right[0][...])
+            for index in range(1, 4):
+                total += dot_tn(left[index][:, cols], right[index][...])
+            grad[cols, :] = total.astype(LOW)
+        return carry
+
+    lax.fori_loop(0, up_grad.shape[0] // tile, product, 0)
+    copies = []
+    for relative, ref in enumerate(outs):
+        half = ref.shape[0] // 2
+        place = pl.ds(pl.multiple_of((column ^ relative) * half, 16), half)
+        for which, grad in enumerate((up_grad, down_grad)):
+            copy = pltpu.make_async_copy(
+                grad.at[place], ref.at[pl.ds(which * half, half)], sems.at[relative, which]
+            )
+            copy.start()
+            copies.append(copy)
+    for copy in copies:
+        copy.wait()
+
+
+VMEM_SPEC = pl.BlockSpec(memory_space=pltpu.VMEM)
+SMEM_SPEC = pl.BlockSpec(memory_space=pltpu.SMEM)
+ANY_SPEC = pl.BlockSpec(memory_space=pl.ANY)
+PARAMS = pltpu.CompilerParams(vmem_limit_bytes=56 * 1024 * 1024)
+
+
+def shape_of(dims, kind=LOW):
+    return jax.ShapeDtypeStruct(dims, kind)
+
+
+def cost(flops, moved, special=0):
+    return pl.CostEstimate(flops=flops, bytes_accessed=moved, transcendentals=special)
+
+
+def swap(value, mask, count):
+    return lax.ppermute(value, AXES, [(i, i ^ mask) for i in range(count)])
+
+
+def spread(block, stages, count):
+    have = {0: block}
+    for masks in stages:
+        fresh = dict(have)
+        for mask in masks:
+            for relative, value in have.items():
+                fresh[relative ^ mask] = swap(value, mask, count)
+        have = fresh
+    return have
+
+
+def padded_exchange(rows, count):
+    length = rows.shape[1]
+    tiles = -(-length // 1024) * 8
+    rows = jnp.pad(rows, ((0, 0), (0, tiles * 128 - length))).reshape(count, tiles, 128)
+    got = lax.all_to_all(rows, AXES, 0, 0, tiled=True)
+    return got.reshape(count, tiles * 128)[:, :length]
+
+
+def fast_body(
+    column_parts,
+    row_parts,
+    inputs,
+    out_cotangent,
+    lengths,
+    timesteps,
+    labels,
+    time_table,
+    class_table,
+    ada_weight,
+    qkv_weight,
+    proj_weight,
+    up_weight,
+    down_weight,
+):
+    count = column_parts * row_parts
+    clips, positions, frames, width = inputs.shape
+    span = positions * frames
+    row_count = clips * span
+    qkv_cols, proj_cols = qkv_weight.shape[1], proj_weight.shape[1]
+    height = qkv_weight.shape[0]
+    part_width = width // row_parts
+    hidden_part = up_weight.shape[1] * column_parts // row_parts
+    sub = up_weight.shape[1] // row_parts
+    x_mask = row_parts
+    z_masks = tuple(row_parts * 2 * i for i in range(1, column_parts // 2))
+    half = height // 2
+
+    own_block = jnp.concatenate([qkv_weight, proj_weight], axis=1)
+    first_half = spread(own_block[:half], (z_masks, (x_mask,), (2,), (1,)), count)
+    second_half = spread(own_block[half:], (z_masks, (2,), (x_mask,), (1,)), count)
+    halves = [first_half[i] for i in range(count)] + [second_half[i] for i in range(count)]
+
+    cond_rows = [
+        lax.dynamic_slice_in_dim(time_table, timesteps[i], 1, 0).astype(F32)
+        + lax.dynamic_slice_in_dim(class_table, labels[i], 1, 0).astype(F32)
+        for i in range(clips)
+    ]
+    cond_low = jax.nn.silu(jnp.concatenate(cond_rows, 0)).astype(LOW)
+    cond_send = cond_low.reshape(clips, row_parts, part_width).transpose(1, 0, 2)
+    cond_send = jnp.broadcast_to(
+        cond_send.reshape(1, row_parts, clips * part_width),
+        (column_parts, row_parts, clips * part_width),
+    ).reshape(count, clips * part_width)
+    cond_all = padded_exchange(cond_send, count).reshape(count * clips, part_width)
+    ada_cols = ada_weight.shape[1]
+    mod_part = jnp.dot(cond_all, ada_weight, preferred_element_type=F32)
+    mod_got = padded_exchange(mod_part.reshape(count, clips * ada_cols), count)
+    mod_own = jnp.sum(mod_got.reshape(column_parts, row_parts, clips, ada_cols), axis=1)
+    mod = mod_own.transpose(1, 0, 2).reshape(clips, 6, width)
+
+    up_send = up_weight.reshape(height, row_parts, sub).transpose(1, 2, 0)
+    down_send = (
+        down_weight.reshape(-1, row_parts, sub, proj_cols)
+        .transpose(1, 3, 0, 2)
+        .reshape(row_parts, proj_cols, -1)
+    )
+    both_send = jnp.stack([up_send, down_send], axis=1)
+    both_send, _ = lax.optimization_barrier((both_send, second_half[z_masks[0]]))
+    both_got = lax.all_to_all(both_send, "fsdp", 0, 0, tiled=True)
+    own_feed = both_got.transpose(1, 2, 0, 3).reshape(2 * sub, width)
+    feed = spread(own_feed, (z_masks, (x_mask,)), count)
+    feed_blocks = [feed[i * row_parts] for i in range(column_parts)]
+
+    tokens = inputs.reshape(row_count, width)
+    cotangent = out_cotangent.reshape(row_count, width)
+    sizes = (clips, span, frames, width, qkv_cols, proj_cols, 32)
+    full = (row_count, width)
+    weight_scratch = [
+        pltpu.VMEM((column_parts, row_parts, height, qkv_cols + proj_cols), LOW),
+        pltpu.SemaphoreType.DMA((count, 2)),
+    ]
+    hidden, mixed, attended, branch, middle, hidden_two = pl.pallas_call(
+        functools.partial(attn_forward_kernel, sizes),
+        out_shape=(
+            shape_of((row_parts, row_count, part_width)),
+            shape_of((column_parts, row_count, qkv_cols)),
+            shape_of((row_parts, row_count, part_width)),
+            shape_of(full, F32),
+            shape_of(full, F32),
+            shape_of(full),
+        ),
+        in_specs=[SMEM_SPEC, VMEM_SPEC, VMEM_SPEC] + [ANY_SPEC] * (2 * count),
+        out_specs=[VMEM_SPEC] * 6,
+        scratch_shapes=weight_scratch,
+        compiler_params=PARAMS,
+        cost_estimate=cost(8 * row_count * width * width, 14_000_000),
+        name="attn_forward",
+    )(lengths, tokens, mod, *halves)
+
+    gate_two = jnp.repeat(mod[:, 5], span, axis=0)
+    d_out = (cotangent.astype(F32) * gate_two).astype(LOW)
+    d_outs = {0: d_out, 1: swap(d_out, 1, count), 2: swap(d_out, 2, count)}
+    d_outs[3] = swap(d_outs[2], 1, count)
+    tokens_two = {0: hidden_two, 1: swap(hidden_two, 1, count), 2: swap(hidden_two, 2, count)}
+    tokens_two[3] = swap(tokens_two[2], 1, count)
+
+    def feed_call(index, kind, name):
+        return pl.pallas_call(
+            functools.partial(feed_kernel, 32),
+            out_shape=[shape_of((row_count, hidden_part))] * 4
+            + [shape_of(full, kind), shape_of(full)] * 2,
+            in_specs=[VMEM_SPEC] * 4 + [ANY_SPEC] * column_parts,
+            out_specs=[VMEM_SPEC] * 8,
+            scratch_shapes=[
+                pltpu.VMEM((hidden_part, width), LOW),
+                pltpu.VMEM((width, hidden_part), LOW),
+                pltpu.SemaphoreType.DMA((column_parts, 2)),
+                pltpu.VMEM((row_count, hidden_part), F32),
+                pltpu.VMEM((row_count, hidden_part), F32),
+                pltpu.VMEM((8, 128), LOW),
+                pltpu.VMEM((8, 128), LOW),
+            ],
+            compiler_params=PARAMS,
+            cost_estimate=cost(16 * row_count * width * hidden_part, 12_000_000),
+            name=name,
+        )(
+            tokens_two[index],
+            tokens_two[index + 1],
+            d_outs[index],
+            d_outs[index + 1],
+            *feed_blocks,
+        )
+
+    near = feed_call(0, F32, "feed_near")
+    distant = feed_call(2, F32, "feed_distant")
+    activ = list(near[0:2]) + list(distant[0:2])
+    d_up = list(near[2:4]) + list(distant[2:4])
+
+    def join(first, second, third, fourth):
+        far = third.astype(F32) + swap(fourth, 1, count).astype(F32)
+        mine = first.astype(F32) + swap(second, 1, count).astype(F32)
+        return mine, swap(far.astype(LOW), 2, count)
+
+    grad_own, grad_far = join(near[4], near[5], distant[4], distant[5])
+    out_own, out_far = join(near[6], near[7], distant[6], distant[7])
+
+    feed_grads = pl.pallas_call(
+        functools.partial(feed_weight_kernel, 128),
+        out_shape=[shape_of((2 * sub, width))] * column_parts,
+        in_specs=[VMEM_SPEC] * 16,
+        out_specs=[ANY_SPEC] * column_parts,
+        scratch_shapes=[
+            pltpu.VMEM((hidden_part, width), LOW),
+            pltpu.VMEM((width, hidden_part), LOW),
+            pltpu.SemaphoreType.DMA((column_parts, 2)),
+        ],
+        compiler_params=PARAMS,
+        cost_estimate=cost(16 * row_count * width * hidden_part, 15_000_000),
+        name="feed_weight",
+    )(
+        *[tokens_two[i] for i in range(4)],
+        *[d_outs[i] for i in range(4)],
+        *activ,
+        *d_up,
+    )
+
+    input_grad, d_both, d_mod = pl.pallas_call(
+        functools.partial(attn_backward_kernel, sizes),
+        out_shape=(
+            shape_of(full),
+            shape_of((column_parts, row_count, qkv_cols + proj_cols)),
+            shape_of((clips, 6, width), F32),
+        ),
+        in_specs=[SMEM_SPEC] + [VMEM_SPEC] * 8 + [ANY_SPEC] * (2 * count),
+        out_specs=[VMEM_SPEC] * 3,
+        scratch_shapes=weight_scratch
+        + [
+            pltpu.VMEM(full, F32),
+            pltpu.VMEM((row_parts, row_count, part_width), LOW),
+            pltpu.VMEM(full, F32),
+        ],
+        compiler_params=PARAMS,
+        cost_estimate=cost(8 * row_count * width * width, 16_000_000),
+        name="attn_backward",
+    )(lengths, tokens, cotangent, mod, middle, branch, mixed, grad_own, grad_far, *halves)
+
+    groups = column_parts // 2
+    attn_grads = pl.pallas_call(
+        functools.partial(attn_weight_kernel, (qkv_cols, proj_cols, half)),
+        out_shape=[shape_of((2, half, qkv_cols + proj_cols))] * (4 * groups),
+        in_specs=[VMEM_SPEC] * 6,
+        out_specs=[VMEM_SPEC] * (4 * groups),
+        compiler_params=PARAMS,
+        cost_estimate=cost(8 * row_count * width * width, 12_000_000),
+        name="attn_weight",
+    )(
+        hidden,
+        attended,
+        d_both,
+        swap(hidden, 1, count),
+        swap(attended, 1, count),
+        swap(d_both, 1, count),
+    )
+
+    def fold(keep, send, mask):
+        return keep.astype(F32) + swap(send, mask, count).astype(F32)
+
+    def last_fold(parts):
+        total = parts[0]
+        for index in range(1, groups):
+            got = swap(parts[index].astype(LOW), z_masks[index - 1], count)
+            total = total + got.astype(F32)
+        return total
+
+    feed_sums = [
+        fold(feed_grads[2 * i], feed_grads[2 * i + 1], x_mask) for i in range(groups)
+    ]
+    feed_sum = last_fold(feed_sums)
+    back = feed_sum.astype(LOW).reshape(2, sub, row_parts, height).transpose(2, 0, 1, 3)
+    back = lax.all_to_all(back, "fsdp", 0, 0, tiled=True)
+    up_grad = back[:, 0].transpose(2, 0, 1).reshape(height, row_parts * sub).astype(F32)
+    down_grad = (
+        back[:, 1]
+        .reshape(row_parts, proj_cols, -1, sub)
+        .transpose(2, 0, 3, 1)
+        .reshape(-1, proj_cols)
+        .astype(F32)
+    )
+
+    def two_folds(keep, send, masks):
+        sums = []
+        for index in range(groups):
+            once = fold(keep[index], send[index], masks[0])
+            low = once[1].astype(LOW)
+            sums.append(fold(once[0], low, masks[1]))
+        return last_fold(sums)
+
+    part = [attn_grads[i * groups : (i + 1) * groups] for i in range(4)]
+    attn_sum = jnp.concatenate(
+        [two_folds(part[0], part[1], (2, x_mask)), two_folds(part[2], part[3], (x_mask, 2))], 0
+    )
+    qkv_grad, proj_grad = attn_sum[:, :qkv_cols], attn_sum[:, qkv_cols:]
+
+    ffn_out = out_own + out_far.astype(F32)
+    result = (middle + gate_two * ffn_out).astype(LOW).reshape(inputs.shape)
+    d_gate_two = jnp.sum((cotangent.astype(F32) * ffn_out).reshape(clips, span, width), axis=1)
+    d_mod = d_mod.at[:, 5].set(d_gate_two)
+    mod_send = d_mod.reshape(clips, column_parts, ada_cols).transpose(1, 0, 2)
+    mod_send = jnp.broadcast_to(
+        mod_send.reshape(column_parts, 1, clips * ada_cols),
+        (column_parts, row_parts, clips * ada_cols),
+    ).reshape(count, clips * ada_cols)
+    d_mod_all = padded_exchange(mod_send, count).reshape(count * clips, ada_cols)
+    ada_grad = lax.dot_general(
+        cond_all.astype(F32),
+        d_mod_all,
+        (((0,), (0,)), ((), ())),
+        precision=lax.Precision.HIGHEST,
+        preferred_element_type=F32,
+    )
+    return (
+        result,
+        input_grad.reshape(inputs.shape),
+        ada_grad,
+        qkv_grad,
+        proj_grad,
+        up_grad,
+        down_grad,
+    )
+
+
 def solution(mesh):
+    column_parts, row_parts = mesh.shape["dp"], mesh.shape["fsdp"]
+    body = general_body
+    if (column_parts, row_parts) == (8, 4):
+        body = functools.partial(fast_body, column_parts, row_parts)
+    clip_spec = P(AXES, None, None, None)
     return jax.shard_map(
         body,
         mesh=mesh,
         in_specs=(
-            P(("dp", "fsdp"), None, None, None),
-            P(("dp", "fsdp"), None, None, None),
-            P(("dp", "fsdp")),
-            P(("dp", "fsdp")),
-            P(("dp", "fsdp")),
+            clip_spec,
+            clip_spec,
+            P(AXES),
+            P(AXES),
+            P(AXES),
             P(),
             P(),
-            P("fsdp", "dp"),
-            P("fsdp", "dp"),
-            P("fsdp", "dp"),
-            P("fsdp", "dp"),
-            P("fsdp", "dp"),
-        ),
-        out_specs=(
-            P(("dp", "fsdp"), None, None, None),
-            P(("dp", "fsdp"), None, None, None),
-            P("fsdp", "dp"),
-            P("fsdp", "dp"),
-            P("fsdp", "dp"),
-            P("fsdp", "dp"),
-            P("fsdp", "dp"),
-        ),
+        )
+        + (P("fsdp", "dp"),) * 5,
+        out_specs=(clip_spec, clip_spec) + (P("fsdp", "dp"),) * 5,
         check_vma=False,
     )

time: 1640 us -> 522 us (0.32)
  waiting for transfers between devices: 1390 us -> 198 us
  Pallas kernels: 0 us -> 117 us
  matrix products: 113 us -> 1.8 us
  starting transfers between devices: 1.24 us -> 110 us
  local copies, waits for them, and re-layouts: 76.2 us -> 49 us
    all_gather x8 -> x0, waiting for transfers between devices: 684 us -> none  [the longest x1 213 us: gather_five(): lax.all_gather(row_set[0], 'dp', axis=1, tiled=True)]
    unnamed x23 -> x0, waiting for transfers between devices: 389 us -> none
    reduce_scatter x5 -> x0, waiting for transfers between devices: 315 us -> none  [the longest x1 119 us: scatter_five(): lax.psum_scatter(totals[0].astype(jnp.bfloat16), 'fsdp', scatter_dimensio...]
    ppermute x0 -> x113, waiting for transfers between devices: none -> 198 us  [swap(): return lax.ppermute(value, AXES, [(i, i ^ mask) for i in range(count)])]
    pallas_call x0 -> x6, Pallas kernels: none -> 117 us  [the longest x1 33.3 us: fast_body(): pl.pallas_call(functools.partial(attn_backward_kernel, sizes), out_shape=...]
    dot_general x21 -> x2, matrix products: 111 us -> 1.8 us  [the longest x1 1.57 us: fast_body(): lax.dot_general(cond_all.astype(F32), d_mod_all, (((0,), (0,)), ((), ()))...]
    ppermute x0 -> x113, starting transfers between devices: none -> 96 us  [swap(): return lax.ppermute(value, AXES, [(i, i ^ mask) for i in range(count)])]
    unnamed x100 -> x186, local copies, waits for them, and re-layouts: 40 us -> 12.9 us
  transfers between devices with their start and end apart: 18 -> 117, of which waited for: 16 -> 31; matrix products, arithmetic and copies ran while one was open for 10% -> 11% of each run, Pallas kernels for 0% -> 23%
where the time goes in v1:
time: 522 us; the launch traced here: 512 us
  waiting for transfers between devices  198 us (38%)
  Pallas kernels  117 us (22%)
  starting transfers between devices  110 us (21%)
  local copies, waits for them, and re-layouts  49 us (9%)
  other arithmetic  15.4 us (3%)
  blocking collectives  10.9 us (2%)
  between operations  10 us (2%)
    ppermute x113, waiting for transfers between devices, swap(): return lax.ppermute(value, AXES, [(i, i ^ mask) for i in range(count)])  198 us
    ppermute x113, starting transfers between devices, swap(): return lax.ppermute(value, AXES, [(i, i ^ mask) for i in range(count)])  96 us
    pallas_call x1, Pallas kernels, fast_body(): pl.pallas_call(functools.partial(attn_backward_kernel, sizes), out_shape=...  33.3 us
    pallas_call x2, Pallas kernels, feed_call(): pl.pallas_call(functools.partial(feed_kernel, 32), out_shape=[shape_of((r...  28.8 us
    pallas_call x1, Pallas kernels, fast_body(): pl.pallas_call(functools.partial(attn_forward_kernel, sizes), out_shape=(...  27.5 us
    pallas_call x1, Pallas kernels, fast_body(): pl.pallas_call(functools.partial(feed_weight_kernel, 128), out_shape=[sha...  14.2 us
    pallas_call x1, Pallas kernels, fast_body(): pl.pallas_call(functools.partial(attn_weight_kernel, (qkv_cols, proj_cols...  13.4 us
    unnamed x186, local copies, waits for them, and re-layouts  12.9 us
  transfers between devices with their start and end apart: 117, of which 31 were waited for; matrix products, arithmetic and copies ran while one was open for 11% of the time, Pallas kernels for 23%

profile of v1, /device:TPU:0, one launch (start us, length us, event | category | flops | bytes accessed | tf_op | source)
XLA Modules:
  0.0 512.2 jit_solution(17992230918355372536)
XLA Ops:
  17.6 7.8 %collective-permute-done.15.refs_19_.refs_25_ = bf16[144,576]{1,0:T(8,128)(2,1)S(1)} collective-permute-done((bf16[144,576]{1,0:T(8,128)(2,1)S(1)}, bf16[144,576]{1,0:T(8,128)(2,1)S(1)}, u32[]{:S(2)}, u32[]{:S(2)}) %collective-permute-start.15) | collective-permute-done | bytes 165920 | tf_op jit(solution)/shard_map/ppermute | solution.py:615
  33.7 8.9 %collective-permute-done.46.refs_51_.refs_57_ = bf16[144,576]{1,0:T(8,128)(2,1)S(1)} collective-permute-done((bf16[144,576]{1,0:T(8,128)(2,1)S(1)}, bf16[144,576]{1,0:T(8,128)(2,1)S(1)}, u32[]{:S(2)}, u32[]{:S(2)}) %collective-permute-start.46) | collective-permute-done | bytes 165920 | tf_op jit(solution)/shard_map/ppermute | solution.py:615
  67.2 10.9 %all_to_all.25 = bf16[32,8,128]{2,1,0:T(8,128)(2,1)S(1)} all-to-all(bf16[32,8,128]{2,1,0:T(8,128)(2,1)S(1)} %bitcast.165), channel_id=1, replica_groups=mesh['dp'=8,'fsdp'=4] {'dp','fsdp'}, dimensions={0} | all-to-all | bytes 131072 | tf_op jit(solution)/shard_map/all_to_all | solution.py:633
  97.5 5.1 %collective-permute-done.21.refs_25_.refs_31_ = bf16[144,576]{1,0:T(8,128)(2,1)S(1)} collective-permute-done((bf16[144,576]{1,0:T(8,128)(2,1)}, bf16[144,576]{1,0:T(8,128)(2,1)S(1)}, u32[]{:S(2)}, u32[]{:S(2)}) %collective-permute-start.21) | collective-permute-done | bytes 165920 | tf_op jit(solution)/shard_map/ppermute | solution.py:615
  132.1 27.5 %attn_forward.1 = (bf16[4,256,288]{2,1,0:T(8,128)(2,1)}, bf16[8,256,432]{2,1,0:T(8,128)(2,1)}, bf16[4,256,288]{2,1,0:T(8,128)(2,1)}, f32[256,1152]{1,0:T(8,128)}...) custom-call(s32[2]{0:T(128)} %refs_0_.3, bf16[256,1152]{1,0:T(8,128)(2,1)} %bitcast.156, f32[2,6,1152]{2,1,0:T(8,128)} %copy-done.55, ...), custom_call_target="tpu_custom_call" | custom-call | flops 2717908992 | bytes 14000000 | tf_op jit(solution)/shard_map/attn_forward/pallas_call | solution.py:710
  161.7 13.3 %collective-permute-done.72.refs_0_.refs_2_ = bf16[256,1152]{1,0:T(8,128)(2,1)} collective-permute-done((bf16[256,1152]{1,0:T(8,128)(2,1)}, bf16[256,1152]{1,0:T(8,128)(2,1)}, u32[]{:S(2)}, u32[]{:S(2)}) %collective-permute-start.72) | collective-permute-done | bytes 589856 | tf_op jit(solution)/shard_map/ppermute | solution.py:615
  182.8 10.0 %collective-permute-done.66.refs_7_ = bf16[288,1152]{1,0:T(8,128)(2,1)S(1)} collective-permute-done((bf16[288,1152]{1,0:T(8,128)(2,1)S(1)}, bf16[288,1152]{1,0:T(8,128)(2,1)S(1)}, u32[]{:S(2)}, u32[]{:S(2)}) %collective-permute-start.66) | collective-permute-done | bytes 663584 | tf_op jit(solution)/shard_map/ppermute | solution.py:615
  192.8 14.3 %collective-permute-done.68.refs_9_ = bf16[288,1152]{1,0:T(8,128)(2,1)} collective-permute-done((bf16[288,1152]{1,0:T(8,128)(2,1)}, bf16[288,1152]{1,0:T(8,128)(2,1)}, u32[]{:S(2)}, u32[]{:S(2)}) %collective-permute-start.68) | collective-permute-done | bytes 663584 | tf_op jit(solution)/shard_map/ppermute | solution.py:615
  207.1 13.8 %collective-permute-done.70.refs_11_ = bf16[288,1152]{1,0:T(8,128)(2,1)} collective-permute-done((bf16[288,1152]{1,0:T(8,128)(2,1)}, bf16[288,1152]{1,0:T(8,128)(2,1)}, u32[]{:S(2)}, u32[]{:S(2)}) %collective-permute-start.70) | collective-permute-done | bytes 663584 | tf_op jit(solution)/shard_map/ppermute | solution.py:615
  220.9 14.3 %feed_near.1 = (bf16[256,1152]{1,0:T(8,128)(2,1)}, bf16[256,1152]{1,0:T(8,128)(2,1)}, bf16[256,1152]{1,0:T(8,128)(2,1)}, bf16[256,1152]{1,0:T(8,128)(2,1)}, f32[...) custom-call(bf16[256,1152]{1,0:T(8,128)(2,1)} %get-tuple-element.70.refs_0_, ...), custom_call_target="tpu_custom_call" | custom-call | flops 5435817984 | bytes 12000000 | tf_op jit(solution)/shard_map/feed_near/pallas_call | solution.py:736
  236.1 14.4 %feed_distant.1 = (bf16[256,1152]{1,0:T(8,128)(2,1)}, bf16[256,1152]{1,0:T(8,128)(2,1)}, bf16[256,1152]{1,0:T(8,128)(2,1)}, bf16[256,1152]{1,0:T(8,128)(2,1)}, f...) custom-call(bf16[256,1152]{1,0:T(8,128)(2,1)} %collective-permute-done.72.refs_, ...), custom_call_target="tpu_custom_call" | custom-call | flops 5435817984 | bytes 12000000 | tf_op jit(solution)/shard_map/feed_distant/pallas_call | solution.py:736
  251.2 14.2 %feed_weight.1 = (bf16[288,1152]{1,0:T(8,128)(2,1)}, bf16[288,1152]{1,0:T(8,128)(2,1)}, bf16[288,1152]{1,0:T(8,128)(2,1)}, bf16[288,1152]{1,0:T(8,128)(2,1)}, bf...) custom-call(bf16[256,1152]{1,0:T(8,128)(2,1)} %get-tuple-element.70., ...), custom_call_target="tpu_custom_call" | custom-call | flops 5435817984 | bytes 15000000 | tf_op jit(solution)/shard_map/feed_weight/pallas_call | solution.py:775
  270.9 12.5 %collective-permute-done.111 = bf16[288,1152]{1,0:T(8,128)(2,1)S(1)} collective-permute-done((bf16[288,1152]{1,0:T(8,128)(2,1)}, bf16[288,1152]{1,0:T(8,128)(2,1)S(1)}, u32[]{:S(2)}, u32[]{:S(2)}) %collective-permute-start.111) | collective-permute-done | bytes 663584 | tf_op jit(solution)/shard_map/ppermute | solution.py:615
  286.0 33.3 %attn_backward.1 = (bf16[256,1152]{1,0:T(8,128)(2,1)}, bf16[8,256,576]{2,1,0:T(8,128)(2,1)}, f32[2,6,1152]{2,1,0:T(8,128)}) custom-call(s32[2]{0:T(128)} %refs_0_.3, bf16[256,1152]{1,0:T(8,128)(2,1)} %bitcast.157, bf16[256,1152]{1,0:T(8,128)(2,1)} %bitcast.152, f32[2,6,1152]{2,1,0:T(8,128)} %copy-done.55, f32[256,1152]{1,0:T(8,128)} %get-tuple-element.69.refs_4_, ...), custom_call_target="tpu_custom_call" | custom-call | flops 2717908992 | bytes 16000000 | tf_op jit(solution)/shard_map/attn_backward/pallas_call | solution.py:795
  330.9 8.1 %collective-permute-done.77 = bf16[256,1152]{1,0:T(8,128)(2,1)S(1)} collective-permute-done((bf16[256,1152]{1,0:T(8,128)(2,1)}, bf16[256,1152]{1,0:T(8,128)(2,1)S(1)}, u32[]{:S(2)}, u32[]{:S(2)}) %collective-permute-start.77) | collective-permute-done | bytes 589856 | tf_op jit(solution)/shard_map/ppermute | solution.py:615
  352.2 4.7 all-to-all-start.3
  358.0 33.3 %collective-permute-done.110 = bf16[288,1152]{1,0:T(8,128)(2,1)} collective-permute-done((bf16[288,1152]{1,0:T(8,128)(2,1)}, bf16[288,1152]{1,0:T(8,128)(2,1)}, u32[]{:S(2)}, u32[]{:S(2)}) %collective-permute-start.110) | collective-permute-done | bytes 663584 | tf_op jit(solution)/shard_map/ppermute | solution.py:615
  404.3 13.4 %attn_weight.1 = (bf16[2,144,576]{2,1,0:T(8,128)(2,1)}, bf16[2,144,576]{2,1,0:T(8,128)(2,1)}, bf16[2,144,576]{2,1,0:T(8,128)(2,1)}, bf16[2,144,576]{2,1,0:T(8,12...) custom-call(bf16[4,256,288]{2,1,0:T(8,128)(2,1)} %get-tuple-element., ...), custom_call_target="tpu_custom_call" | custom-call | flops 2717908992 | bytes 12000000 | tf_op jit(solution)/shard_map/attn_weight/pallas_call | solution.py:816
  431.6 14.1 %collective-permute-done.89 = bf16[2,144,576]{2,1,0:T(8,128)(2,1)S(1)} collective-permute-done((bf16[2,144,576]{2,1,0:T(8,128)(2,1)S(1)}, bf16[2,144,576]{2,1,0:T(8,128)(2,1)S(1)}, u32[]{:S(2)}, u32[]{:S(2)}) %collective-permute-start.89) | collective-permute-done | bytes 331808 | tf_op jit(solution)/shard_map/ppermute | solution.py:615
  447.1 5.5 %collective-permute-done.86 = bf16[2,144,576]{2,1,0:T(8,128)(2,1)S(1)} collective-permute-done((bf16[2,144,576]{2,1,0:T(8,128)(2,1)S(1)}, bf16[2,144,576]{2,1,0:T(8,128)(2,1)S(1)}, u32[]{:S(2)}, u32[]{:S(2)}) %collective-permute-start.86) | collective-permute-done | bytes 331808 | tf_op jit(solution)/shard_map/ppermute | solution.py:615
  457.4 6.7 %collective-permute-done.97 = bf16[2,144,576]{2,1,0:T(8,128)(2,1)S(1)} collective-permute-done((bf16[2,144,576]{2,1,0:T(8,128)(2,1)S(1)}, bf16[2,144,576]{2,1,0:T(8,128)(2,1)S(1)}, u32[]{:S(2)}, u32[]{:S(2)}) %collective-permute-start.97) | collective-permute-done | bytes 331808 | tf_op jit(solution)/shard_map/ppermute | solution.py:615
  487.3 8.6 %collective-permute-start.102 = (bf16[144,576]{1,0:T(8,128)(2,1)S(1)}, bf16[144,576]{1,0:T(8,128)(2,1)S(1)}, u32[]{:S(2)}, u32[]{:S(2)}) collective-permute-start(bf16[144,576]{1,0:T(8,128)(2,1)S(1)} %fusion.8), channel_id=1, source_target_pairs={{0,16},{1,17},{2,18},{3,19},{4,20},{5,21},{6,22},{7,23},{8,24},{9,... | collective-permute-start | bytes 497672 | tf_op jit(solution)/shard_map/ppermute | solution.py:615
  495.9 6.4 %collective-permute-done.91 = bf16[144,576]{1,0:T(8,128)(2,1)S(1)} collective-permute-done((bf16[144,576]{1,0:T(8,128)(2,1)S(1)}, bf16[144,576]{1,0:T(8,128)(2,1)S(1)}, u32[]{:S(2)}, u32[]{:S(2)}) %collective-permute-start.91) | collective-permute-done | bytes 165920 | tf_op jit(solution)/shard_map/ppermute | solution.py:615
  502.5 5.8 %collective-permute-done.102 = bf16[144,576]{1,0:T(8,128)(2,1)S(1)} collective-permute-done((bf16[144,576]{1,0:T(8,128)(2,1)S(1)}, bf16[144,576]{1,0:T(8,128)(2,1)S(1)}, u32[]{:S(2)}, u32[]{:S(2)}) %collective-permute-start.102) | collective-permute-done | bytes 165920 | tf_op jit(solution)/shard_map/ppermute | solution.py:615
  (488 shorter events, 195.1 us)
Async XLA Ops:
  82.4 26.7 %all-to-all-start.1 = ((f32[32,16,128]{2,1,0:T(8,128)}), f32[32,16,128]{2,1,0:T(8,128)S(1)}, u32[]{:S(2)}, u32[]{:S(2)}) async-start(f32[32,16,128]{2,1,0:T(8,128)} %bitcast.49), calls=%async_computation.1 | async-start | bytes 524288 | tf_op jit(solution)/shard_map/all_to_all | solution.py:633
  116.1 43.6 %collective-permute-start.74 = (bf16[256,1152]{1,0:T(8,128)(2,1)}, bf16[256,1152]{1,0:T(8,128)(2,1)}, u32[]{:S(2)}, u32[]{:S(2)}) collective-permute-start(bf16[256,1152]{1,0:T(8,128)(2,1)} %fusion.refs_2_.refs_4_), channel_id=1, source_target_pairs={{0,2},{1,3},{2,0},{3,1},{4,6},{5,7},{6,4},{7,5},{8,10},{9,11},{10,... | collective-permute-start | bytes 1769480 | tf_op jit(solution)/shard_map/ppermute | solution.py:615
  127.5 33.0 %collective-permute-start.63 = (bf16[256,1152]{1,0:T(8,128)(2,1)}, bf16[256,1152]{1,0:T(8,128)(2,1)S(1)}, u32[]{:S(2)}, u32[]{:S(2)}) collective-permute-start(bf16[256,1152]{1,0:T(8,128)(2,1)} %fusion.refs_2_.refs_4_), channel_id=1, source_target_pairs={{0,1},{1,0},{2,3},{3,2},{4,5},{5,4},{6,7},{7,6},{8,9},{9,8},{10,11... | collective-permute-start | bytes 1769480 | tf_op jit(solution)/shard_map/ppermute | solution.py:615
  127.7 47.3 %collective-permute-start.65 = (bf16[288,1152]{1,0:T(8,128)(2,1)S(1)}, bf16[288,1152]{1,0:T(8,128)(2,1)S(1)}, u32[]{:S(2)}, u32[]{:S(2)}) collective-permute-start(bf16[288,1152]{1,0:T(8,128)(2,1)S(1)} %reshape.157.refs_4_), channel_id=1, source_target_pairs={{0,8},{1,9},{2,10},{3,11},{4,12},{5,13},{6,14},{7,15},{8,0},{9,1},... | collective-permute-start | bytes 1990664 | tf_op jit(solution)/shard_map/ppermute | solution.py:615
  129.3 47.2 %collective-permute-start.67 = (bf16[288,1152]{1,0:T(8,128)(2,1)S(1)}, bf16[288,1152]{1,0:T(8,128)(2,1)}, u32[]{:S(2)}, u32[]{:S(2)}) collective-permute-start(bf16[288,1152]{1,0:T(8,128)(2,1)S(1)} %reshape.157.refs_4_), channel_id=1, source_target_pairs={{0,16},{1,17},{2,18},{3,19},{4,20},{5,21},{6,22},{7,23},{8,24},{9,... | collective-permute-start | bytes 1990664 | tf_op jit(solution)/shard_map/ppermute | solution.py:615
  131.8 45.4 %collective-permute-start.69 = (bf16[288,1152]{1,0:T(8,128)(2,1)S(1)}, bf16[288,1152]{1,0:T(8,128)(2,1)}, u32[]{:S(2)}, u32[]{:S(2)}) collective-permute-start(bf16[288,1152]{1,0:T(8,128)(2,1)S(1)} %reshape.157.refs_4_), channel_id=1, source_target_pairs={{0,24},{1,25},{2,26},{3,27},{4,28},{5,29},{6,30},{7,31},{8,16},{9,... | collective-permute-start | bytes 1990664 | tf_op jit(solution)/shard_map/ppermute | solution.py:615
  176.6 30.5 %collective-permute-start.68 = (bf16[288,1152]{1,0:T(8,128)(2,1)}, bf16[288,1152]{1,0:T(8,128)(2,1)}, u32[]{:S(2)}, u32[]{:S(2)}) collective-permute-start(bf16[288,1152]{1,0:T(8,128)(2,1)} %collective-permute-done.67.refs_8_), channel_id=1, source_target_pairs={{0,4},{1,5},{2,6},{3,7},{4,0},{5,1},{6,2},{7,3},{8,12},{9,13},{10,... | collective-permute-start | bytes 1990664 | tf_op jit(solution)/shard_map/ppermute | solution.py:615
  177.2 43.6 %collective-permute-start.70 = (bf16[288,1152]{1,0:T(8,128)(2,1)}, bf16[288,1152]{1,0:T(8,128)(2,1)}, u32[]{:S(2)}, u32[]{:S(2)}) collective-permute-start(bf16[288,1152]{1,0:T(8,128)(2,1)} %collective-permute-done.69.refs_10_), channel_id=1, source_target_pairs={{0,4},{1,5},{2,6},{3,7},{4,0},{5,1},{6,2},{7,3},{8,12},{9,13},{10,... | collective-permute-start | bytes 1990664 | tf_op jit(solution)/shard_map/ppermute | solution.py:615
  178.6 56.6 %collective-permute-start.75 = (bf16[256,1152]{1,0:T(8,128)(2,1)}, bf16[256,1152]{1,0:T(8,128)(2,1)}, u32[]{:S(2)}, u32[]{:S(2)}) collective-permute-start(bf16[256,1152]{1,0:T(8,128)(2,1)} %collective-permute-done.74.refs_2_.refs_6_), channel_id=1, source_target_pairs={{0,1},{1,0},{2,3},{3,2},{4,5},{5,4},{6,7},{7,6},{8,9},{9,8},{10,11... | collective-permute-start | bytes 1769480 | tf_op jit(solution)/shard_map/ppermute | solution.py:615
  178.6 56.6 %collective-permute-start.73 = (bf16[256,1152]{1,0:T(8,128)(2,1)}, bf16[256,1152]{1,0:T(8,128)(2,1)S(1)}, u32[]{:S(2)}, u32[]{:S(2)}) collective-permute-start(bf16[256,1152]{1,0:T(8,128)(2,1)} %collective-permute-done.72.refs_0_.refs_2_), channel_id=1, source_target_pairs={{0,1},{1,0},{2,3},{3,2},{4,5},{5,4},{6,7},{7,6},{8,9},{9,8},{10,11... | collective-permute-start | bytes 1769480 | tf_op jit(solution)/shard_map/ppermute | solution.py:615
  192.8 134.3 %collective-permute-start.81 = (bf16[4,256,288]{1,2,0:T(8,128)(2,1)}, bf16[4,256,288]{1,2,0:T(8,128)(2,1)}, u32[]{:S(2)}, u32[]{:S(2)}) collective-permute-start(bf16[4,256,288]{1,2,0:T(8,128)(2,1)} %copy.45), channel_id=1, source_target_pairs={{0,1},{1,0},{2,3},{3,2},{4,5},{5,4},{6,7},{7,6},{8,9},{9,8},{10,11... | collective-permute-start | bytes 1769480 | tf_op jit(solution)/shard_map/ppermute | solution.py:615
  207.1 120.8 %collective-permute-start.82 = (bf16[4,256,288]{1,2,0:T(8,128)(2,1)}, bf16[4,256,288]{1,2,0:T(8,128)(2,1)}, u32[]{:S(2)}, u32[]{:S(2)}) collective-permute-start(bf16[4,256,288]{1,2,0:T(8,128)(2,1)} %copy.46), channel_id=1, source_target_pairs={{0,1},{1,0},{2,3},{3,2},{4,5},{5,4},{6,7},{7,6},{8,9},{9,8},{10,11... | collective-permute-start | bytes 1769480 | tf_op jit(solution)/shard_map/ppermute | solution.py:615
  235.2 30.2 %collective-permute-start.78 = (bf16[256,1152]{1,0:T(8,128)(2,1)}, bf16[256,1152]{1,0:T(8,128)(2,1)S(1)}, u32[]{:S(2)}, u32[]{:S(2)}) collective-permute-start(bf16[256,1152]{1,0:T(8,128)(2,1)} %get-tuple-element.79), channel_id=1, source_target_pairs={{0,1},{1,0},{2,3},{3,2},{4,5},{5,4},{6,7},{7,6},{8,9},{9,8},{10,11... | collective-permute-start | bytes 1769480 | tf_op jit(solution)/shard_map/ppermute | solution.py:615
  267.4 56.4 %collective-permute-start.109 = (bf16[288,1152]{1,0:T(8,128)(2,1)}, bf16[288,1152]{1,0:T(8,128)(2,1)S(1)}, u32[]{:S(2)}, u32[]{:S(2)}) collective-permute-start(bf16[288,1152]{1,0:T(8,128)(2,1)} %get-tuple-element.116), channel_id=1, source_target_pairs={{0,4},{1,5},{2,6},{3,7},{4,0},{5,1},{6,2},{7,3},{8,12},{9,13},{10,... | collective-permute-start | bytes 1990664 | tf_op jit(solution)/shard_map/ppermute | solution.py:615
  283.4 41.6 %collective-permute-start.107 = (bf16[288,1152]{1,0:T(8,128)(2,1)}, bf16[288,1152]{1,0:T(8,128)(2,1)S(1)}, u32[]{:S(2)}, u32[]{:S(2)}) collective-permute-start(bf16[288,1152]{1,0:T(8,128)(2,1)} %get-tuple-element.114), channel_id=1, source_target_pairs={{0,4},{1,5},{2,6},{3,7},{4,0},{5,1},{6,2},{7,3},{8,12},{9,13},{10,... | collective-permute-start | bytes 1990664 | tf_op jit(solution)/shard_map/ppermute | solution.py:615
  285.2 45.7 %collective-permute-start.71 = (bf16[256,1152]{1,0:T(8,128)(2,1)}, bf16[256,1152]{1,0:T(8,128)(2,1)S(1)}, u32[]{:S(2)}, u32[]{:S(2)}) collective-permute-start(bf16[256,1152]{1,0:T(8,128)(2,1)} %get-tuple-element.73), channel_id=1, source_target_pairs={{0,1},{1,0},{2,3},{3,2},{4,5},{5,4},{6,7},{7,6},{8,9},{9,8},{10,11... | collective-permute-start | bytes 1769480 | tf_op jit(solution)/shard_map/ppermute | solution.py:615
  325.0 74.9 %collective-permute-start.83 = (bf16[8,256,576]{1,2,0:T(8,128)(2,1)}, bf16[8,256,576]{1,2,0:T(8,128)(2,1)}, u32[]{:S(2)}, u32[]{:S(2)}) collective-permute-start(bf16[8,256,576]{1,2,0:T(8,128)(2,1)} %copy.47), channel_id=1, source_target_pairs={{0,1},{1,0},{2,3},{3,2},{4,5},{5,4},{6,7},{7,6},{8,9},{9,8},{10,11... | collective-permute-start | bytes 7077896 | tf_op jit(solution)/shard_map/ppermute | solution.py:615
  327.1 31.0 %collective-permute-start.106 = (bf16[288,1152]{1,0:T(8,128)(2,1)}, bf16[288,1152]{1,0:T(8,128)(2,1)}, u32[]{:S(2)}, u32[]{:S(2)}) collective-permute-start(bf16[288,1152]{1,0:T(8,128)(2,1)} %get-tuple-element.112), channel_id=1, source_target_pairs={{0,4},{1,5},{2,6},{3,7},{4,0},{5,1},{6,2},{7,3},{8,12},{9,13},{10,... | collective-permute-start | bytes 1990664 | tf_op jit(solution)/shard_map/ppermute | solution.py:615
  327.9 30.2 %collective-permute-start.112 = (bf16[288,1152]{1,0:T(8,128)(2,1)}, bf16[288,1152]{1,0:T(8,128)(2,1)}, u32[]{:S(2)}, u32[]{:S(2)}) collective-permute-start(bf16[288,1152]{1,0:T(8,128)(2,1)} %add_convert_fusion.1), channel_id=1, source_target_pairs={{0,24},{1,25},{2,26},{3,27},{4,28},{5,29},{6,30},{7,31},{8,16},{9,... | collective-permute-start | bytes 1990664 | tf_op jit(solution)/shard_map/ppermute | solution.py:615
  330.9 60.4 %collective-permute-start.110 = (bf16[288,1152]{1,0:T(8,128)(2,1)}, bf16[288,1152]{1,0:T(8,128)(2,1)}, u32[]{:S(2)}, u32[]{:S(2)}) collective-permute-start(bf16[288,1152]{1,0:T(8,128)(2,1)} %add_convert_fusion.2), channel_id=1, source_target_pairs={{0,16},{1,17},{2,18},{3,19},{4,20},{5,21},{6,22},{7,23},{8,24},{9,... | collective-permute-start | bytes 1990664 | tf_op jit(solution)/shard_map/ppermute | solution.py:615
  339.0 52.3 %collective-permute-start.108 = (bf16[288,1152]{1,0:T(8,128)(2,1)}, bf16[288,1152]{1,0:T(8,128)(2,1)}, u32[]{:S(2)}, u32[]{:S(2)}) collective-permute-start(bf16[288,1152]{1,0:T(8,128)(2,1)} %add_convert_fusion.3), channel_id=1, source_target_pairs={{0,8},{1,9},{2,10},{3,11},{4,12},{5,13},{6,14},{7,15},{8,0},{9,1},... | collective-permute-start | bytes 1990664 | tf_op jit(solution)/shard_map/ppermute | solution.py:615
  352.2 43.0 %all-to-all-start.3 = ((f32[32,16,128]{2,1,0:T(8,128)}), f32[32,16,128]{2,1,0:T(8,128)}, u32[]{:S(2)}, u32[]{:S(2)}) async-start(f32[32,16,128]{2,1,0:T(8,128)} %bitcast.161), calls=%async_computation.3 | async-start | bytes 524288 | tf_op jit(solution)/shard_map/all_to_all | solution.py:633
  426.3 27.8 %collective-permute-start.84 = (bf16[2,144,576]{2,1,0:T(8,128)(2,1)S(1)}, bf16[2,144,576]{2,1,0:T(8,128)(2,1)S(1)}, u32[]{:S(2)}, u32[]{:S(2)}) collective-permute-start(bf16[2,144,576]{2,1,0:T(8,128)(2,1)S(1)} %copy-done.83), channel_id=1, source_target_pairs={{0,2},{1,3},{2,0},{3,1},{4,6},{5,7},{6,4},{7,5},{8,10},{9,11},{10,... | collective-permute-start | bytes 995336 | tf_op jit(solution)/shard_map/ppermute | solution.py:615
  428.4 37.2 %collective-permute-start.95 = (bf16[2,144,576]{2,1,0:T(8,128)(2,1)S(1)}, bf16[2,144,576]{2,1,0:T(8,128)(2,1)S(1)}, u32[]{:S(2)}, u32[]{:S(2)}) collective-permute-start(bf16[2,144,576]{2,1,0:T(8,128)(2,1)S(1)} %copy-done.79), channel_id=1, source_target_pairs={{0,4},{1,5},{2,6},{3,7},{4,0},{5,1},{6,2},{7,3},{8,12},{9,13},{10,... | collective-permute-start | bytes 995336 | tf_op jit(solution)/shard_map/ppermute | solution.py:615
  (179 other events, 2681.4 us)

commit v2 on v1

--- a/solution.py
+++ b/solution.py
@@ -266,26 +266,67 @@
     return lax.axis_index(names[0]), lax.axis_index(names[1])
 
 
-def start_blocks(half_refs, weight_ref, sems):
+def start_blocks(block_refs, weight_ref, sems):
     column, row = here(AXES)
     row_parts = weight_ref.shape[1]
-    copies = {}
-    for relative, halves in enumerate(half_refs):
-        copies[relative] = []
-        for part, ref in enumerate(halves):
-            height = ref.shape[0]
-            copy = pltpu.make_async_copy(
-                ref,
-                weight_ref.at[
-                    column ^ (relative // row_parts),
-                    row ^ (relative % row_parts),
-                    pl.ds(part * height, height),
-                ],
-                sems.at[relative, part],
-            )
-            copy.start()
-            copies[relative].append(copy)
+    copies = []
+    for relative, ref in enumerate(block_refs):
+        copy = pltpu.make_async_copy(
+            ref,
+            weight_ref.at[column ^ (relative // row_parts), row ^ (relative % row_parts)],
+            sems.at[relative],
+        )
+        copy.start()
+        copies.append(copy)
     return copies
+
+
+class Packing:
+    def __init__(self, half, qkv_cols, proj_cols):
+        self.half, self.qkv_cols, self.proj_cols = half, qkv_cols, proj_cols
+        self.qkv_main, self.proj_main = qkv_cols // 128 * 128, proj_cols // 128 * 128
+        self.qkv_rest, self.proj_rest = qkv_cols - self.qkv_main, proj_cols - self.proj_main
+        self.rest = self.qkv_rest + self.proj_rest
+        self.proj_start = 2 * self.qkv_main
+        self.rest_start = self.proj_start + 2 * self.proj_main
+        self.width = self.rest_start + 2 * self.rest
+
+    def pack(self, qkv, proj):
+        halves = [slice(i * self.half, (i + 1) * self.half) for i in range(2)]
+        return jnp.concatenate(
+            [qkv[rows, : self.qkv_main] for rows in halves]
+            + [proj[rows, : self.proj_main] for rows in halves]
+            + [
+                piece
+                for rows in halves
+                for piece in (qkv[rows, self.qkv_main :], proj[rows, self.proj_main :])
+            ],
+            axis=1,
+        )
+
+    def qkv_of(self, block, side):
+        rest = self.rest_start + side * self.rest
+        return jnp.concatenate(
+            [
+                block[:, side * self.qkv_main : (side + 1) * self.qkv_main],
+                block[:, rest : rest + self.qkv_rest],
+            ],
+            axis=1,
+        )
+
+    def proj_of(self, block, side):
+        main = self.proj_start + side * self.proj_main
+        rest = self.rest_start + side * self.rest + self.qkv_rest
+        return jnp.concatenate(
+            [block[:, main : main + self.proj_main], block[:, rest : rest + self.proj_rest]],
+            axis=1,
+        )
+
+    def unpack(self, block):
+        return tuple(
+            jnp.concatenate([part(block, side) for side in range(2)], axis=0)
+            for part in (self.qkv_of, self.proj_of)
+        )
 
 
 def pair_mask(span, frames, live):
@@ -307,17 +348,21 @@
     return ref[slot // per, rows, (slot % per) * size : (slot % per + 1) * size]
 
 
-def attn_forward_kernel(sizes, *refs):
-    clips, span, frames, width, qkv_cols, proj_cols, chunk = sizes
-    column_parts, row_parts = sizes_parts(refs[-2])
-    blocks = column_parts * row_parts
+def columns_of(ref, rows, index, size):
+    return ref[rows, index * size : (index + 1) * size]
+
+
+def attn_forward_kernel(sizes, packing, *refs):
+    clips, span, frames, width, chunk = sizes
+    blocks = len(refs) - 13
     lengths, tokens, mod = refs[:3]
-    half_refs = [(refs[3 + i], refs[3 + blocks + i]) for i in range(blocks)]
-    hidden, mixed, attended, branch, middle, hidden_two = refs[3 + 2 * blocks : 9 + 2 * blocks]
-    weight, sems = refs[9 + 2 * blocks :]
-    copies = start_blocks(half_refs, weight, sems)
+    block_refs = refs[3 : 3 + blocks]
+    hidden, mixed, probs_out, attended, branch, middle, hidden_two = refs[3 + blocks : 10 + blocks]
+    weight, pieces, sems = refs[10 + blocks :]
+    copies = start_blocks(block_refs, weight, sems)
+    column_parts, row_parts = weight.shape[0], weight.shape[1]
     size = width // HEADS
-    part_width = width // row_parts
+    half, proj_cols = packing.half, packing.proj_cols
     scale = 1.0 / math.sqrt(size)
 
     def first_norm(step, carry):
@@ -325,23 +370,25 @@
         clip_mod = mod[step * chunk // span]
         unit, _ = stats(tokens[rows, :].astype(F32))
         value = (unit * (1.0 + clip_mod[1:2]) + clip_mod[0:1]).astype(LOW)
-        for part in range(row_parts):
-            hidden[part, rows, :] = value[:, part * part_width : (part + 1) * part_width]
+        hidden[rows, :] = value
+        for index in range(2 * row_parts):
+            pieces[index, rows, :] = value[:, index * half : (index + 1) * half]
         return carry
 
     lax.fori_loop(0, clips * span // chunk, first_norm, 0)
     column, row = here(AXES)
     for relative in range(column_parts):
         for other in range(row_parts):
-            for copy in copies[relative * row_parts + other]:
-                copy.wait()
+            copies[relative * row_parts + other].wait()
         place = column ^ relative
-        total = dot_nn(hidden[0], weight[place, 0, :, 0:qkv_cols])
-        for part in range(1, row_parts):
-            total += dot_nn(hidden[part], weight[place, part, :, 0:qkv_cols])
+        total = None
+        for part in range(row_parts):
+            block = weight.at[place, part]
+            for side in range(2):
+                term = dot_nn(pieces[2 * part + side], packing.qkv_of(block, side))
+                total = term if total is None else total + term
         mixed[place] = total.astype(LOW)
 
-    per = part_width // size
     for clip in range(clips):
         rows = slice(clip * span, (clip + 1) * span)
         live_mask = pair_mask(span, frames, lengths[clip])
@@ -352,15 +399,19 @@
                 live_mask,
                 scale,
             )
+            probs_out[clip, head] = probs
             value = dot_nn(probs.astype(LOW), head_slices(mixed, 2, head, rows, size))
-            attended[head // per, rows, (head % per) * size : (head % per + 1) * size] = (
-                value.astype(LOW)
-            )
-
+            attended[rows, head * size : (head + 1) * size] = value.astype(LOW)
+
+    for index in range(2 * row_parts):
+        pieces[index] = attended[:, index * half : (index + 1) * half]
     for place in range(column_parts):
-        total = dot_nn(attended[0], weight[place, 0, :, qkv_cols : qkv_cols + proj_cols])
-        for part in range(1, row_parts):
-            total += dot_nn(attended[part], weight[place, part, :, qkv_cols : qkv_cols + proj_cols])
+        total = None
+        for part in range(row_parts):
+            block = weight.at[place, part]
+            for side in range(2):
+                term = dot_nn(pieces[2 * part + side], packing.proj_of(block, side))
+                total = term if total is None else total + term
         branch[:, place * proj_cols : (place + 1) * proj_cols] = total
 
     def second_norm(step, carry):
@@ -375,25 +426,28 @@
     lax.fori_loop(0, clips * span // chunk, second_norm, 0)
 
 
-def sizes_parts(weight_ref):
-    return weight_ref.shape[0], weight_ref.shape[1]
-
-
-def attn_backward_kernel(sizes, *refs):
-    clips, span, frames, width, qkv_cols, proj_cols, chunk = sizes
-    column_parts, row_parts = sizes_parts(refs[-5])
-    blocks = column_parts * row_parts
-    lengths, tokens, cotangent, mod, middle, branch, mixed, grad_own, grad_far = refs[:9]
-    half_refs = [(refs[9 + i], refs[9 + blocks + i]) for i in range(blocks)]
-    input_grad, d_both, d_mod = refs[9 + 2 * blocks : 12 + 2 * blocks]
-    weight, sems, d_middle, d_attended, d_hidden = refs[12 + 2 * blocks :]
-    copies = start_blocks(half_refs, weight, sems)
-    size = width // HEADS
-    part_width = width // row_parts
-    scale = 1.0 / math.sqrt(size)
+def norm_back(grad, values, scale_row):
+    unit, inverse = stats(values)
+    d_unit = grad * (1.0 + scale_row)
+    d_value = inverse * (
+        d_unit
+        - jnp.mean(d_unit, -1, keepdims=True)
+        - unit * jnp.mean(d_unit * unit, -1, keepdims=True)
+    )
+    return unit, d_value
+
+
+def proj_backward_kernel(sizes, packing, *refs):
+    clips, span, frames, width, chunk = sizes
+    blocks = len(refs) - 13
+    cotangent, mod, middle, branch, grad_own, grad_far = refs[:6]
+    d_middle, d_branch, d_attended, d_mod = refs[6 + blocks : 10 + blocks]
+    weight, pieces, sems = refs[10 + blocks :]
+    copies = start_blocks(refs[6 : 6 + blocks], weight, sems)
+    column_parts, row_parts = weight.shape[0], weight.shape[1]
+    half, proj_cols = packing.half, packing.proj_cols
+    zero_row = jnp.zeros((1, width), F32)
     steps = span // chunk
-    zero_row = jnp.zeros((1, width), F32)
-
     for clip in range(clips):
         clip_mod = mod[clip]
 
@@ -401,19 +455,13 @@
             d_shift, d_scale, d_gate = carry
             rows = pl.ds(pl.multiple_of(clip * span + step * chunk, chunk), chunk)
             grad = grad_own[rows, :] + grad_far[rows, :].astype(F32)
-            unit, inverse = stats(middle[rows, :])
-            d_unit = grad * (1.0 + clip_mod[4:5])
-            d_value = cotangent[rows, :].astype(F32) + inverse * (
-                d_unit
-                - jnp.mean(d_unit, -1, keepdims=True)
-                - unit * jnp.mean(d_unit * unit, -1, keepdims=True)
-            )
+            unit, d_value = norm_back(grad, middle[rows, :], clip_mod[4:5])
+            d_value = cotangent[rows, :].astype(F32) + d_value
             d_middle[rows, :] = d_value
-            d_branch = (d_value * clip_mod[2:3]).astype(LOW)
+            low = (d_value * clip_mod[2:3]).astype(LOW)
+            d_branch[rows, :] = low
             for place in range(column_parts):
-                d_both[place, rows, qkv_cols : qkv_cols + proj_cols] = d_branch[
-                    :, place * proj_cols : (place + 1) * proj_cols
-                ]
+                pieces[place, rows, :] = low[:, place * proj_cols : (place + 1) * proj_cols]
             return (
                 d_shift + jnp.sum(grad, 0, keepdims=True),
                 d_scale + jnp.sum(grad * unit, 0, keepdims=True),
@@ -421,50 +469,69 @@
             )
 
         sums = lax.fori_loop(0, steps, second_back, (zero_row, zero_row, zero_row))
-        d_mod[clip, 2:3, :] = sums[2]
-        d_mod[clip, 3:4, :] = sums[0]
-        d_mod[clip, 4:5, :] = sums[1]
-        d_mod[clip, 5:6, :] = zero_row
-
-    for group in copies.values():
-        for copy in group:
-            copy.wait()
-
-    proj = slice(qkv_cols, qkv_cols + proj_cols)
+        d_mod[clip, 0:1, :] = sums[2]
+        d_mod[clip, 1:2, :] = sums[0]
+        d_mod[clip, 2:3, :] = sums[1]
+
+    for copy in copies:
+        copy.wait()
     for part in range(row_parts):
-        total = dot_nt(d_both[0, :, proj], weight[0, part, :, proj])
-        for place in range(1, column_parts):
-            total += dot_nt(d_both[place, :, proj], weight[place, part, :, proj])
-        d_attended[part] = total.astype(LOW)
-
-    per = part_width // size
+        for side in range(2):
+            total = None
+            for place in range(column_parts):
+                term = dot_nt(pieces[place], packing.proj_of(weight.at[place, part], side))
+                total = term if total is None else total + term
+            start = (2 * part + side) * half
+            d_attended[:, start : start + half] = total.astype(LOW)
+
+
+def attn_backward_kernel(sizes, *refs):
+    clips, span, frames, width, qkv_cols = sizes
+    mixed, probs_ref, d_attended, d_mixed = refs
+    size = width // HEADS
+    scale = 1.0 / math.sqrt(size)
+    cols = qkv_cols // size
     for clip in range(clips):
         rows = slice(clip * span, (clip + 1) * span)
-        live_mask = pair_mask(span, frames, lengths[clip])
         for head in range(HEADS):
             queries = head_slices(mixed, 0, head, rows, size)
             keys = head_slices(mixed, 1, head, rows, size)
             values = head_slices(mixed, 2, head, rows, size)
-            probs = head_probs(queries, keys, live_mask, scale)
-            grad = d_attended[head // per, rows, (head % per) * size : (head % per + 1) * size]
+            probs = probs_ref[clip, head]
+            grad = columns_of(d_attended, rows, head, size)
             d_value = dot_tn(probs.astype(LOW), grad)
             d_probs = dot_nt(grad, values)
             d_scores = (probs * (d_probs - jnp.sum(probs * d_probs, -1, keepdims=True))).astype(LOW)
             d_query = dot_nn(d_scores, keys) * scale
             d_key = dot_tn(d_scores, queries) * scale
-            cols = qkv_cols // size
             for which, piece in enumerate((d_query, d_key, d_value)):
                 slot = which * HEADS + head
-                d_both[
-                    slot // cols, rows, (slot % cols) * size : (slot % cols + 1) * size
-                ] = piece.astype(LOW)
-
+                place, start = slot // cols, (slot % cols) * size
+                d_mixed[place, rows, start : start + size] = piece.astype(LOW)
+
+
+def qkv_backward_kernel(sizes, packing, *refs):
+    clips, span, frames, width, chunk = sizes
+    blocks = len(refs) - 9
+    tokens, mod, d_middle, d_mixed = refs[:4]
+    input_grad, d_mod = refs[4 + blocks : 6 + blocks]
+    weight, d_hidden, sems = refs[6 + blocks :]
+    copies = start_blocks(refs[4 : 4 + blocks], weight, sems)
+    column_parts, row_parts = weight.shape[0], weight.shape[1]
+    half, qkv_cols = packing.half, packing.qkv_cols
+    for copy in copies:
+        copy.wait()
     for part in range(row_parts):
-        total = dot_nt(d_both[0, :, 0:qkv_cols], weight[0, part, :, 0:qkv_cols])
-        for place in range(1, column_parts):
-            total += dot_nt(d_both[place, :, 0:qkv_cols], weight[place, part, :, 0:qkv_cols])
-        d_hidden[:, part * part_width : (part + 1) * part_width] = total
-
+        for side in range(2):
+            total = None
+            for place in range(column_parts):
+                term = dot_nt(
+                    d_mixed[place, :, 0:qkv_cols], packing.qkv_of(weight.at[place, part], side)
+                )
+                total = term if total is None else total + term
+            start = (2 * part + side) * half
+            d_hidden[:, start : start + half] = total
+    zero_row = jnp.zeros((1, width), F32)
     for clip in range(clips):
         clip_mod = mod[clip]
 
@@ -472,59 +539,52 @@
             d_shift, d_scale = carry
             rows = pl.ds(pl.multiple_of(clip * span + step * chunk, chunk), chunk)
             grad = d_hidden[rows, :]
-            unit, inverse = stats(tokens[rows, :].astype(F32))
-            d_unit = grad * (1.0 + clip_mod[1:2])
-            input_grad[rows, :] = (
-                d_middle[rows, :]
-                + inverse
-                * (
-                    d_unit
-                    - jnp.mean(d_unit, -1, keepdims=True)
-                    - unit * jnp.mean(d_unit * unit, -1, keepdims=True)
-                )
-            ).astype(LOW)
+            unit, d_value = norm_back(grad, tokens[rows, :].astype(F32), clip_mod[1:2])
+            input_grad[rows, :] = (d_middle[rows, :] + d_value).astype(LOW)
             return (
                 d_shift + jnp.sum(grad, 0, keepdims=True),
                 d_scale + jnp.sum(grad * unit, 0, keepdims=True),
             )
 
-        sums = lax.fori_loop(0, steps, first_back, (zero_row, zero_row))
+        sums = lax.fori_loop(0, span // chunk, first_back, (zero_row, zero_row))
         d_mod[clip, 0:1, :] = sums[0]
         d_mod[clip, 1:2, :] = sums[1]
 
 
-def attn_weight_kernel(sizes, *refs):
-    qkv_cols, proj_cols, half = sizes
-    own, far = refs[:3], refs[3:6]
-    outs = refs[6:]
-    column_parts, row_parts = own[2].shape[0], own[0].shape[0]
+def attn_weight_kernel(packing, *refs):
+    own, far, outs = refs[:4], refs[4:8], refs[8:-3]
+    hidden_t, attended_t, d_pieces = refs[-3:]
+    half, qkv_cols, proj_cols = packing.half, packing.qkv_cols, packing.proj_cols
+    row_count = own[0].shape[0]
+    column_parts = own[2].shape[0]
+    row_parts = own[0].shape[1] // (2 * half)
+    for start, group in ((0, own), (row_count, far)):
+        hidden_t[:, start : start + row_count] = group[0][...].T
+        attended_t[:, start : start + row_count] = group[1][...].T
+        for place in range(column_parts):
+            d_pieces[place, start : start + row_count, :] = columns_of(
+                group[3], slice(None), place, proj_cols
+            )
     column, row = here(AXES)
-    for other in range(row_parts // 2):
-        part = row ^ (2 * other)
-        for relative in range(column_parts):
-            place = column ^ relative
-            x_bit, z_bits = relative % 2, relative // 2
-            groups = column_parts // 2
-            first = outs[other * groups + z_bits]
-            second = outs[(2 + x_bit) * groups + z_bits]
-            total = dot_tn(own[0][part], own[2][place, :, 0:qkv_cols]) + dot_tn(
-                far[0][part], far[2][place, :, 0:qkv_cols]
-            )
-            first[x_bit, :, 0:qkv_cols] = total[:half].astype(LOW)
-            second[other, :, 0:qkv_cols] = total[half:].astype(LOW)
-            proj = slice(qkv_cols, qkv_cols + proj_cols)
-            total = dot_tn(own[1][part], own[2][place, :, proj]) + dot_tn(
-                far[1][part], far[2][place, :, proj]
-            )
-            first[x_bit, :, proj] = total[:half].astype(LOW)
-            second[other, :, proj] = total[half:].astype(LOW)
+    for relative in range(column_parts):
+        place = column ^ relative
+        d_qkv = jnp.concatenate(
+            [own[2][place, :, 0:qkv_cols], far[2][place, :, 0:qkv_cols]], axis=0
+        )
+        d_proj = d_pieces[place]
+        x_bit, z_bits = relative % 2, relative // 2
+        for other in range(row_parts // 2):
+            rows = pl.ds(pl.multiple_of((row ^ (2 * other)) * 2 * half, 16), 2 * half)
+            qkv = dot_nn(hidden_t[rows, :], d_qkv)
+            proj = dot_nn(attended_t[rows, :], d_proj)
+            first, second = (other, x_bit) if z_bits % 2 == 0 else (x_bit, other)
+            outs[2 * z_bits + first][second] = packing.pack(qkv, proj).astype(LOW)
 
 
 def feed_kernel(chunk, *refs):
     hidden, d_outs = refs[0:2], refs[2:4]
-    blocks = refs[4:-7]
-    outs, blocks = blocks[-8:], blocks[:-8]
-    up_weight, down_weight, sems, up_proj, d_activ, activ_s, d_up_s = refs[-7:]
+    blocks, outs = refs[4:-13], refs[-13:-5]
+    up_weight, down_weight, sems, up_proj, d_activ = refs[-5:]
     activ, d_up, d_hidden, partial = outs[0:2], outs[2:4], outs[4:6], outs[6:8]
     column, _ = here(AXES)
     copies = []
@@ -597,6 +657,32 @@
         copy.wait()
 
 
+def prepare_kernel(packing, sub, *refs):
+    timesteps, labels, time_table, class_table, qkv, proj_t, up, down_t, packed, cond, send = refs
+    packed[...] = packing.pack(qkv[...], proj_t[...].T)
+    row_parts = send.shape[0]
+    clips = cond.shape[0]
+
+    def look_up(indices, table):
+        count = table.shape[0]
+        row = lax.broadcasted_iota(jnp.int32, (16, count), 0)
+        column = lax.broadcasted_iota(jnp.int32, (16, count), 1)
+        picked = jnp.zeros((16, count), jnp.bool_)
+        for clip in range(clips):
+            picked = picked | ((row == clip) & (column == indices[clip]))
+        return dot_nn(picked.astype(F32).astype(LOW), table[...])
+
+    embedded = look_up(timesteps, time_table) + look_up(labels, class_table)
+    cond[...] = (embedded * (1.0 / (1.0 + jnp.exp(-embedded))))[:clips].astype(LOW)
+    up_t = up[...].T
+    pairs = send.shape[3] // sub
+    for part in range(row_parts):
+        send[part, 0] = up_t[part * sub : (part + 1) * sub, :]
+        for pair in range(pairs):
+            start = (pair * row_parts + part) * sub
+            send[part, 1, :, pair * sub : (pair + 1) * sub] = down_t[:, start : start + sub]
+
+
 VMEM_SPEC = pl.BlockSpec(memory_space=pltpu.VMEM)
 SMEM_SPEC = pl.BlockSpec(memory_space=pltpu.SMEM)
 ANY_SPEC = pl.BlockSpec(memory_space=pl.ANY)
@@ -607,23 +693,16 @@
     return jax.ShapeDtypeStruct(dims, kind)
 
 
-def cost(flops, moved, special=0):
-    return pl.CostEstimate(flops=flops, bytes_accessed=moved, transcendentals=special)
+def cost(micros):
+    return pl.CostEstimate(flops=1000, bytes_accessed=int(micros * 3_000_000), transcendentals=0)
+
+
+def after(value, *others):
+    return lax.optimization_barrier((value,) + others)[0]
 
 
 def swap(value, mask, count):
     return lax.ppermute(value, AXES, [(i, i ^ mask) for i in range(count)])
-
-
-def spread(block, stages, count):
-    have = {0: block}
-    for masks in stages:
-        fresh = dict(have)
-        for mask in masks:
-            for relative, value in have.items():
-                fresh[relative ^ mask] = swap(value, mask, count)
-        have = fresh
-    return have
 
 
 def padded_exchange(rows, count):
@@ -661,76 +740,124 @@
     sub = up_weight.shape[1] // row_parts
     x_mask = row_parts
     z_masks = tuple(row_parts * 2 * i for i in range(1, column_parts // 2))
-    half = height // 2
-
-    own_block = jnp.concatenate([qkv_weight, proj_weight], axis=1)
-    first_half = spread(own_block[:half], (z_masks, (x_mask,), (2,), (1,)), count)
-    second_half = spread(own_block[half:], (z_masks, (2,), (x_mask,), (1,)), count)
-    halves = [first_half[i] for i in range(count)] + [second_half[i] for i in range(count)]
-
-    cond_rows = [
-        lax.dynamic_slice_in_dim(time_table, timesteps[i], 1, 0).astype(F32)
-        + lax.dynamic_slice_in_dim(class_table, labels[i], 1, 0).astype(F32)
-        for i in range(clips)
-    ]
-    cond_low = jax.nn.silu(jnp.concatenate(cond_rows, 0)).astype(LOW)
+    packing = Packing(height // 2, qkv_cols, proj_cols)
+
+    packed, cond_low, both_send = pl.pallas_call(
+        functools.partial(prepare_kernel, packing, sub),
+        out_shape=(
+            shape_of((height // 2, packing.width)),
+            shape_of((clips, width)),
+            shape_of((row_parts, 2, sub, height)),
+        ),
+        in_specs=[SMEM_SPEC] * 2 + [VMEM_SPEC] * 6,
+        out_specs=[VMEM_SPEC] * 3,
+        compiler_params=PARAMS,
+        cost_estimate=cost(3),
+        name="prepare",
+    )(timesteps, labels, time_table, class_table, qkv_weight, proj_weight.T, up_weight, down_weight.T)
+
+    z_one, z_two, z_three = z_masks
+    y_mask, c_mask = 2, 1
+    ada_cols = ada_weight.shape[1]
+    have = {0: packed}
+
+    def move(mask, *sources):
+        for source in sources:
+            have[source ^ mask] = swap(have[source], mask, count)
+        return [source ^ mask for source in sources]
+
+    def close(keys, *others):
+        got = lax.optimization_barrier(tuple(have[key] for key in keys) + others)
+        have.update(zip(keys, got))
+        return got[len(keys) :]
+
+    for mask in z_masks + (x_mask, y_mask):
+        move(mask, 0)
     cond_send = cond_low.reshape(clips, row_parts, part_width).transpose(1, 0, 2)
     cond_send = jnp.broadcast_to(
         cond_send.reshape(1, row_parts, clips * part_width),
         (column_parts, row_parts, clips * part_width),
     ).reshape(count, clips * part_width)
     cond_all = padded_exchange(cond_send, count).reshape(count * clips, part_width)
-    ada_cols = ada_weight.shape[1]
+    cond_all, both_send = close([z_one, x_mask, y_mask], cond_all, both_send)
+
     mod_part = jnp.dot(cond_all, ada_weight, preferred_element_type=F32)
     mod_got = padded_exchange(mod_part.reshape(count, clips * ada_cols), count)
+    both_got = lax.all_to_all(both_send, "fsdp", 0, 0, tiled=True)
+    own_feed = both_got.transpose(1, 2, 0, 3).reshape(2 * sub, width)
+    keys = move(x_mask, z_one) + move(y_mask, z_one, x_mask) + move(c_mask, 0, x_mask, y_mask)
+    mod_got, own_feed = close(keys + [z_two, z_three], mod_got, own_feed)
     mod_own = jnp.sum(mod_got.reshape(column_parts, row_parts, clips, ada_cols), axis=1)
     mod = mod_own.transpose(1, 0, 2).reshape(clips, 6, width)
 
-    up_send = up_weight.reshape(height, row_parts, sub).transpose(1, 2, 0)
-    down_send = (
-        down_weight.reshape(-1, row_parts, sub, proj_cols)
-        .transpose(1, 3, 0, 2)
-        .reshape(row_parts, proj_cols, -1)
-    )
-    both_send = jnp.stack([up_send, down_send], axis=1)
-    both_send, _ = lax.optimization_barrier((both_send, second_half[z_masks[0]]))
-    both_got = lax.all_to_all(both_send, "fsdp", 0, 0, tiled=True)
-    own_feed = both_got.transpose(1, 2, 0, 3).reshape(2 * sub, width)
-    feed = spread(own_feed, (z_masks, (x_mask,)), count)
+    z_of = [i // (2 * row_parts) for i in range(count)]
+    inner = [i for i in range(count) if z_of[i] in (1, 2)]
+
+    def inner_pairs(mask):
+        return [(i, i ^ mask) for i in inner]
+
+    feed = {0: own_feed, z_one: swap(own_feed, z_one, count)}
+    feed_inner = lax.ppermute(own_feed, AXES, inner_pairs(z_three))
+    feed[x_mask] = swap(own_feed, x_mask, count)
+    keys = move(x_mask, z_two, z_three) + move(y_mask, z_two, z_one ^ x_mask)
+    keys += move(c_mask, z_one, z_one ^ x_mask, z_one ^ y_mask, x_mask ^ y_mask)
+    feed[z_one], feed_inner, feed[x_mask] = close(keys, feed[z_one], feed_inner, feed[x_mask])
+
+    feed_two = lax.ppermute(feed[z_one], AXES, inner_pairs(z_three))
+    feed_two_outer = lax.ppermute(feed_inner, AXES, inner_pairs(z_one))
+    feed[z_one ^ x_mask] = swap(feed[z_one], x_mask, count)
+    keys = move(y_mask, z_two ^ x_mask, z_three)
+    keys += move(
+        c_mask, z_two, z_two ^ x_mask, z_two ^ y_mask, z_three, z_three ^ x_mask, z_one ^ x_mask ^ y_mask
+    )
+    feed_two, feed_two_outer, feed[z_one ^ x_mask] = close(
+        keys, feed_two, feed_two_outer, feed[z_one ^ x_mask]
+    )
+    feed[z_two] = feed_two + feed_two_outer
+    feed_three = lax.ppermute(feed[z_two], AXES, inner_pairs(z_one))
+    feed[z_two ^ x_mask] = swap(feed[z_two], x_mask, count)
+    move(y_mask, z_three ^ x_mask)
+    move(c_mask, z_two ^ x_mask ^ y_mask, z_three ^ y_mask)
+    move(c_mask, z_three ^ x_mask ^ y_mask)
+    feed[z_three] = feed_inner + feed_three
+    feed[z_three ^ x_mask] = swap(feed[z_three], x_mask, count)
+    blocks = [have[i] for i in range(count)]
     feed_blocks = [feed[i * row_parts] for i in range(column_parts)]
 
     tokens = inputs.reshape(row_count, width)
     cotangent = out_cotangent.reshape(row_count, width)
-    sizes = (clips, span, frames, width, qkv_cols, proj_cols, 32)
+    sizes = (clips, span, frames, width, 32)
     full = (row_count, width)
-    weight_scratch = [
-        pltpu.VMEM((column_parts, row_parts, height, qkv_cols + proj_cols), LOW),
-        pltpu.SemaphoreType.DMA((count, 2)),
-    ]
-    hidden, mixed, attended, branch, middle, hidden_two = pl.pallas_call(
-        functools.partial(attn_forward_kernel, sizes),
+    weight_scratch = pltpu.VMEM((column_parts, row_parts, height // 2, packing.width), LOW)
+    weight_sems = pltpu.SemaphoreType.DMA((count,))
+    hidden, mixed, probs, attended, branch, middle, hidden_two = pl.pallas_call(
+        functools.partial(attn_forward_kernel, sizes, packing),
         out_shape=(
-            shape_of((row_parts, row_count, part_width)),
+            shape_of(full),
             shape_of((column_parts, row_count, qkv_cols)),
-            shape_of((row_parts, row_count, part_width)),
+            shape_of((clips, HEADS, span, span), F32),
+            shape_of(full),
             shape_of(full, F32),
             shape_of(full, F32),
             shape_of(full),
         ),
-        in_specs=[SMEM_SPEC, VMEM_SPEC, VMEM_SPEC] + [ANY_SPEC] * (2 * count),
-        out_specs=[VMEM_SPEC] * 6,
-        scratch_shapes=weight_scratch,
+        in_specs=[SMEM_SPEC, VMEM_SPEC, VMEM_SPEC] + [ANY_SPEC] * count,
+        out_specs=[VMEM_SPEC] * 7,
+        scratch_shapes=[
+            weight_scratch,
+            pltpu.VMEM((2 * row_parts, row_count, height // 2), LOW),
+            weight_sems,
+        ],
         compiler_params=PARAMS,
-        cost_estimate=cost(8 * row_count * width * width, 14_000_000),
+        cost_estimate=cost(20),
         name="attn_forward",
-    )(lengths, tokens, mod, *halves)
+    )(lengths, tokens, mod, *blocks)
 
     gate_two = jnp.repeat(mod[:, 5], span, axis=0)
     d_out = (cotangent.astype(F32) * gate_two).astype(LOW)
     d_outs = {0: d_out, 1: swap(d_out, 1, count), 2: swap(d_out, 2, count)}
     d_outs[3] = swap(d_outs[2], 1, count)
     tokens_two = {0: hidden_two, 1: swap(hidden_two, 1, count), 2: swap(hidden_two, 2, count)}
-    tokens_two[3] = swap(tokens_two[2], 1, count)
 
     def feed_call(index, kind, name):
         return pl.pallas_call(
@@ -745,11 +872,9 @@
                 pltpu.SemaphoreType.DMA((column_parts, 2)),
                 pltpu.VMEM((row_count, hidden_part), F32),
                 pltpu.VMEM((row_count, hidden_part), F32),
-                pltpu.VMEM((8, 128), LOW),
-                pltpu.VMEM((8, 128), LOW),
             ],
             compiler_params=PARAMS,
-            cost_estimate=cost(16 * row_count * width * hidden_part, 12_000_000),
+            cost_estimate=cost(14),
             name=name,
         )(
             tokens_two[index],
@@ -760,6 +885,8 @@
         )
 
     near = feed_call(0, F32, "feed_near")
+    tokens_two[2] = after(tokens_two[2], near[0])
+    tokens_two[3] = swap(tokens_two[2], 1, count)
     distant = feed_call(2, F32, "feed_distant")
     activ = list(near[0:2]) + list(distant[0:2])
     d_up = list(near[2:4]) + list(distant[2:4])
@@ -767,10 +894,12 @@
     def join(first, second, third, fourth):
         far = third.astype(F32) + swap(fourth, 1, count).astype(F32)
         mine = first.astype(F32) + swap(second, 1, count).astype(F32)
-        return mine, swap(far.astype(LOW), 2, count)
-
-    grad_own, grad_far = join(near[4], near[5], distant[4], distant[5])
-    out_own, out_far = join(near[6], near[7], distant[6], distant[7])
+        return mine, far.astype(LOW)
+
+    grad_own, grad_send = join(near[4], near[5], distant[4], distant[5])
+    out_own, out_send = join(near[6], near[7], distant[6], distant[7])
+    grad_far = swap(grad_send, 2, count)
+    out_far = swap(after(out_send, grad_far), 2, count)
 
     feed_grads = pl.pallas_call(
         functools.partial(feed_weight_kernel, 128),
@@ -783,67 +912,107 @@
             pltpu.SemaphoreType.DMA((column_parts, 2)),
         ],
         compiler_params=PARAMS,
-        cost_estimate=cost(16 * row_count * width * hidden_part, 15_000_000),
+        cost_estimate=cost(14),
         name="feed_weight",
     )(
-        *[tokens_two[i] for i in range(4)],
+        after(tokens_two[0], grad_send),
+        *[tokens_two[i] for i in range(1, 4)],
         *[d_outs[i] for i in range(4)],
         *activ,
         *d_up,
     )
 
-    input_grad, d_both, d_mod = pl.pallas_call(
-        functools.partial(attn_backward_kernel, sizes),
+    groups = column_parts // 2
+
+    def fold(keep, got):
+        return keep.astype(F32) + got.astype(F32)
+
+    feed_x = {i: swap(feed_grads[2 * i + 1], x_mask, count) for i in reversed(range(groups))}
+    feed_sums = {i: fold(feed_grads[2 * i], feed_x[i]) for i in range(groups)}
+    feed_z = {i: swap(feed_sums[i].astype(LOW), z_masks[i - 1], count) for i in range(1, groups)}
+
+    d_middle, d_branch, d_attended, d_mod_two = pl.pallas_call(
+        functools.partial(proj_backward_kernel, sizes, packing),
         out_shape=(
+            shape_of(full, F32),
             shape_of(full),
-            shape_of((column_parts, row_count, qkv_cols + proj_cols)),
-            shape_of((clips, 6, width), F32),
+            shape_of(full),
+            shape_of((clips, 3, width), F32),
         ),
-        in_specs=[SMEM_SPEC] + [VMEM_SPEC] * 8 + [ANY_SPEC] * (2 * count),
-        out_specs=[VMEM_SPEC] * 3,
-        scratch_shapes=weight_scratch
-        + [
-            pltpu.VMEM(full, F32),
-            pltpu.VMEM((row_parts, row_count, part_width), LOW),
-            pltpu.VMEM(full, F32),
+        in_specs=[VMEM_SPEC] * 6 + [ANY_SPEC] * count,
+        out_specs=[VMEM_SPEC] * 4,
+        scratch_shapes=[
+            weight_scratch,
+            pltpu.VMEM((column_parts, row_count, proj_cols), LOW),
+            weight_sems,
         ],
         compiler_params=PARAMS,
-        cost_estimate=cost(8 * row_count * width * width, 16_000_000),
+        cost_estimate=cost(10),
+        name="proj_backward",
+    )(cotangent, mod, middle, branch, grad_own, grad_far, *blocks)
+
+    d_mixed = pl.pallas_call(
+        functools.partial(attn_backward_kernel, (clips, span, frames, width, qkv_cols)),
+        out_shape=shape_of((column_parts, row_count, -(-qkv_cols // 128) * 128)),
+        in_specs=[VMEM_SPEC] * 3,
+        out_specs=VMEM_SPEC,
+        compiler_params=PARAMS,
+        cost_estimate=cost(15),
         name="attn_backward",
-    )(lengths, tokens, cotangent, mod, middle, branch, mixed, grad_own, grad_far, *halves)
-
-    groups = column_parts // 2
+    )(mixed, probs, after(d_attended, feed_x[3]))
+
+    input_grad, d_mod_one = pl.pallas_call(
+        functools.partial(qkv_backward_kernel, sizes, packing),
+        out_shape=(shape_of(full), shape_of((clips, 2, width), F32)),
+        in_specs=[VMEM_SPEC] * 4 + [ANY_SPEC] * count,
+        out_specs=[VMEM_SPEC] * 2,
+        scratch_shapes=[weight_scratch, pltpu.VMEM(full, F32), weight_sems],
+        compiler_params=PARAMS,
+        cost_estimate=cost(14),
+        name="qkv_backward",
+    )(tokens, mod, d_middle, after(d_mixed, feed_x[2]), *blocks)
+
+    own_side = (hidden, attended, d_mixed, d_branch)
     attn_grads = pl.pallas_call(
-        functools.partial(attn_weight_kernel, (qkv_cols, proj_cols, half)),
-        out_shape=[shape_of((2, half, qkv_cols + proj_cols))] * (4 * groups),
-        in_specs=[VMEM_SPEC] * 6,
-        out_specs=[VMEM_SPEC] * (4 * groups),
+        functools.partial(attn_weight_kernel, packing),
+        out_shape=[shape_of((2, height // 2, packing.width))] * (2 * groups),
+        in_specs=[VMEM_SPEC] * 8,
+        out_specs=[VMEM_SPEC] * (2 * groups),
+        scratch_shapes=[
+            pltpu.VMEM((width, 2 * row_count), LOW),
+            pltpu.VMEM((width, 2 * row_count), LOW),
+            pltpu.VMEM((column_parts, 2 * row_count, proj_cols), LOW),
+        ],
         compiler_params=PARAMS,
-        cost_estimate=cost(8 * row_count * width * width, 12_000_000),
+        cost_estimate=cost(10),
         name="attn_weight",
     )(
         hidden,
         attended,
-        d_both,
-        swap(hidden, 1, count),
-        swap(attended, 1, count),
-        swap(d_both, 1, count),
-    )
-
-    def fold(keep, send, mask):
-        return keep.astype(F32) + swap(send, mask, count).astype(F32)
-
-    def last_fold(parts):
-        total = parts[0]
-        for index in range(1, groups):
-            got = swap(parts[index].astype(LOW), z_masks[index - 1], count)
-            total = total + got.astype(F32)
-        return total
-
-    feed_sums = [
-        fold(feed_grads[2 * i], feed_grads[2 * i + 1], x_mask) for i in range(groups)
-    ]
-    feed_sum = last_fold(feed_sums)
+        after(d_mixed, input_grad, feed_x[1], feed_z[3]),
+        d_branch,
+        *[swap(array, 1, count) for array in own_side],
+    )
+
+    orders = [(y_mask, x_mask) if index % 2 == 0 else (x_mask, y_mask) for index in range(groups)]
+    first = {i: swap(attn_grads[2 * i + 1], orders[i][0], count) for i in range(groups)}
+    first[3], first[2] = lax.optimization_barrier((first[3], first[2]))
+    once = {i: fold(attn_grads[2 * i], first[i]) for i in range(groups)}
+    second = {i: swap(once[i][1].astype(LOW), orders[i][1], count) for i in range(groups)}
+    second[3], second[2], first_one, first_zero = lax.optimization_barrier(
+        (second[3], second[2], first[1], first[0])
+    )
+    for i, got in ((1, first_one), (0, first_zero)):
+        once[i] = fold(attn_grads[2 * i], got)
+        second[i] = swap(once[i][1].astype(LOW), orders[i][1], count)
+    attn_sums = [fold(once[i][0], second[i]) for i in range(groups)]
+    attn_sum = attn_sums[0]
+    for i in range(1, groups):
+        attn_sum += swap(attn_sums[i].astype(LOW), z_masks[i - 1], count).astype(F32)
+    qkv_grad, proj_grad = packing.unpack(attn_sum)
+
+    feed_z[2] = after(feed_z[2], second[3])
+    feed_sum = feed_sums[0] + sum(got.astype(F32) for got in feed_z.values())
     back = feed_sum.astype(LOW).reshape(2, sub, row_parts, height).transpose(2, 0, 1, 3)
     back = lax.all_to_all(back, "fsdp", 0, 0, tiled=True)
     up_grad = back[:, 0].transpose(2, 0, 1).reshape(height, row_parts * sub).astype(F32)
@@ -855,24 +1024,10 @@
         .astype(F32)
     )
 
-    def two_folds(keep, send, masks):
-        sums = []
-        for index in range(groups):
-            once = fold(keep[index], send[index], masks[0])
-            low = once[1].astype(LOW)
-            sums.append(fold(once[0], low, masks[1]))
-        return last_fold(sums)
-
-    part = [attn_grads[i * groups : (i + 1) * groups] for i in range(4)]
-    attn_sum = jnp.concatenate(
-        [two_folds(part[0], part[1], (2, x_mask)), two_folds(part[2], part[3], (x_mask, 2))], 0
-    )
-    qkv_grad, proj_grad = attn_sum[:, :qkv_cols], attn_sum[:, qkv_cols:]
-
     ffn_out = out_own + out_far.astype(F32)
     result = (middle + gate_two * ffn_out).astype(LOW).reshape(inputs.shape)
     d_gate_two = jnp.sum((cotangent.astype(F32) * ffn_out).reshape(clips, span, width), axis=1)
-    d_mod = d_mod.at[:, 5].set(d_gate_two)
+    d_mod = jnp.concatenate([d_mod_one, d_mod_two, d_gate_two[:, None]], axis=1)
     mod_send = d_mod.reshape(clips, column_parts, ada_cols).transpose(1, 0, 2)
     mod_send = jnp.broadcast_to(
         mod_send.reshape(column_parts, 1, clips * ada_cols),

time: 522 us -> 435 us (0.83)
  waiting for transfers between devices: 198 us -> 163 us
  starting transfers between devices: 110 us -> 78.2 us
  local copies, waits for them, and re-layouts: 49 us -> 24.5 us
  other arithmetic: 15.4 us -> 24.2 us
  between operations: 10 us -> 2.25 us
  Pallas kernels: 117 us -> 124 us
    ppermute x113 -> x70, waiting for transfers between devices: 198 us -> 129 us  [swap(): return lax.ppermute(value, AXES, [(i, i ^ mask) for i in range(count)])]
    ppermute x113 -> x70, starting transfers between devices: 96 us -> 60.3 us  [swap(): return lax.ppermute(value, AXES, [(i, i ^ mask) for i in range(count)])]
    ppermute x0 -> x4, waiting for transfers between devices: none -> 17.5 us  [the longest x1 10.6 us: fast_body(): feed_two_outer = lax.ppermute(feed_inner, AXES, inner_pairs(z_one))]
    all_to_all x1, waiting for transfers between devices: 0.01 us -> 9.24 us  [fast_body(): both_got = lax.all_to_all(both_send, 'fsdp', 0, 0, tiled=True)]
    ppermute x3 -> x0, local copies, waits for them, and re-layouts: 8.86 us -> none  [swap(): return lax.ppermute(value, AXES, [(i, i ^ mask) for i in range(count)])]
    pallas_call x3 -> x0, local copies, waits for them, and re-layouts: 7.77 us -> none  [the longest x1 4.43 us: fast_body(): pl.pallas_call(functools.partial(attn_backward_kernel, sizes), out_shape=...]
    pallas_call x3 -> x6, Pallas kernels: 74.3 us -> 81.6 us  [the longest x1 28.2 us: fast_body(): pl.pallas_call(functools.partial(attn_forward_kernel, sizes, packing), ou...]
    all_to_all x2, waiting for transfers between devices: 0.01 us -> 6.95 us  [padded_exchange(): got = lax.all_to_all(rows, AXES, 0, 0, tiled=True)]
  transfers between devices with their start and end apart: 117 -> 78, of which waited for: 31 -> 28; matrix products, arithmetic and copies ran while one was open for 11% -> 8% of each run, Pallas kernels for 23% -> 21%
where the time goes in v2:
time: 435 us; the launch traced here: 428 us
  waiting for transfers between devices  163 us (37%)
  Pallas kernels  124 us (29%)
  starting transfers between devices  78.2 us (18%)
  local copies, waits for them, and re-layouts  24.5 us (6%)
  other arithmetic  24.2 us (6%)
  blocking collectives  10.2 us (2%)
    ppermute x70, waiting for transfers between devices, swap(): return lax.ppermute(value, AXES, [(i, i ^ mask) for i in range(count)])  129 us
    ppermute x70, starting transfers between devices, swap(): return lax.ppermute(value, AXES, [(i, i ^ mask) for i in range(count)])  60.3 us
    pallas_call x2, Pallas kernels, feed_call(): pl.pallas_call(functools.partial(feed_kernel, 32), out_shape=[shape_of((r...  28.4 us
    pallas_call x1, Pallas kernels, fast_body(): pl.pallas_call(functools.partial(attn_forward_kernel, sizes, packing), ou...  28.2 us
    pallas_call x1, Pallas kernels, fast_body(): pl.pallas_call(functools.partial(attn_backward_kernel, (clips, span, fram...  15.1 us
    pallas_call x1, Pallas kernels, fast_body(): pl.pallas_call(functools.partial(qkv_backward_kernel, sizes, packing), ou...  14.5 us
    pallas_call x1, Pallas kernels, fast_body(): pl.pallas_call(functools.partial(feed_weight_kernel, 128), out_shape=[sha...  14.3 us
    unnamed x172, local copies, waits for them, and re-layouts  13.5 us
  transfers between devices with their start and end apart: 78, of which 28 were waited for; matrix products, arithmetic and copies ran while one was open for 8% of the time, Pallas kernels for 21%

profile of v2, /device:TPU:0, one launch (start us, length us, event | category | flops | bytes accessed | tf_op | source)
XLA Modules:
  0.0 428.1 jit_solution(13084009081224054124)
XLA Ops:
  11.2 10.2 %all_to_all.25 = bf16[32,8,128]{2,1,0:T(8,128)(2,1)S(1)} all-to-all(bf16[32,8,128]{2,1,0:T(8,128)(2,1)S(1)} %bitcast.116), channel_id=1, replica_groups=mesh['dp'=8,'fsdp'=4] {'dp','fsdp'}, dimensions={0} | all-to-all | bytes 131072 | tf_op jit(solution)/shard_map/all_to_all | solution.py:712
  28.5 9.2 %all-to-all-done.2 = bf16[4,2,144,288]{3,2,1,0:T(8,128)(2,1)S(1)} async-done(((bf16[4,2,144,288]{3,2,1,0:T(8,128)(2,1)}), bf16[4,2,144,288]{3,2,1,0:T(8,128)(2,1)S(1)}, u32[]{:S(2)}, u32[]{:S(2)}) %all-to-all-start.2) | async-done | bytes 663584 | tf_op jit(solution)/shard_map/all_to_all | solution.py:786
  44.7 15.2 %collective-permute-done.9.refs_19_.refs_22_.refs_20_ = bf16[144,1152]{1,0:T(8,128)(2,1)S(1)} collective-permute-done((bf16[144,1152]{1,0:T(8,128)(2,1)S(1)}, bf16[144,1152]{1,0:T(8,128)(2,1)S(1)}, u32[]{:S(2)}, u32[]{:S(2)}) %collective-permute-start.9) | collective-permute-done | bytes 331808 | tf_op jit(solution)/shard_map/ppermute | solution.py:705
  68.4 6.5 %collective-permute-done.11.refs_23_.refs_26_.refs_24_ = bf16[144,1152]{1,0:T(8,128)(2,1)S(1)} collective-permute-done((bf16[144,1152]{1,0:T(8,128)(2,1)S(1)}, bf16[144,1152]{1,0:T(8,128)(2,1)S(1)}, u32[]{:S(2)}, u32[]{:S(2)}) %collective-permute-start.11) | collective-permute-done | bytes 331808 | tf_op jit(solution)/shard_map/ppermute | solution.py:705
  75.7 6.1 %collective-permute-done.12.refs_31_.refs_34_.refs_32_ = bf16[144,1152]{1,0:T(8,128)(2,1)} collective-permute-done((bf16[144,1152]{1,0:T(8,128)(2,1)S(1)}, bf16[144,1152]{1,0:T(8,128)(2,1)}, u32[]{:S(2)}, u32[]{:S(2)}) %collective-permute-start.12) | collective-permute-done | bytes 331808 | tf_op jit(solution)/shard_map/ppermute | solution.py:705
  91.1 8.1 %collective-permute-done.21.refs_5_ = bf16[288,1152]{1,0:T(8,128)(2,1)} collective-permute-done((bf16[288,1152]{1,0:T(8,128)(2,1)S(1)}, bf16[288,1152]{1,0:T(8,128)(2,1)}, u32[]{:S(2)}, u32[]{:S(2)}) %collective-permute-start.21) | collective-permute-done | bytes 663584 | tf_op jit(solution)/shard_map/ppermute | solution.py:705
  111.4 10.6 %collective-permute-done.31 = bf16[288,1152]{1,0:T(8,128)(2,1)S(1)} collective-permute-done((bf16[288,1152]{1,0:T(8,128)(2,1)S(1)}, bf16[288,1152]{1,0:T(8,128)(2,1)S(1)}, u32[]{:S(2)}, u32[]{:S(2)}) %collective-permute-start.31) | collective-permute-done | bytes 663584 | tf_op jit(solution)/shard_map/ppermute | solution.py:807
  126.4 7.5 %collective-permute-done.35.refs_33_.refs_36_.refs_34_ = bf16[144,1152]{1,0:T(8,128)(2,1)} collective-permute-done((bf16[144,1152]{1,0:T(8,128)(2,1)}, bf16[144,1152]{1,0:T(8,128)(2,1)}, u32[]{:S(2)}, u32[]{:S(2)}) %collective-permute-start.35) | collective-permute-done | bytes 331808 | tf_op jit(solution)/shard_map/ppermute | solution.py:705
  134.4 6.8 %collective-permute-done.40 = bf16[288,1152]{1,0:T(8,128)(2,1)} collective-permute-done((bf16[288,1152]{1,0:T(8,128)(2,1)S(1)}, bf16[288,1152]{1,0:T(8,128)(2,1)}, u32[]{:S(2)}, u32[]{:S(2)}) %collective-permute-start.40) | collective-permute-done | bytes 663584 | tf_op jit(solution)/shard_map/ppermute | solution.py:817
  147.2 28.2 %attn_forward.1 = (bf16[256,1152]{1,0:T(8,128)(2,1)}, bf16[8,256,432]{2,1,0:T(8,128)(2,1)}, f32[2,16,128,128]{3,2,1,0:T(8,128)}, bf16[256,1152]{1,0:T(8,128)(2,1...) custom-call(s32[2]{0:T(128)} %refs_0_.3, bf16[256,1152]{1,0:T(8,128)(2,1)} %bitcast.109, ...), custom_call_target="tpu_custom_call" | custom-call | flops 1000 | bytes 60000000 | tf_op jit(solution)/shard_map/attn_forward/pallas_call | solution.py:833
  179.4 14.2 %feed_near.1 = (bf16[256,1152]{1,0:T(8,128)(2,1)}, bf16[256,1152]{1,0:T(8,128)(2,1)}, bf16[256,1152]{1,0:T(8,128)(2,1)}, bf16[256,1152]{1,0:T(8,128)(2,1)}, f32[...) custom-call(bf16[256,1152]{1,0:T(8,128)(2,1)} %get-tuple-element.163.refs_0_, ...), custom_call_target="tpu_custom_call" | custom-call | flops 1000 | bytes 42000000 | tf_op jit(solution)/shard_map/feed_near/pallas_call | solution.py:863
  196.5 14.2 %feed_distant.1 = (bf16[256,1152]{1,0:T(8,128)(2,1)}, bf16[256,1152]{1,0:T(8,128)(2,1)}, bf16[256,1152]{1,0:T(8,128)(2,1)}, bf16[256,1152]{1,0:T(8,128)(2,1)}, f...) custom-call(bf16[256,1152]{1,0:T(8,128)(2,1)} %copy-done.51, ...), custom_call_target="tpu_custom_call" | custom-call | flops 1000 | bytes 42000000 | tf_op jit(solution)/shard_map/feed_distant/pallas_call | solution.py:863
  214.4 14.3 %feed_weight.1 = (bf16[288,1152]{1,0:T(8,128)(2,1)}, bf16[288,1152]{1,0:T(8,128)(2,1)}, bf16[288,1152]{1,0:T(8,128)(2,1)}, bf16[288,1152]{1,0:T(8,128)(2,1)}, bf...) custom-call(bf16[256,1152]{1,0:T(8,128)(2,1)} %get-tuple-element.163, ...), custom_call_target="tpu_custom_call" | custom-call | flops 1000 | bytes 42000000 | tf_op jit(solution)/shard_map/feed_weight/pallas_call | solution.py:904
  231.7 13.6 %collective-permute-done.49.refs_5_ = bf16[256,1152]{1,0:T(8,128)(2,1)S(1)} collective-permute-done((bf16[256,1152]{1,0:T(8,128)(2,1)S(1)}, bf16[256,1152]{1,0:T(8,128)(2,1)S(1)}, u32[]{:S(2)}, u32[]{:S(2)}) %collective-permute-start.49) | collective-permute-done | bytes 589856 | tf_op jit(solution)/shard_map/ppermute | solution.py:705
  246.1 10.0 %proj_backward.1 = (f32[256,1152]{1,0:T(8,128)}, bf16[256,1152]{1,0:T(8,128)(2,1)}, bf16[256,1152]{1,0:T(8,128)(2,1)}, f32[2,3,1152]{2,1,0:T(4,128)}) custom-call(bf16[256,1152]{1,0:T(8,128)(2,1)} %bitcast.105, f32[2,6,1152]{2,1,0:T(8,128)} %copy-done.55, f32[256,1152]{1,0:T(8,128)} %get-tuple-element.141.refs_2_, f32[256,1152]{1,0:T(8,128)} %get-tuple-element.156.refs_3_, ...), custom_call_target="tpu_custom_call" | custom-call | flops 1000 | bytes 30000000 | tf_op jit(solution)/shard_map/proj_backward/pallas_call | solution.py:934
  256.1 15.1 %attn_backward.1.refs_3_.refs_2_ = bf16[8,256,512]{2,1,0:T(8,128)(2,1)} custom-call(bf16[8,256,432]{2,1,0:T(8,128)(2,1)} %get-tuple-element.160.refs_0_, f32[2,16,128,128]{3,2,1,0:T(8,128)} %get-tuple-element.161.refs_1_, bf16[256,1152]{1,0:T(8,128)(2,1)} %get-tuple-element.172.refs_2_), custom_call_target="tpu_custom_call" | custom-call | flops 1000 | bytes 45000000 | tf_op jit(solution)/shard_map/attn_backward/pallas_call | solution.py:954
  278.1 11.6 %collective-permute-done.54 = bf16[288,1152]{1,0:T(8,128)(2,1)S(1)} collective-permute-done((bf16[288,1152]{1,0:T(8,128)(2,1)}, bf16[288,1152]{1,0:T(8,128)(2,1)S(1)}, u32[]{:S(2)}, u32[]{:S(2)}) %collective-permute-start.54) | collective-permute-done | bytes 663584 | tf_op jit(solution)/shard_map/ppermute | solution.py:705
  289.9 13.2 %collective-permute-done.53 = bf16[288,1152]{1,0:T(8,128)(2,1)S(1)} collective-permute-done((bf16[288,1152]{1,0:T(8,128)(2,1)S(1)}, bf16[288,1152]{1,0:T(8,128)(2,1)S(1)}, u32[]{:S(2)}, u32[]{:S(2)}) %collective-permute-start.53) | collective-permute-done | bytes 663584 | tf_op jit(solution)/shard_map/ppermute | solution.py:705
  304.8 14.5 %qkv_backward.1 = (bf16[256,1152]{1,0:T(8,128)(2,1)}, f32[2,2,1152]{2,1,0:T(2,128)}) custom-call(bf16[256,1152]{1,0:T(8,128)(2,1)} %bitcast.110, f32[2,6,1152]{2,1,0:T(8,128)} %copy-done.55, f32[256,1152]{1,0:T(8,128)} %get-tuple-element.159.refs_2_, bf16[8,256,512]{2,1,0:T(8,128)(2,1)} %attn_backward.1.refs_3_.refs_2_, ...), custom_call_target="tpu_custom_call" | custom-call | flops 1000 | bytes 42000000 | tf_op jit(solution)/shard_map/qkv_backward/pallas_call | solution.py:964
  322.1 10.3 %attn_weight.1 = (bf16[2,144,1152]{2,1,0:T(8,128)(2,1)}, bf16[2,144,1152]{2,1,0:T(8,128)(2,1)}, bf16[2,144,1152]{2,1,0:T(8,128)(2,1)}, bf16[2,144,1152]{2,1,0:T(...) custom-call(bf16[256,1152]{1,0:T(8,128)(2,1)} %get-tuple-element.178, ...), custom_call_target="tpu_custom_call" | custom-call | flops 1000 | bytes 30000000 | tf_op jit(solution)/shard_map/attn_weight/pallas_call | solution.py:976
  357.1 10.9 %collective-permute-done.64 = bf16[2,144,1152]{2,1,0:T(8,128)(2,1)} collective-permute-done((bf16[2,144,1152]{2,1,0:T(8,128)(2,1)}, bf16[2,144,1152]{2,1,0:T(8,128)(2,1)}, u32[]{:S(2)}, u32[]{:S(2)}) %collective-permute-start.64) | collective-permute-done | bytes 663584 | tf_op jit(solution)/shard_map/ppermute | solution.py:705
  371.3 5.6 %all-to-all-done.3 = f32[32,16,128]{2,1,0:T(8,128)S(1)} async-done(((f32[32,16,128]{2,1,0:T(8,128)}), f32[32,16,128]{2,1,0:T(8,128)S(1)}, u32[]{:S(2)}, u32[]{:S(2)}) %all-to-all-start.3) | async-done | bytes 262176 | tf_op jit(solution)/shard_map/all_to_all | solution.py:712
  401.7 5.3 %collective-permute-done.67 = bf16[144,1152]{1,0:T(8,128)(2,1)S(1)} collective-permute-done((bf16[144,1152]{1,0:T(8,128)(2,1)S(1)}, bf16[144,1152]{1,0:T(8,128)(2,1)S(1)}, u32[]{:S(2)}, u32[]{:S(2)}) %collective-permute-start.67) | collective-permute-done | bytes 331808 | tf_op jit(solution)/shard_map/ppermute | solution.py:705
  419.0 5.3 %collective-permute-done.68 = bf16[144,1152]{1,0:T(8,128)(2,1)} collective-permute-done((bf16[144,1152]{1,0:T(8,128)(2,1)}, bf16[144,1152]{1,0:T(8,128)(2,1)}, u32[]{:S(2)}, u32[]{:S(2)}) %collective-permute-start.68) | collective-permute-done | bytes 331808 | tf_op jit(solution)/shard_map/ppermute | solution.py:705
  (377 shorter events, 159.3 us)
Async XLA Ops:
  26.2 33.7 %collective-permute-start.9 = (bf16[144,1152]{1,0:T(8,128)(2,1)S(1)}, bf16[144,1152]{1,0:T(8,128)(2,1)S(1)}, u32[]{:S(2)}, u32[]{:S(2)}) collective-permute-start(bf16[144,1152]{1,0:T(8,128)(2,1)S(1)} %copy-done.14), channel_id=1, source_target_pairs={{0,16},{1,17},{2,18},{3,19},{4,20},{5,21},{6,22},{7,23},{8,24},{9,... | collective-permute-start | bytes 995336 | tf_op jit(solution)/shard_map/ppermute | solution.py:705
  37.8 25.3 %all-to-all-start.1 = ((f32[32,16,128]{2,1,0:T(8,128)}), f32[32,16,128]{2,1,0:T(8,128)}, u32[]{:S(2)}, u32[]{:S(2)}) async-start(f32[32,16,128]{2,1,0:T(8,128)} %bitcast.33), calls=%async_computation.1 | async-start | bytes 524288 | tf_op jit(solution)/shard_map/all_to_all | solution.py:712
  41.1 23.1 %collective-permute-start.3 = (bf16[144,1152]{1,0:T(8,128)(2,1)S(1)}, bf16[144,1152]{1,0:T(8,128)(2,1)}, u32[]{:S(2)}, u32[]{:S(2)}) collective-permute-start(bf16[144,1152]{1,0:T(8,128)(2,1)S(1)} %collective-permute-done.refs_11_.refs_14_.refs_12_), channel_id=1, source_target_pairs={{0,4},{1,5},{2,6},{3,7},{4,0},{5,1},{6,2},{7,3},{8,12},{9,13},{10,... | collective-permute-start | bytes 995336 | tf_op jit(solution)/shard_map/ppermute | solution.py:705
  42.7 21.5 %collective-permute-start.4 = (bf16[144,1152]{1,0:T(8,128)(2,1)S(1)}, bf16[144,1152]{1,0:T(8,128)(2,1)}, u32[]{:S(2)}, u32[]{:S(2)}) collective-permute-start(bf16[144,1152]{1,0:T(8,128)(2,1)S(1)} %collective-permute-done.refs_11_.refs_14_.refs_12_), channel_id=1, source_target_pairs={{0,2},{1,3},{2,0},{3,1},{4,6},{5,7},{6,4},{7,5},{8,10},{9,11},{10,... | collective-permute-start | bytes 995336 | tf_op jit(solution)/shard_map/ppermute | solution.py:705
  101.4 20.6 %collective-permute-start.31 = (bf16[288,1152]{1,0:T(8,128)(2,1)S(1)}, bf16[288,1152]{1,0:T(8,128)(2,1)S(1)}, u32[]{:S(2)}, u32[]{:S(2)}) collective-permute-start(bf16[288,1152]{1,0:T(8,128)(2,1)S(1)} %collective-permute-done.20), channel_id=1, source_target_pairs={{8,0},{9,1},{10,2},{11,3},{12,4},{13,5},{14,6},{15,7},{16,24},{17,... | collective-permute-start | bytes 1990664 | tf_op jit(solution)/shard_map/ppermute | solution.py:807
  126.3 49.2 %collective-permute-start.38 = (bf16[256,1152]{1,0:T(8,128)(2,1)S(1)}, bf16[256,1152]{1,0:T(8,128)(2,1)S(1)}, u32[]{:S(2)}, u32[]{:S(2)}) collective-permute-start(bf16[256,1152]{1,0:T(8,128)(2,1)S(1)} %fusion.refs_2_.refs_4_), channel_id=1, source_target_pairs={{0,1},{1,0},{2,3},{3,2},{4,5},{5,4},{6,7},{7,6},{8,9},{9,8},{10,11... | collective-permute-start | bytes 1769480 | tf_op jit(solution)/shard_map/ppermute | solution.py:705
  141.3 34.9 %collective-permute-start.39 = (bf16[288,1152]{1,0:T(8,128)(2,1)S(1)}, bf16[288,1152]{1,0:T(8,128)(2,1)S(1)}, u32[]{:S(2)}, u32[]{:S(2)}) collective-permute-start(bf16[288,1152]{1,0:T(8,128)(2,1)S(1)} %add.84.refs_8_), channel_id=1, source_target_pairs={{0,4},{1,5},{2,6},{3,7},{4,0},{5,1},{6,2},{7,3},{8,12},{9,13},{10,... | collective-permute-start | bytes 1990664 | tf_op jit(solution)/shard_map/ppermute | solution.py:705
  144.2 33.4 %collective-permute-start.41 = (bf16[288,1152]{1,0:T(8,128)(2,1)S(1)}, bf16[288,1152]{1,0:T(8,128)(2,1)S(1)}, u32[]{:S(2)}, u32[]{:S(2)}) collective-permute-start(bf16[288,1152]{1,0:T(8,128)(2,1)S(1)} %add.85.refs_10_), channel_id=1, source_target_pairs={{0,4},{1,5},{2,6},{3,7},{4,0},{5,1},{6,2},{7,3},{8,12},{9,13},{10,... | collective-permute-start | bytes 1990664 | tf_op jit(solution)/shard_map/ppermute | solution.py:705
  144.9 31.1 %collective-permute-start.45 = (bf16[256,1152]{1,0:T(8,128)(2,1)S(1)}, bf16[256,1152]{1,0:T(8,128)(2,1)S(1)}, u32[]{:S(2)}, u32[]{:S(2)}) collective-permute-start(bf16[256,1152]{1,0:T(8,128)(2,1)S(1)} %fusion.refs_2_.refs_4_), channel_id=1, source_target_pairs={{0,2},{1,3},{2,0},{3,1},{4,6},{5,7},{6,4},{7,5},{8,10},{9,11},{10,... | collective-permute-start | bytes 1769480 | tf_op jit(solution)/shard_map/ppermute | solution.py:705
  228.7 27.4 %collective-permute-start.52 = (bf16[288,1152]{1,0:T(8,128)(2,1)}, bf16[288,1152]{1,0:T(8,128)(2,1)S(1)}, u32[]{:S(2)}, u32[]{:S(2)}) collective-permute-start(bf16[288,1152]{1,0:T(8,128)(2,1)} %get-tuple-element.171), channel_id=1, source_target_pairs={{0,4},{1,5},{2,6},{3,7},{4,0},{5,1},{6,2},{7,3},{8,12},{9,13},{10,... | collective-permute-start | bytes 1990664 | tf_op jit(solution)/shard_map/ppermute | solution.py:705
  271.3 48.6 %collective-permute-start.58 = (bf16[8,256,512]{2,1,0:T(8,128)(2,1)}, bf16[8,256,512]{2,1,0:T(8,128)(2,1)S(1)}, u32[]{:S(2)}, u32[]{:S(2)}) collective-permute-start(bf16[8,256,512]{2,1,0:T(8,128)(2,1)} %attn_backward.1.refs_3_.refs_2_), channel_id=1, source_target_pairs={{0,1},{1,0},{2,3},{3,2},{4,5},{5,4},{6,7},{7,6},{8,9},{9,8},{10,11... | collective-permute-start | bytes 6291464 | tf_op jit(solution)/shard_map/ppermute | solution.py:705
  272.3 30.8 %collective-permute-start.53 = (bf16[288,1152]{1,0:T(8,128)(2,1)S(1)}, bf16[288,1152]{1,0:T(8,128)(2,1)S(1)}, u32[]{:S(2)}, u32[]{:S(2)}) collective-permute-start(bf16[288,1152]{1,0:T(8,128)(2,1)S(1)} %copy-done.78), channel_id=1, source_target_pairs={{0,4},{1,5},{2,6},{3,7},{4,0},{5,1},{6,2},{7,3},{8,12},{9,13},{10,... | collective-permute-start | bytes 1990664 | tf_op jit(solution)/shard_map/ppermute | solution.py:705
  276.7 26.4 %collective-permute-start.55 = (bf16[288,1152]{1,0:T(8,128)(2,1)S(1)}, bf16[288,1152]{1,0:T(8,128)(2,1)S(1)}, u32[]{:S(2)}, u32[]{:S(2)}) collective-permute-start(bf16[288,1152]{1,0:T(8,128)(2,1)S(1)} %add_convert_fusion.3), channel_id=1, source_target_pairs={{0,24},{1,25},{2,26},{3,27},{4,28},{5,29},{6,30},{7,31},{8,16},{9,... | collective-permute-start | bytes 1990664 | tf_op jit(solution)/shard_map/ppermute | solution.py:705
  278.0 41.3 %collective-permute-start.57 = (bf16[256,1152]{1,0:T(8,128)(2,1)S(1)}, bf16[256,1152]{1,0:T(8,128)(2,1)S(1)}, u32[]{:S(2)}, u32[]{:S(2)}) collective-permute-start(bf16[256,1152]{1,0:T(8,128)(2,1)S(1)} %copy-done.70), channel_id=1, source_target_pairs={{0,1},{1,0},{2,3},{3,2},{4,5},{5,4},{6,7},{7,6},{8,9},{9,8},{10,11... | collective-permute-start | bytes 1769480 | tf_op jit(solution)/shard_map/ppermute | solution.py:705
  289.7 30.1 %collective-permute-start.59 = (bf16[256,1152]{1,0:T(8,128)(2,1)}, bf16[256,1152]{1,0:T(8,128)(2,1)S(1)}, u32[]{:S(2)}, u32[]{:S(2)}) collective-permute-start(bf16[256,1152]{1,0:T(8,128)(2,1)} %get-tuple-element.183.refs_3_), channel_id=1, source_target_pairs={{0,1},{1,0},{2,3},{3,2},{4,5},{5,4},{6,7},{7,6},{8,9},{9,8},{10,11... | collective-permute-start | bytes 1769480 | tf_op jit(solution)/shard_map/ppermute | solution.py:705
  303.1 33.4 %collective-permute-start.42 = (bf16[256,1152]{1,0:T(8,128)(2,1)}, bf16[256,1152]{1,0:T(8,128)(2,1)S(1)}, u32[]{:S(2)}, u32[]{:S(2)}) collective-permute-start(bf16[256,1152]{1,0:T(8,128)(2,1)} %get-tuple-element.148), channel_id=1, source_target_pairs={{0,1},{1,0},{2,3},{3,2},{4,5},{5,4},{6,7},{7,6},{8,9},{9,8},{10,11... | collective-permute-start | bytes 1769480 | tf_op jit(solution)/shard_map/ppermute | solution.py:705
  303.1 37.8 %collective-permute-start.50 = (bf16[256,1152]{1,0:T(8,128)(2,1)S(1)}, bf16[256,1152]{1,0:T(8,128)(2,1)S(1)}, u32[]{:S(2)}, u32[]{:S(2)}) collective-permute-start(bf16[256,1152]{1,0:T(8,128)(2,1)S(1)} %add_convert_fusion.5), channel_id=1, source_target_pairs={{0,2},{1,3},{2,0},{3,1},{4,6},{5,7},{6,4},{7,5},{8,10},{9,11},{10,... | collective-permute-start | bytes 1769480 | tf_op jit(solution)/shard_map/ppermute | solution.py:705
  319.3 57.8 %collective-permute-start.71 = (bf16[288,1152]{1,0:T(8,128)(2,1)}, bf16[288,1152]{1,0:T(8,128)(2,1)}, u32[]{:S(2)}, u32[]{:S(2)}) collective-permute-start(bf16[288,1152]{1,0:T(8,128)(2,1)} %get-tuple-element.199), channel_id=1, source_target_pairs={{0,4},{1,5},{2,6},{3,7},{4,0},{5,1},{6,2},{7,3},{8,12},{9,13},{10,... | collective-permute-start | bytes 1990664 | tf_op jit(solution)/shard_map/ppermute | solution.py:705
  336.5 40.6 %collective-permute-start.72 = (bf16[288,1152]{1,0:T(8,128)(2,1)}, bf16[288,1152]{1,0:T(8,128)(2,1)}, u32[]{:S(2)}, u32[]{:S(2)}) collective-permute-start(bf16[288,1152]{1,0:T(8,128)(2,1)} %add_convert_fusion.2), channel_id=1, source_target_pairs={{0,8},{1,9},{2,10},{3,11},{4,12},{5,13},{6,14},{7,15},{8,0},{9,1},... | collective-permute-start | bytes 1990664 | tf_op jit(solution)/shard_map/ppermute | solution.py:705
  340.9 36.2 %collective-permute-start.73 = (bf16[288,1152]{1,0:T(8,128)(2,1)}, bf16[288,1152]{1,0:T(8,128)(2,1)}, u32[]{:S(2)}, u32[]{:S(2)}) collective-permute-start(bf16[288,1152]{1,0:T(8,128)(2,1)} %add_convert_fusion.1), channel_id=1, source_target_pairs={{0,16},{1,17},{2,18},{3,19},{4,20},{5,21},{6,22},{7,23},{8,24},{9,... | collective-permute-start | bytes 1990664 | tf_op jit(solution)/shard_map/ppermute | solution.py:705
  343.0 33.9 %all-to-all-start.3 = ((f32[32,16,128]{2,1,0:T(8,128)}), f32[32,16,128]{2,1,0:T(8,128)S(1)}, u32[]{:S(2)}, u32[]{:S(2)}) async-start(f32[32,16,128]{2,1,0:T(8,128)} %bitcast.37), calls=%async_computation.3 | async-start | bytes 524288 | tf_op jit(solution)/shard_map/all_to_all | solution.py:712
  383.5 28.5 %all-to-all-start.4 = ((bf16[4,2,144,288]{3,2,1,0:T(8,128)(2,1)}), bf16[4,2,144,288]{3,2,1,0:T(8,128)(2,1)S(1)}, u32[]{:S(2)}, u32[]{:S(2)}) async-start(bf16[4,2,144,288]{3,2,1,0:T(8,128)(2,1)} %bitcast.99), calls=%async_computation.4 | async-start | bytes 1769472 | tf_op jit(solution)/shard_map/all_to_all | solution.py:1017
  392.0 27.0 %collective-permute-start.69 = (bf16[144,1152]{1,0:T(8,128)(2,1)S(1)}, bf16[144,1152]{1,0:T(8,128)(2,1)}, u32[]{:S(2)}, u32[]{:S(2)}) collective-permute-start(bf16[144,1152]{1,0:T(8,128)(2,1)S(1)} %fusion.6), channel_id=1, source_target_pairs={{0,16},{1,17},{2,18},{3,19},{4,20},{5,21},{6,22},{7,23},{8,24},{9,... | collective-permute-start | bytes 995336 | tf_op jit(solution)/shard_map/ppermute | solution.py:705
  396.4 22.6 %collective-permute-start.66 = (bf16[144,1152]{1,0:T(8,128)(2,1)S(1)}, bf16[144,1152]{1,0:T(8,128)(2,1)}, u32[]{:S(2)}, u32[]{:S(2)}) collective-permute-start(bf16[144,1152]{1,0:T(8,128)(2,1)S(1)} %fusion.16), channel_id=1, source_target_pairs={{0,4},{1,5},{2,6},{3,7},{4,0},{5,1},{6,2},{7,3},{8,12},{9,13},{10,... | collective-permute-start | bytes 995336 | tf_op jit(solution)/shard_map/ppermute | solution.py:705
  (134 other events, 1904.4 us)

commit v3 on v0

--- a/solution.py
+++ b/solution.py
@@ -1,11 +1,18 @@
+import functools
 import math
 
 import jax
 import jax.numpy as jnp
 from jax import lax
+from jax.experimental import pallas as pl
+from jax.experimental.pallas import tpu as pltpu
 from jax.sharding import PartitionSpec as P
 
 HEADS = 16
+AXES = ("dp", "fsdp")
+EPS = 1e-06
+F32, LOW = jnp.float32, jnp.bfloat16
+SCALE = 100
 
 
 def norm_mod(values, shift_add, scale_mul):
@@ -88,7 +95,7 @@
     )
 
 
-def body(
+def general_body(
     inputs,
     out_cotangent,
     lengths,
@@ -236,32 +243,905 @@
     return (result, input_grad, ada_grad, qkv_grad, proj_grad, up_grad, down_grad)
 
 
+def dot_nn(left, right):
+    return lax.dot_general(left, right, (((1,), (0,)), ((), ())), preferred_element_type=F32)
+
+
+def dot_nt(left, right):
+    return lax.dot_general(left, right, (((1,), (1,)), ((), ())), preferred_element_type=F32)
+
+
+def dot_tn(left, right):
+    return lax.dot_general(left, right, (((0,), (0,)), ((), ())), preferred_element_type=F32)
+
+
+def stats(values):
+    mean = jnp.mean(values, -1, keepdims=True)
+    center = values - mean
+    spread = jnp.mean(center * center, -1, keepdims=True)
+    inverse = lax.rsqrt(spread + EPS)
+    return center * inverse, inverse
+
+
+def here(names):
+    return lax.axis_index(names[0]), lax.axis_index(names[1])
+
+
+def start_blocks(places, block_refs, weight_ref, sems):
+    column, row = here(AXES)
+    row_parts = weight_ref.shape[1]
+    copies = {}
+    for ref, held in zip(block_refs, places):
+        for index, relative in enumerate(held):
+            copy = pltpu.make_async_copy(
+                ref.at[index],
+                weight_ref.at[column ^ (relative // row_parts), row ^ (relative % row_parts)],
+                sems.at[relative],
+            )
+            copy.start()
+            copies[relative] = copy
+    return [copies[relative] for relative in sorted(copies)]
+
+
+class Packing:
+    def __init__(self, half, qkv_cols, proj_cols):
+        self.half, self.qkv_cols, self.proj_cols = half, qkv_cols, proj_cols
+        self.qkv_main, self.proj_main = qkv_cols // 128 * 128, proj_cols // 128 * 128
+        self.qkv_rest, self.proj_rest = qkv_cols - self.qkv_main, proj_cols - self.proj_main
+        self.rest = self.qkv_rest + self.proj_rest
+        self.proj_start = 2 * self.qkv_main
+        self.rest_start = self.proj_start + 2 * self.proj_main
+        self.width = self.rest_start + 2 * self.rest
+
+    def pack(self, qkv, proj):
+        halves = [slice(i * self.half, (i + 1) * self.half) for i in range(2)]
+        return jnp.concatenate(
+            [qkv[rows, : self.qkv_main] for rows in halves]
+            + [proj[rows, : self.proj_main] for rows in halves]
+            + [
+                piece
+                for rows in halves
+                for piece in (qkv[rows, self.qkv_main :], proj[rows, self.proj_main :])
+            ],
+            axis=1,
+        )
+
+    def qkv_of(self, block, side):
+        rest = self.rest_start + side * self.rest
+        return jnp.concatenate(
+            [
+                block[:, side * self.qkv_main : (side + 1) * self.qkv_main],
+                block[:, rest : rest + self.qkv_rest],
+            ],
+            axis=1,
+        )
+
+    def proj_of(self, block, side):
+        main = self.proj_start + side * self.proj_main
+        rest = self.rest_start + side * self.rest + self.qkv_rest
+        return jnp.concatenate(
+            [block[:, main : main + self.proj_main], block[:, rest : rest + self.proj_rest]],
+            axis=1,
+        )
+
+    def unpack(self, block):
+        return tuple(
+            jnp.concatenate([part(block, side) for side in range(2)], axis=0)
+            for part in (self.qkv_of, self.proj_of)
+        )
+
+
+def pair_mask(span, frames, live):
+    query = lax.broadcasted_iota(jnp.int32, (span, span), 0)
+    key = lax.broadcasted_iota(jnp.int32, (span, span), 1)
+    return ((query // frames) == (key // frames)) & ((key % frames) < live)
+
+
+def head_groups(count, size):
+    return [range(start, start + size) for start in range(0, count, size)]
+
+
+def head_slices(ref, which, head, rows, size):
+    per = ref.shape[2] // size
+    slot = which * HEADS + head
+    return ref[slot // per, rows, (slot % per) * size : (slot % per + 1) * size]
+
+
+def columns_of(ref, rows, index, size):
+    return ref[rows, index * size : (index + 1) * size]
+
+
+def join_proj(packing, weight, proj):
+    for place in range(weight.shape[0]):
+        start = place * packing.proj_cols
+        for part in range(weight.shape[1]):
+            for side in range(2):
+                row = (2 * part + side) * packing.half
+                proj[row : row + packing.half, start : start + packing.proj_cols] = packing.proj_of(
+                    weight.at[place, part], side
+                )
+
+
+def attn_forward_kernel(sizes, packing, places, *refs):
+    clips, span, frames, width, chunk = sizes
+    blocks = len(places)
+    lengths, tokens, mod = refs[:3]
+    block_refs = refs[3 : 3 + blocks]
+    hidden, mixed, probs_out, attended, branch, middle, hidden_two, proj = refs[3 + blocks : 11 + blocks]
+    weight, branch_full, sems = refs[11 + blocks :]
+    copies = start_blocks(places, block_refs, weight, sems)
+    column_parts, row_parts = weight.shape[0], weight.shape[1]
+    size = width // HEADS
+    scale = 1.0 / math.sqrt(size)
+
+    def first_norm(step, carry):
+        rows = pl.ds(pl.multiple_of(step * chunk, chunk), chunk)
+        clip_mod = mod[step * chunk // span]
+        unit, _ = stats(tokens[rows, :].astype(F32))
+        hidden[rows, :] = (unit * (1.0 + clip_mod[1:2]) + clip_mod[0:1]).astype(LOW)
+        return carry
+
+    lax.fori_loop(0, clips * span // chunk, first_norm, 0)
+    column, row = here(AXES)
+    for relative in range(column_parts):
+        for other in range(row_parts):
+            copies[relative * row_parts + other].wait()
+        place = column ^ relative
+        columns = jnp.concatenate(
+            [
+                packing.qkv_of(weight.at[place, part], side)
+                for part in range(row_parts)
+                for side in range(2)
+            ],
+            axis=0,
+        )
+        mixed[place] = dot_nn(hidden[...], columns).astype(LOW)
+
+    for clip in range(clips):
+        rows = slice(clip * span, (clip + 1) * span)
+        live_mask = pair_mask(span, frames, lengths[clip])
+        for group in head_groups(HEADS, 4):
+            scores = [
+                dot_nt(
+                    head_slices(mixed, 0, head, rows, size), head_slices(mixed, 1, head, rows, size)
+                )
+                for head in group
+            ]
+            scores = [jnp.where(live_mask, score * scale, -1e30) for score in scores]
+            exps = [jnp.exp(score - jnp.max(score, -1, keepdims=True)) for score in scores]
+            probs = [(e * (1.0 / jnp.sum(e, -1, keepdims=True))).astype(LOW) for e in exps]
+            values = [
+                dot_nn(prob, head_slices(mixed, 2, head, rows, size))
+                for head, prob in zip(group, probs)
+            ]
+            for head, prob, value in zip(group, probs, values):
+                probs_out[clip, head] = prob
+                attended[rows, head * size : (head + 1) * size] = value.astype(LOW)
+
+    join_proj(packing, weight, proj)
+    branch_full[...] = dot_nn(attended[...], proj[...])
+
+    def second_norm(step, carry):
+        rows = pl.ds(pl.multiple_of(step * chunk, chunk), chunk)
+        clip_mod = mod[step * chunk // span]
+        value = branch_full[rows, :]
+        branch[rows, :] = value.astype(LOW)
+        value = tokens[rows, :].astype(F32) + clip_mod[2:3] * value
+        middle[rows, :] = value
+        unit, _ = stats(value)
+        hidden_two[rows, :] = (unit * (1.0 + clip_mod[4:5]) + clip_mod[3:4]).astype(LOW)
+        return carry
+
+    lax.fori_loop(0, clips * span // chunk, second_norm, 0)
+
+
+def norm_back(grad, values, scale_row):
+    unit, inverse = stats(values)
+    d_unit = grad * (1.0 + scale_row)
+    d_value = inverse * (
+        d_unit
+        - jnp.mean(d_unit, -1, keepdims=True)
+        - unit * jnp.mean(d_unit * unit, -1, keepdims=True)
+    )
+    return unit, d_value
+
+
+def proj_backward_kernel(sizes, *refs):
+    clips, span, frames, width, chunk = sizes
+    cotangent, mod, middle, branch, grad_own, grad_core, grad_far, proj = refs[:8]
+    d_middle, d_branch, d_attended, d_mod = refs[8:]
+    zero_row = jnp.zeros((1, width), F32)
+    steps = span // chunk
+    for clip in range(clips):
+        clip_mod = mod[clip]
+
+        def second_back(step, carry, clip=clip, clip_mod=clip_mod):
+            d_shift, d_scale, d_gate = carry
+            rows = pl.ds(pl.multiple_of(clip * span + step * chunk, chunk), chunk)
+            grad = grad_own[rows, :] + grad_core[rows, :].astype(F32)
+            grad += grad_far[rows, :].astype(F32)
+            unit, d_value = norm_back(grad, middle[rows, :], clip_mod[4:5])
+            d_value = cotangent[rows, :].astype(F32) + d_value
+            d_middle[rows, :] = d_value
+            d_branch[rows, :] = (d_value * clip_mod[2:3]).astype(LOW)
+            return (
+                d_shift + jnp.sum(grad, 0, keepdims=True),
+                d_scale + jnp.sum(grad * unit, 0, keepdims=True),
+                d_gate + jnp.sum(d_value * branch[rows, :].astype(F32), 0, keepdims=True),
+            )
+
+        sums = lax.fori_loop(0, steps, second_back, (zero_row, zero_row, zero_row))
+        d_mod[clip, 0:1, :] = sums[2]
+        d_mod[clip, 1:2, :] = sums[0]
+        d_mod[clip, 2:3, :] = sums[1]
+
+    d_attended[...] = dot_nt(d_branch[...], proj[...]).astype(LOW)
+
+
+def attn_backward_kernel(sizes, *refs):
+    clips, span, frames, width, qkv_cols = sizes
+    mixed, probs_ref, d_attended, d_mixed = refs
+    size = width // HEADS
+    scale = 1.0 / math.sqrt(size)
+    cols = qkv_cols // size
+    for clip in range(clips):
+        rows = slice(clip * span, (clip + 1) * span)
+        for group in head_groups(HEADS, 4):
+            queries, keys, values = (
+                [head_slices(mixed, which, head, rows, size) for head in group]
+                for which in range(3)
+            )
+            probs = [probs_ref[clip, head] for head in group]
+            grads = [columns_of(d_attended, rows, head, size) for head in group]
+            d_probs = [dot_nt(grad, value) for grad, value in zip(grads, values)]
+            d_values = [dot_tn(prob, grad) for prob, grad in zip(probs, grads)]
+            d_scores = []
+            for prob, d_prob in zip(probs, d_probs):
+                prob = prob.astype(F32)
+                inner = jnp.sum(prob * d_prob, -1, keepdims=True)
+                d_scores.append((prob * (d_prob - inner) * scale).astype(LOW))
+            d_queries = [dot_nn(score, key) for score, key in zip(d_scores, keys)]
+            d_keys = [dot_tn(score, query) for score, query in zip(d_scores, queries)]
+            for which, pieces in enumerate((d_queries, d_keys, d_values)):
+                for head, piece in zip(group, pieces):
+                    slot = which * HEADS + head
+                    place, start = slot // cols, (slot % cols) * size
+                    d_mixed[place, rows, start : start + size] = piece.astype(LOW)
+
+
+def qkv_backward_kernel(sizes, packing, places, *refs):
+    clips, span, frames, width, chunk = sizes
+    blocks = len(places)
+    tokens, mod, d_middle, d_mixed = refs[:4]
+    input_grad, d_mod = refs[4 + blocks : 6 + blocks]
+    weight, d_hidden, sems = refs[6 + blocks :]
+    copies = start_blocks(places, refs[4 : 4 + blocks], weight, sems)
+    column_parts, row_parts = weight.shape[0], weight.shape[1]
+    for copy in copies:
+        copy.wait()
+    for place in range(column_parts):
+        columns = jnp.concatenate(
+            [
+                packing.qkv_of(weight.at[place, part], side)
+                for part in range(row_parts)
+                for side in range(2)
+            ],
+            axis=0,
+        )
+        term = dot_nt(d_mixed[place, :, 0 : packing.qkv_cols], columns)
+        if place == 0:
+            d_hidden[...] = term
+        else:
+            d_hidden[...] += term
+    zero_row = jnp.zeros((1, width), F32)
+    for clip in range(clips):
+        clip_mod = mod[clip]
+
+        def first_back(step, carry, clip=clip, clip_mod=clip_mod):
+            d_shift, d_scale = carry
+            rows = pl.ds(pl.multiple_of(clip * span + step * chunk, chunk), chunk)
+            grad = d_hidden[rows, :]
+            unit, d_value = norm_back(grad, tokens[rows, :].astype(F32), clip_mod[1:2])
+            input_grad[rows, :] = (d_middle[rows, :] + d_value).astype(LOW)
+            return (
+                d_shift + jnp.sum(grad, 0, keepdims=True),
+                d_scale + jnp.sum(grad * unit, 0, keepdims=True),
+            )
+
+        sums = lax.fori_loop(0, span // chunk, first_back, (zero_row, zero_row))
+        d_mod[clip, 0:1, :] = sums[0]
+        d_mod[clip, 1:2, :] = sums[1]
+
+
+def attn_weight_kernel(packing, distances, *refs):
+    own, far, outs = refs[:4], refs[4:8], refs[8:-3]
+    hidden_t, attended_t, d_pieces = refs[-3:]
+    half, qkv_cols, proj_cols = packing.half, packing.qkv_cols, packing.proj_cols
+    row_count = own[0].shape[0]
+    column_parts = own[2].shape[0]
+    row_parts = own[0].shape[1] // (2 * half)
+    for start, group in ((0, own), (row_count, far)):
+        hidden_t[:, start : start + row_count] = group[0][...].T
+        attended_t[:, start : start + row_count] = group[1][...].T
+        for place in range(column_parts):
+            d_pieces[place, start : start + row_count, :] = columns_of(
+                group[3], slice(None), place, proj_cols
+            )
+    column, row = here(AXES)
+    for index, z_bits in enumerate(distances):
+        for x_bit in range(2):
+            place = column ^ (2 * z_bits + x_bit)
+            d_qkv = jnp.concatenate(
+                [own[2][place, :, 0:qkv_cols], far[2][place, :, 0:qkv_cols]], axis=0
+            )
+            d_proj = d_pieces[place]
+            for other in range(row_parts // 2):
+                rows = pl.ds(pl.multiple_of((row ^ (2 * other)) * 2 * half, 16), 2 * half)
+                qkv = dot_nn(hidden_t[rows, :], d_qkv)
+                proj = dot_nn(attended_t[rows, :], d_proj)
+                outs[2 * index + other][x_bit] = packing.pack(qkv, proj).astype(LOW)
+
+
+def feed_kernel(chunk, parts, *refs):
+    sources, stacked, outs = refs[0:4], refs[4], refs[5:13]
+    hidden, d_outs, up_weight, down_weight, up_proj, d_activ, activ, d_up, wide, narrow = refs[13:23]
+    in_sems, weight_sems, out_sems = refs[23:]
+    rows_each = sources[0].shape[0]
+    half = stacked.shape[0] // (2 * parts)
+    halves = [pl.ds(index * rows_each, rows_each) for index in range(2)]
+
+    def started(source, target, sem):
+        copy = pltpu.make_async_copy(source, target, sem)
+        copy.start()
+        return copy
+
+    waits = []
+    for which, (target, weight) in enumerate(((hidden, up_weight), (d_outs, down_weight))):
+        waits.append(
+            [
+                started(sources[2 * which + index], target.at[rows], in_sems.at[which, index])
+                for index, rows in enumerate(halves)
+            ]
+            + [
+                started(
+                    stacked.at[pl.ds((2 * part + which) * half, half)],
+                    weight.at[pl.ds(part * half, half)],
+                    weight_sems.at[part, which],
+                )
+                for part in range(parts)
+            ]
+        )
+    sent = []
+    tilt = math.sqrt(2.0 / math.pi)
+    for copy in waits[0]:
+        copy.wait()
+    up_proj[...] = dot_nt(hidden[...], up_weight[...])
+    for copy in waits[1]:
+        copy.wait()
+    d_activ[...] = dot_nn(d_outs[...], down_weight[...])
+
+    def gelu(step, carry):
+        rows = pl.ds(pl.multiple_of(step * chunk, chunk), chunk)
+        value = up_proj[rows, :]
+        square = value * value
+        bend = jnp.tanh(value * (tilt + (tilt * 0.044715) * square))
+        half_value = 0.5 * value
+        activ[rows, :] = (half_value + half_value * bend).astype(LOW)
+        slope = (0.5 + 0.5 * bend) + half_value * (1.0 - bend * bend) * (
+            tilt + (tilt * 3.0 * 0.044715) * square
+        )
+        d_up[rows, :] = (d_activ[rows, :] * slope).astype(LOW)
+        return carry
+
+    lax.fori_loop(0, 2 * rows_each // chunk, gelu, 0)
+    for index, rows in enumerate(halves):
+        sent.append(started(activ.at[rows], outs[index], out_sems.at[index]))
+        sent.append(started(d_up.at[rows], outs[2 + index], out_sems.at[2 + index]))
+    for which, total in enumerate(
+        (lambda: dot_nn(d_up[...], up_weight[...]), lambda: dot_nt(activ[...], down_weight[...]))
+    ):
+        value = total()
+        wide[which] = value[:rows_each]
+        narrow[which] = value[rows_each:].astype(LOW)
+        sent.append(started(narrow.at[which], outs[5 + 2 * which], out_sems.at[5 + 2 * which]))
+        sent.append(started(wide.at[which], outs[4 + 2 * which], out_sems.at[4 + 2 * which]))
+    for copy in sent:
+        copy.wait()
+
+
+def feed_weight_kernel(*refs):
+    stacked = refs[16]
+    hidden, d_outs, activ, d_up = (
+        jnp.concatenate([ref[...] for ref in refs[i : i + 4]], axis=0) for i in (0, 4, 8, 12)
+    )
+    parts, half = stacked.shape[0], stacked.shape[1] // 2
+    for side, (left, right) in enumerate(((d_up, hidden), (d_outs, activ))):
+        total = dot_tn(left, right).astype(LOW)
+        for part in range(parts):
+            stacked[part, side * half : (side + 1) * half, :] = total[
+                part * half : (part + 1) * half
+            ]
+
+
+def modulation_kernel(conds, ada, part_out, ordered):
+    groups, rows, _ = ordered.shape
+    for group in range(groups):
+        ordered[group] = conds[group, 0:rows, 0 : ada.shape[0]]
+        part_out[group * rows : (group + 1) * rows, :] = dot_nn(ordered[group], ada[...])
+
+
+def prepare_kernel(packing, sub, clips, *refs):
+    timesteps, labels, time_table, class_table, qkv, proj_t, up, down_t, packed, send = refs
+    packed[...] = packing.pack(qkv[...], proj_t[...].T)
+    row_parts = send.shape[0]
+
+    def look_up(indices, table):
+        count = table.shape[0]
+        row = lax.broadcasted_iota(jnp.int32, (16, count), 0)
+        column = lax.broadcasted_iota(jnp.int32, (16, count), 1)
+        picked = jnp.zeros((16, count), jnp.bool_)
+        for clip in range(clips):
+            picked = picked | ((row == clip) & (column == indices[clip]))
+        return dot_nn(picked.astype(F32).astype(LOW), table[...])
+
+    embedded = look_up(timesteps, time_table) + look_up(labels, class_table)
+    cond = (embedded * (1.0 / (1.0 + jnp.exp(-embedded)))).astype(LOW)
+    up_t = up[...].T
+    height = send.shape[2]
+    pairs = height // sub
+    for part in range(row_parts):
+        send[part, 0:sub] = up_t[part * sub : (part + 1) * sub, :]
+        send[part, 2 * sub :] = cond[:, part * height : (part + 1) * height]
+        for pair in range(pairs):
+            start = (pair * row_parts + part) * sub
+            send[part, sub : 2 * sub, pair * sub : (pair + 1) * sub] = down_t[:, start : start + sub]
+
+
+def sum_kernel(*refs):
+    total = refs[0][...].astype(F32)
+    for ref in refs[1:-1]:
+        total += ref[...].astype(F32)
+    refs[-1][...] = total.astype(refs[-1].dtype)
+
+
+def split_sum_kernel(kept, got, stay, leave):
+    total = kept[...].astype(F32) + got[...].astype(F32)
+    stay[...] = total[0]
+    leave[...] = total[1].astype(LOW)
+
+
+def feed_total_kernel(*refs):
+    total = refs[0][...].astype(F32)
+    for ref in refs[1:-1]:
+        total += ref[...].astype(F32)
+    out = refs[-1]
+    parts, sides, half, height = out.shape
+    for part in range(parts):
+        for side in range(sides):
+            out[part, side] = total[
+                side * half : (side + 1) * half, part * height : (part + 1) * height
+            ].astype(LOW)
+
+
+def feed_finish_kernel(back, up_grad, down_grad_t):
+    parts, _, sub, height = back.shape
+    pairs = height // sub
+    for part in range(parts):
+        up_grad[:, part * sub : (part + 1) * sub] = back[part, 0].astype(F32).T
+        for pair in range(pairs):
+            start = (pair * parts + part) * sub
+            down_grad_t[:, start : start + sub] = back[
+                part, 1, :, pair * sub : (pair + 1) * sub
+            ].astype(F32)
+
+
+def attn_finish_kernel(packing, *refs):
+    total = refs[0][...].astype(F32)
+    for ref in refs[1:-2]:
+        total += ref[...].astype(F32)
+    qkv_grad, proj_grad_t = refs[-2:]
+    for side in range(2):
+        rows = slice(side * packing.half, (side + 1) * packing.half)
+        qkv_grad[rows, :] = packing.qkv_of(total, side)
+        proj_grad_t[:, rows] = packing.proj_of(total, side).T
+
+
+def out_finish_kernel(sizes, *refs):
+    clips, span, chunk = sizes
+    first, second, third, middle, cotangent, mod, result, d_gate = refs
+    zero_row = jnp.zeros((1, middle.shape[1]), F32)
+    for clip in range(clips):
+
+        def step_rows(step, carry, clip=clip):
+            rows = pl.ds(pl.multiple_of(clip * span + step * chunk, chunk), chunk)
+            value = first[rows, :] + second[rows, :].astype(F32) + third[rows, :].astype(F32)
+            result[rows, :] = (middle[rows, :] + mod[clip, 5:6, :] * value).astype(LOW)
+            return carry + jnp.sum(cotangent[rows, :].astype(F32) * value, 0, keepdims=True)
+
+        d_gate[clip] = lax.fori_loop(0, span // chunk, step_rows, zero_row)
+
+
+VMEM_SPEC = pl.BlockSpec(memory_space=pltpu.VMEM)
+SMEM_SPEC = pl.BlockSpec(memory_space=pltpu.SMEM)
+ANY_SPEC = pl.BlockSpec(memory_space=pl.ANY)
+PARAMS = pltpu.CompilerParams(vmem_limit_bytes=56 * 1024 * 1024)
+
+
+def shape_of(dims, kind=LOW):
+    return jax.ShapeDtypeStruct(dims, kind)
+
+
+def cost(micros):
+    return pl.CostEstimate(flops=1000, bytes_accessed=int(micros * SCALE), transcendentals=0)
+
+
+def after(value, *others):
+    return lax.optimization_barrier((value,) + others)[0]
+
+
+class Sequence:
+    def __init__(self):
+        self.token = None
+
+    def call(self, kernel, shapes, arrays, name, specs=None, scratch=(), tied=0, out_spec=None):
+        arrays = list(arrays)
+        if self.token is not None:
+            arrays[tied] = after(arrays[tied], self.token)
+        results = pl.pallas_call(
+            kernel,
+            out_shape=shapes,
+            in_specs=specs or [VMEM_SPEC] * len(arrays),
+            out_specs=jax.tree.map(lambda _: out_spec or VMEM_SPEC, shapes),
+            scratch_shapes=scratch,
+            compiler_params=PARAMS,
+            cost_estimate=cost(1),
+            name=name,
+        )(*arrays)
+        self.token = min(jax.tree.leaves(results), key=lambda result: result.size)
+        return results
+
+    def sum_low(self, *arrays):
+        return self.call(sum_kernel, shape_of(arrays[0].shape), arrays, "sum_low")
+
+
+def swap(value, mask, count):
+    return lax.ppermute(value, AXES, [(i, i ^ mask) for i in range(count)])
+
+
+def padded_exchange(rows, count):
+    length = rows.shape[1]
+    tiles = -(-length // 1024) * 8
+    rows = jnp.pad(rows, ((0, 0), (0, tiles * 128 - length))).reshape(count, tiles, 128)
+    got = lax.all_to_all(rows, AXES, 0, 0, tiled=True)
+    return got.reshape(count, tiles * 128)[:, :length]
+
+
+def fast_body(
+    column_parts,
+    row_parts,
+    inputs,
+    out_cotangent,
+    lengths,
+    timesteps,
+    labels,
+    time_table,
+    class_table,
+    ada_weight,
+    qkv_weight,
+    proj_weight,
+    up_weight,
+    down_weight,
+):
+    count = column_parts * row_parts
+    clips, positions, frames, width = inputs.shape
+    span = positions * frames
+    row_count = clips * span
+    qkv_cols, proj_cols = qkv_weight.shape[1], proj_weight.shape[1]
+    height = qkv_weight.shape[0]
+    part_width = width // row_parts
+    hidden_part = up_weight.shape[1] * column_parts // row_parts
+    sub = up_weight.shape[1] // row_parts
+    x_mask = row_parts
+    z_masks = tuple(row_parts * 2 * i for i in range(1, column_parts // 2))
+    packing = Packing(height // 2, qkv_cols, proj_cols)
+
+    line = Sequence()
+    packed, both_send = line.call(
+        functools.partial(prepare_kernel, packing, sub, clips),
+        (
+            shape_of((height // 2, packing.width)),
+            shape_of((row_parts, 2 * sub + 16, height)),
+        ),
+        (timesteps, labels, time_table, class_table)
+        + (qkv_weight, proj_weight.T, up_weight, down_weight.T),
+        "prepare",
+        [SMEM_SPEC] * 2 + [VMEM_SPEC] * 6,
+    )
+
+    y_mask, c_mask = 2, 1
+    ada_cols = ada_weight.shape[1]
+
+    def gate(*values):
+        return lax.optimization_barrier(values)
+
+    own = packed[None]
+    far = [swap(own, mask, count) for mask in z_masks]
+    own_x, own_y = swap(own, x_mask, count), swap(own, y_mask, count)
+    both_got = lax.all_to_all(both_send, "fsdp", 0, 0, tiled=True)
+    *far, own_x, own_y, both_got = gate(*far, own_x, own_y, both_got)
+    own_feed = both_got[:, : 2 * sub].reshape(row_parts, 2, sub, height)
+    own_feed = own_feed.transpose(1, 2, 0, 3).reshape(2 * sub, width)
+    conds = both_got[:, 2 * sub : 2 * sub + clips].reshape(row_parts * clips, height)
+    feed = lax.all_gather(own_feed, "dp", axis=0, tiled=True)
+
+    far = jnp.concatenate(far)
+    pads = (-row_parts * clips % 16, -height % 128)
+    conds = jnp.pad(conds, ((0, pads[0]), (0, pads[1])))
+    conds = jnp.broadcast_to(conds[None], (column_parts,) + conds.shape)
+    conds = lax.all_to_all(conds, "dp", 0, 0, tiled=True)
+    far_x, far_y = swap(far, x_mask, count), swap(far, y_mask, count)
+    cores = [swap(array, c_mask, count) for array in (own, own_x, own_y, far)]
+    far_x, far_y, conds, *cores = gate(far_x, far_y, conds, *cores)
+
+    mod_part, conds = line.call(
+        modulation_kernel,
+        (
+            shape_of((count * clips, ada_cols), F32),
+            shape_of((column_parts, row_parts * clips, part_width)),
+        ),
+        (conds, ada_weight),
+        "modulation",
+    )
+    cond_all = conds.reshape(count * clips, part_width)
+    mod_got = padded_exchange(mod_part.reshape(count, clips * ada_cols), count)
+    own_xy, far_xy = swap(own_x, y_mask, count), swap(far_x, y_mask, count)
+    cores += [swap(array, c_mask, count) for array in (far_x, far_y)]
+    own_xy, far_xy, mod_got, *cores = gate(own_xy, far_xy, mod_got, *cores)
+    mod_own = jnp.sum(mod_got.reshape(column_parts, row_parts, clips, ada_cols), axis=1)
+    mod = mod_own.transpose(1, 0, 2).reshape(clips, 6, width)
+    cores += [swap(array, c_mask, count) for array in (own_xy, far_xy)]
+
+    blocks = [own, own_x, own_y, far, far_x, far_y, own_xy, far_xy]
+    places = [[0], [x_mask], [y_mask], list(z_masks)]
+    places += [[z ^ side for z in z_masks] for side in (x_mask, y_mask)]
+    places += [[x_mask ^ y_mask]]
+    places += [[z ^ x_mask ^ y_mask for z in z_masks]]
+    blocks += cores
+    places += [[place ^ c_mask for place in held] for held in places]
+
+    tokens = inputs.reshape(row_count, width)
+    cotangent = out_cotangent.reshape(row_count, width)
+    gate_two = jnp.repeat(mod[:, 5], span, axis=0)
+    d_out = (cotangent.astype(F32) * gate_two).astype(LOW)
+    d_outs = {0: d_out, 1: swap(d_out, 1, count), 2: swap(d_out, 2, count)}
+    d_outs[3] = swap(d_outs[2], 1, count)
+    sizes = (clips, span, frames, width, 32)
+    full = (row_count, width)
+    weight_scratch = pltpu.VMEM((column_parts, row_parts, height // 2, packing.width), LOW)
+    weight_sems = pltpu.SemaphoreType.DMA((count,))
+    hidden, mixed, probs, attended, branch, middle, hidden_two, proj_full = line.call(
+        functools.partial(attn_forward_kernel, sizes, packing, places),
+        (
+            shape_of(full),
+            shape_of((column_parts, row_count, qkv_cols)),
+            shape_of((clips, HEADS, span, span)),
+            shape_of(full),
+            shape_of(full),
+            shape_of(full, F32),
+            shape_of(full),
+            shape_of((width, width)),
+        ),
+        (lengths, tokens, mod, *blocks),
+        "attn_forward",
+        [SMEM_SPEC, VMEM_SPEC, VMEM_SPEC] + [ANY_SPEC] * len(blocks),
+        (
+            weight_scratch,
+            pltpu.VMEM(full, F32),
+            weight_sems,
+        ),
+        tied=2,
+    )
+
+    tokens_two = {0: hidden_two, 1: swap(hidden_two, 1, count), 2: swap(hidden_two, 2, count)}
+    pair = (2 * row_count, width)
+    pair_hidden = (2 * row_count, hidden_part)
+    feed_scratch = (
+        pltpu.VMEM(pair, LOW),
+        pltpu.VMEM(pair, LOW),
+        pltpu.VMEM((hidden_part, width), LOW),
+        pltpu.VMEM((width, hidden_part), LOW),
+        pltpu.VMEM(pair_hidden, F32),
+        pltpu.VMEM(pair_hidden, F32),
+        pltpu.VMEM(pair_hidden, LOW),
+        pltpu.VMEM(pair_hidden, LOW),
+        pltpu.VMEM((2,) + full, F32),
+        pltpu.VMEM((2,) + full, LOW),
+        pltpu.SemaphoreType.DMA((2, 2)),
+        pltpu.SemaphoreType.DMA((column_parts, 2)),
+        pltpu.SemaphoreType.DMA((8,)),
+    )
+
+    def feed_call(index, name):
+        return line.call(
+            functools.partial(feed_kernel, 32, column_parts),
+            [shape_of((row_count, hidden_part))] * 4 + [shape_of(full, F32), shape_of(full)] * 2,
+            (
+                tokens_two[index],
+                tokens_two[index + 1],
+                d_outs[index],
+                d_outs[index + 1],
+                feed,
+            ),
+            name,
+            [ANY_SPEC] * 5,
+            feed_scratch,
+            out_spec=ANY_SPEC,
+        )
+
+    near = feed_call(0, "feed_near")
+    tokens_two[2] = after(tokens_two[2], line.token)
+    tokens_two[3] = swap(tokens_two[2], 1, count)
+    distant = feed_call(2, "feed_distant")
+
+    grad_send = line.sum_low(distant[4], swap(distant[5], 1, count))
+    grad_far = swap(grad_send, 2, count)
+    grad_parts = (near[4], swap(near[5], 1, count), grad_far)
+    feed_grads = line.call(
+        feed_weight_kernel,
+        shape_of((column_parts, 2 * sub, width)),
+        [tokens_two[i] for i in range(4)]
+        + [d_outs[i] for i in range(4)]
+        + [*near[0:2], *distant[0:2], *near[2:4], *distant[2:4]],
+        "feed_weight",
+    ).reshape(2 * sub * column_parts, width)
+    feed_grads, grad_far = lax.optimization_barrier((feed_grads, grad_far))
+    grad_parts = grad_parts[:2] + (grad_far,)
+    line.token = grad_far
+    groups = column_parts // 2
+    feed_sum = lax.psum_scatter(feed_grads, "dp", scatter_dimension=0, tiled=True)
+
+    d_middle, d_branch, d_attended, d_mod_two = line.call(
+        functools.partial(proj_backward_kernel, sizes),
+        (
+            shape_of(full, F32),
+            shape_of(full),
+            shape_of(full),
+            shape_of((clips, 3, width), F32),
+        ),
+        (cotangent, mod, middle, branch, *grad_parts, proj_full),
+        "proj_backward",
+    )
+    d_mixed = line.call(
+        functools.partial(attn_backward_kernel, (clips, span, frames, width, qkv_cols)),
+        shape_of((column_parts, row_count, -(-qkv_cols // 128) * 128)),
+        (mixed, probs, d_attended),
+        "attn_backward",
+    )
+    own_side = (hidden, attended, d_mixed, d_branch)
+    far_side = [swap(array, 1, count) for array in own_side]
+    out_send = line.sum_low(distant[6], swap(distant[7], 1, count))
+    out_far = swap(out_send, 2, count)
+
+    attn_grads, first = {}, {}
+    for distances in (range(groups - 1, groups // 2 - 1, -1), range(groups // 2 - 1, -1, -1)):
+        grads = line.call(
+            functools.partial(attn_weight_kernel, packing, distances),
+            [shape_of((2, height // 2, packing.width))] * (2 * len(distances)),
+            (*own_side, *far_side),
+            "attn_weight",
+            scratch=(
+                pltpu.VMEM((width, 2 * row_count), LOW),
+                pltpu.VMEM((width, 2 * row_count), LOW),
+                pltpu.VMEM((column_parts, 2 * row_count, proj_cols), LOW),
+            ),
+        )
+        for index, distance in enumerate(distances):
+            attn_grads[distance] = grads[2 * index]
+            first[distance] = swap(grads[2 * index + 1], y_mask, count)
+    input_grad, d_mod_one = line.call(
+        functools.partial(qkv_backward_kernel, sizes, packing, places),
+        (shape_of(full), shape_of((clips, 2, width), F32)),
+        (tokens, mod, d_middle, d_mixed, *blocks),
+        "qkv_backward",
+        [VMEM_SPEC] * 4 + [ANY_SPEC] * len(blocks),
+        (weight_scratch, pltpu.VMEM(full, F32), weight_sems),
+    )
+    block_shape = (height // 2, packing.width)
+    stay, second, attn_z = {}, {}, {}
+
+    def split_sum(index):
+        stay[index], leave = line.call(
+            split_sum_kernel,
+            (shape_of(block_shape, F32), shape_of(block_shape)),
+            (attn_grads[index], first[index]),
+            "split_sum",
+        )
+        second[index] = swap(leave, x_mask, count)
+
+    def attn_sum(index):
+        summed = line.sum_low(stay[index], second[index])
+        attn_z[index] = swap(summed, z_masks[index - 1], count)
+
+    split_sum(3)
+    split_sum(2)
+    attn_sum(3)
+    attn_sum(2)
+    result, d_gate_two = line.call(
+        functools.partial(out_finish_kernel, (clips, span, 32)),
+        (shape_of(full), shape_of((clips, 1, width), F32)),
+        (near[6], swap(near[7], 1, count), out_far, middle, cotangent, mod),
+        "out_finish",
+    )
+    result = result.reshape(inputs.shape)
+    d_mod = jnp.concatenate([d_mod_one, d_mod_two, d_gate_two], axis=1)
+    split_sum(1)
+    split_sum(0)
+    attn_sum(1)
+    back = line.call(
+        feed_total_kernel,
+        shape_of((row_parts, 2, sub, height)),
+        (feed_sum,),
+        "feed_total",
+    )
+    back = lax.all_to_all(back, "fsdp", 0, 0, tiled=True)
+    up_grad, down_grad_t = line.call(
+        feed_finish_kernel,
+        (shape_of(up_weight.shape, F32), shape_of(down_weight.shape[::-1], F32)),
+        (back,),
+        "feed_finish",
+    )
+    down_grad = down_grad_t.T
+    qkv_grad, proj_grad_t = line.call(
+        functools.partial(attn_finish_kernel, packing),
+        (shape_of((height, qkv_cols), F32), shape_of((proj_cols, height), F32)),
+        (stay[0], second[0], attn_z[3], attn_z[2], attn_z[1]),
+        "attn_finish",
+    )
+    proj_grad = proj_grad_t.T
+
+    mod_send = d_mod.reshape(clips, column_parts, ada_cols).transpose(1, 0, 2)
+    mod_send = jnp.broadcast_to(
+        mod_send.reshape(column_parts, 1, clips * ada_cols),
+        (column_parts, row_parts, clips * ada_cols),
+    ).reshape(count, clips * ada_cols)
+    d_mod_all = padded_exchange(mod_send, count).reshape(count * clips, ada_cols)
+    ada_grad = lax.dot_general(
+        cond_all.astype(F32),
+        d_mod_all,
+        (((0,), (0,)), ((), ())),
+        precision=lax.Precision.HIGHEST,
+        preferred_element_type=F32,
+    )
+    return (
+        result,
+        input_grad.reshape(inputs.shape),
+        ada_grad,
+        qkv_grad,
+        proj_grad,
+        up_grad,
+        down_grad,
+    )
+
+
 def solution(mesh):
+    column_parts, row_parts = mesh.shape["dp"], mesh.shape["fsdp"]
+    body = general_body
+    if (column_parts, row_parts) == (8, 4):
+        body = functools.partial(fast_body, column_parts, row_parts)
+    clip_spec = P(AXES, None, None, None)
     return jax.shard_map(
         body,
         mesh=mesh,
         in_specs=(
-            P(("dp", "fsdp"), None, None, None),
-            P(("dp", "fsdp"), None, None, None),
-            P(("dp", "fsdp")),
-            P(("dp", "fsdp")),
-            P(("dp", "fsdp")),
+            clip_spec,
+            clip_spec,
+            P(AXES),
+            P(AXES),
+            P(AXES),
             P(),
             P(),
-            P("fsdp", "dp"),
-            P("fsdp", "dp"),
-            P("fsdp", "dp"),
-            P("fsdp", "dp"),
-            P("fsdp", "dp"),
-        ),
-        out_specs=(
-            P(("dp", "fsdp"), None, None, None),
-            P(("dp", "fsdp"), None, None, None),
-            P("fsdp", "dp"),
-            P("fsdp", "dp"),
-            P("fsdp", "dp"),
-            P("fsdp", "dp"),
-            P("fsdp", "dp"),
-        ),
+        )
+        + (P("fsdp", "dp"),) * 5,
+        out_specs=(clip_spec, clip_spec) + (P("fsdp", "dp"),) * 5,
         check_vma=False,
     )

time: 1640 us -> 378 us (0.23)
  the two profiles are of different devices: /device:TPU:0 before, /device:TPU:12 now
where the time goes in v3:
time: 378 us; the launch traced here: 372 us
  Pallas kernels  145 us (38%)
  waiting for transfers between devices  106 us (28%)
  starting transfers between devices  47.9 us (13%)
  local copies, waits for them, and re-layouts  30.1 us (8%)
  blocking collectives  25.8 us (7%)
  between operations  14.9 us (4%)
    pallas_call x24, Pallas kernels, call(): pl.pallas_call(kernel, out_shape=shapes, in_specs=specs or [VMEM_SPEC] *...  145 us
    ppermute x44, waiting for transfers between devices, swap(): return lax.ppermute(value, AXES, [(i, i ^ mask) for i in range(count)])  86.5 us
    ppermute x44, starting transfers between devices, swap(): return lax.ppermute(value, AXES, [(i, i ^ mask) for i in range(count)])  28.4 us
    all_to_all x1, blocking collectives, fast_body(): conds = lax.all_to_all(conds, 'dp', 0, 0, tiled=True)  25.8 us
    unnamed x121, local copies, waits for them, and re-layouts  21.3 us
    all_to_all x2, waiting for transfers between devices, padded_exchange(): got = lax.all_to_all(rows, AXES, 0, 0, tiled=True)  16.7 us
    all_to_all x2, starting transfers between devices, padded_exchange(): got = lax.all_to_all(rows, AXES, 0, 0, tiled=True)  11.3 us
  transfers between devices with their start and end apart: 50, of which 20 were waited for; matrix products, arithmetic and copies ran while one was open for 2% of the time, Pallas kernels for 33%

profile of v3, /device:TPU:12, one launch (start us, length us, event | category | flops | bytes accessed | tf_op | source)
XLA Modules:
  0.0 372.5 jit_solution(14464142920540634768)
XLA Ops:
  13.0 4.1 %all-to-all-start = ((bf16[4,304,288]{1,2,0:T(8,128)(2,1)}), bf16[4,304,288]{1,2,0:T(8,128)(2,1)S(1)}, u32[]{:S(2)}, u32[]{:S(2)}) async-start(bf16[4,304,288]{1,2,0:T(8,128)(2,1)} %copy.26), calls=%async_computation | async-start | bytes 1769472 | tf_op jit(solution)/shard_map/all_to_all | solution.py:870
  22.2 9.0 %collective-permute-done = bf16[1,144,1152]{2,1,0:T(8,128)(2,1)S(1)} collective-permute-done((bf16[1,144,1152]{2,1,0:T(8,128)(2,1)S(1)}, bf16[1,144,1152]{2,1,0:T(8,128)(2,1)S(1)}, u32[]{:S(2)}, u32[]{:S(2)}) %collective-permute-start) | collective-permute-done | bytes 331808 | tf_op jit(solution)/shard_map/ppermute | solution.py:808
  31.3 11.3 %collective-permute-done.1 = bf16[1,144,1152]{2,1,0:T(8,128)(2,1)S(1)} collective-permute-done((bf16[1,144,1152]{2,1,0:T(8,128)(2,1)S(1)}, bf16[1,144,1152]{2,1,0:T(8,128)(2,1)S(1)}, u32[]{:S(2)}, u32[]{:S(2)}) %collective-permute-start.1) | collective-permute-done | bytes 331808 | tf_op jit(solution)/shard_map/ppermute | solution.py:808
  42.5 7.0 %collective-permute-done.2 = bf16[1,144,1152]{2,1,0:T(8,128)(2,1)S(1)} collective-permute-done((bf16[1,144,1152]{2,1,0:T(8,128)(2,1)S(1)}, bf16[1,144,1152]{2,1,0:T(8,128)(2,1)S(1)}, u32[]{:S(2)}, u32[]{:S(2)}) %collective-permute-start.2) | collective-permute-done | bytes 331808 | tf_op jit(solution)/shard_map/ppermute | solution.py:808
  61.1 25.8 %all_to_all.25.conds = bf16[8,16,384]{2,1,0:T(8,128)(2,1)} all-to-all(bf16[8,16,384]{2,1,0:T(8,128)(2,1)S(1)} %broadcast_in_dim.20), channel_id=1, replica_groups=mesh['dp'=8,'fsdp'=4] {'dp'}, dimensions={0} | all-to-all | bytes 196608 | tf_op jit(solution)/shard_map/all_to_all | solution.py:881
  92.2 5.2 %all-to-all-start.2 = ((f32[32,16,128]{2,1,0:T(8,128)}), f32[32,16,128]{2,1,0:T(8,128)S(1)}, u32[]{:S(2)}, u32[]{:S(2)}) async-start(f32[32,16,128]{2,1,0:T(8,128)} %bitcast.57), calls=%async_computation.2 | async-start | bytes 524288 | tf_op jit(solution)/shard_map/all_to_all | solution.py:815
  98.1 16.7 %all-to-all-done.2 = f32[32,16,128]{2,1,0:T(8,128)S(1)} async-done(((f32[32,16,128]{2,1,0:T(8,128)}), f32[32,16,128]{2,1,0:T(8,128)S(1)}, u32[]{:S(2)}, u32[]{:S(2)}) %all-to-all-start.2) | async-done | bytes 262176 | tf_op jit(solution)/shard_map/all_to_all | solution.py:815
  114.9 5.8 %collective-permute-done.5.refs_9_.refs_10_ = bf16[1,144,1152]{2,1,0:T(8,128)(2,1)S(1)} collective-permute-done((bf16[1,144,1152]{2,1,0:T(8,128)(2,1)S(1)}, bf16[1,144,1152]{2,1,0:T(8,128)(2,1)S(1)}, u32[]{:S(2)}, u32[]{:S(2)}) %collective-permute-start.5) | collective-permute-done | bytes 331808 | tf_op jit(solution)/shard_map/ppermute | solution.py:808
  125.3 21.7 %attn_forward.1 = (bf16[256,1152]{1,0:T(8,128)(2,1)}, bf16[8,256,432]{2,1,0:T(8,128)(2,1)}, bf16[2,16,128,128]{3,2,1,0:T(8,128)(2,1)}, bf16[256,1152]{1,0:T(8,12...) custom-call(s32[2]{0:T(128)} %refs_0_.3, ...), custom_call_target="tpu_custom_call" | custom-call | flops 1000 | bytes 100 | tf_op jit(solution)/shard_map/attn_forward/pallas_call | solution.py:790
  150.1 13.8 %feed_near.1 = (bf16[256,1152]{1,0:T(8,128)(2,1)}, bf16[256,1152]{1,0:T(8,128)(2,1)}, bf16[256,1152]{1,0:T(8,128)(2,1)}, bf16[256,1152]{1,0:T(8,128)(2,1)}, f32[...) custom-call(bf16[256,1152]{1,0:T(8,128)(2,1)} %get-tuple-element.152.refs_0_, ...), custom_call_target="tpu_custom_call" | custom-call | flops 1000 | bytes 100 | tf_op jit(solution)/shard_map/feed_near/pallas_call | solution.py:790
  166.8 13.5 %feed_distant.1 = (bf16[256,1152]{1,0:T(8,128)(2,1)}, bf16[256,1152]{1,0:T(8,128)(2,1)}, bf16[256,1152]{1,0:T(8,128)(2,1)}, bf16[256,1152]{1,0:T(8,128)(2,1)}, f...) custom-call(bf16[256,1152]{1,0:T(8,128)(2,1)} %copy-done.10, ...), custom_call_target="tpu_custom_call" | custom-call | flops 1000 | bytes 100 | tf_op jit(solution)/shard_map/feed_distant/pallas_call | solution.py:790
  186.1 12.3 %feed_weight.1 = bf16[8,288,1152]{2,1,0:T(8,128)(2,1)} custom-call(bf16[256,1152]{1,0:T(8,128)(2,1)} %get-tuple-element.152.refs_0_, bf16[256,1152]{1,0:T(8,128)(2,1)} %copy-done.9, bf16[256,1152]{1,0:T(8,128)(2,1)} %copy-done.10, bf16[256,1152]{1,0:T(8,128)(2,1)} %copy-done.12, bf16[256,1152]{1,0:T(8,128)(2,1)} %copy-done.3, bf16[256,1152]{1,0:T(8,128)(2,1)} %copy-done.7, ...), custom_call_target="tpu_custom_call" | custom-call | flops 1000 | bytes 100 | tf_op jit(solution)/shard_map/feed_weight/pallas_call | solution.py:790
  205.4 7.9 %proj_backward.1 = (f32[256,1152]{1,0:T(8,128)}, bf16[256,1152]{1,0:T(8,128)(2,1)}, bf16[256,1152]{1,0:T(8,128)(2,1)}, f32[2,3,1152]{2,1,0:T(4,128)}) custom-call(bf16[256,1152]{1,0:T(8,128)(2,1)} %bitcast.42, f32[2,6,1152]{2,1,0:T(8,128)} %copy-done.19, f32[256,1152]{1,0:T(8,128)} %get-tuple-element.161.refs_2_.refs_3_, ...), custom_call_target="tpu_custom_call" | custom-call | flops 1000 | bytes 100 | tf_op jit(solution)/shard_map/proj_backward/pallas_call | solution.py:790
  213.4 10.5 %attn_backward.1.refs_2_.refs_3_ = bf16[8,256,512]{2,1,0:T(8,128)(2,1)} custom-call(bf16[8,256,432]{2,1,0:T(8,128)(2,1)} %get-tuple-element.167.refs_0_, bf16[2,16,128,128]{3,2,1,0:T(8,128)(2,1)} %get-tuple-element.168.refs_1_, bf16[256,1152]{1,0:T(8,128)(2,1)} %get-tuple-element.169.refs_2_), custom_call_target="tpu_custom_call" | custom-call | flops 1000 | bytes 100 | tf_op jit(solution)/shard_map/attn_backward/pallas_call | solution.py:790
  234.4 7.5 %attn_weight.2 = (bf16[2,144,1152]{2,1,0:T(8,128)(2,1)}, bf16[2,144,1152]{2,1,0:T(8,128)(2,1)}, bf16[2,144,1152]{2,1,0:T(8,128)(2,1)}, bf16[2,144,1152]{2,1,0:T(8,128)(2,1)}) custom-call(bf16[256,1152]{1,0:T(8,128)(2,1)} %get-tuple-element.177.refs_0_, bf16[256,1152]{1,0:T(8,128)(2,1)} %get-tuple-element.173.refs_1_, ...), custom_call_target="tpu_custom_call" | custom-call | flops 1000 | bytes 100 | tf_op jit(solution)/shard_map/attn_weight/pallas_call | solution.py:790
  244.4 7.7 %attn_weight.3 = (bf16[2,144,1152]{2,1,0:T(8,128)(2,1)}, bf16[2,144,1152]{2,1,0:T(8,128)(2,1)}, bf16[2,144,1152]{2,1,0:T(8,128)(2,1)}, bf16[2,144,1152]{2,1,0:T(8,128)(2,1)}) custom-call(bf16[256,1152]{1,0:T(8,128)(2,1)} %get-tuple-element.177.refs_0_, bf16[256,1152]{1,0:T(8,128)(2,1)} %get-tuple-element.173.refs_1_, ...), custom_call_target="tpu_custom_call" | custom-call | flops 1000 | bytes 100 | tf_op jit(solution)/shard_map/attn_weight/pallas_call | solution.py:790
  252.1 12.8 %qkv_backward.1 = (bf16[256,1152]{1,0:T(8,128)(2,1)}, f32[2,2,1152]{2,1,0:T(2,128)}) custom-call(bf16[256,1152]{1,0:T(8,128)(2,1)} %bitcast.46, f32[2,6,1152]{2,1,0:T(8,128)} %copy-done.19, f32[256,1152]{1,0:T(8,128)} %get-tuple-element.180.refs_2_, bf16[8,256,512]{2,1,0:T(8,128)(2,1)} %attn_backward.1.refs_2_.refs_3_, bf16[1,144,1152]{2,1,0:T(8,128)(2,1)} %bitcast.48, ...), custom_call_target="tpu_custom_call" | custom-call | flops 1000 | bytes 100 | tf_op jit(solution)/shard_map/qkv_backward/pallas_call | solution.py:790
  269.7 4.3 %collective-permute-done.32.got = bf16[2,144,1152]{2,1,0:T(8,128)(2,1)S(1)} collective-permute-done((bf16[2,144,1152]{2,1,0:T(8,128)(2,1)}, bf16[2,144,1152]{2,1,0:T(8,128)(2,1)S(1)}, u32[]{:S(2)}, u32[]{:S(2)}) %collective-permute-start.32) | collective-permute-done | bytes 663584 | tf_op jit(solution)/shard_map/ppermute | solution.py:808
  282.8 3.7 collective-permute-done.34.refs_1_
  296.2 6.1 %all-to-all-start.3 = ((f32[32,16,128]{2,1,0:T(8,128)}), f32[32,16,128]{2,1,0:T(8,128)S(1)}, u32[]{:S(2)}, u32[]{:S(2)}) async-start(f32[32,16,128]{2,1,0:T(8,128)} %bitcast.23), calls=%async_computation.3 | async-start | bytes 524288 | tf_op jit(solution)/shard_map/all_to_all | solution.py:815
  306.9 10.2 %collective-permute-done.38.got = bf16[2,144,1152]{2,1,0:T(8,128)(2,1)S(1)} collective-permute-done((bf16[2,144,1152]{2,1,0:T(8,128)(2,1)}, bf16[2,144,1152]{2,1,0:T(8,128)(2,1)S(1)}, u32[]{:S(2)}, u32[]{:S(2)}) %collective-permute-start.38) | collective-permute-done | bytes 663584 | tf_op jit(solution)/shard_map/ppermute | solution.py:808
  325.3 4.2 %all-to-all-start.4 = ((bf16[4,2,144,288]{3,2,1,0:T(8,128)(2,1)}), bf16[4,2,144,288]{3,2,1,0:T(8,128)(2,1)S(1)}, u32[]{:S(2)}, u32[]{:S(2)}) async-start(bf16[4,2,144,288]{3,2,1,0:T(8,128)(2,1)} %feed_total.1), calls=%async_computation.5 | async-start | bytes 1769472 | tf_op jit(solution)/shard_map/all_to_all | solution.py:1086
  344.2 9.3 %collective-permute-done.42.refs_3_ = bf16[144,1152]{1,0:T(8,128)(2,1)S(1)} collective-permute-done((bf16[144,1152]{1,0:T(8,128)(2,1)S(1)}, bf16[144,1152]{1,0:T(8,128)(2,1)S(1)}, u32[]{:S(2)}, u32[]{:S(2)}) %collective-permute-start.42) | collective-permute-done | bytes 331808 | tf_op jit(solution)/shard_map/ppermute | solution.py:808
  353.5 8.4 %collective-permute-done.41.refs_2_ = bf16[144,1152]{1,0:T(8,128)(2,1)S(1)} collective-permute-done((bf16[144,1152]{1,0:T(8,128)(2,1)S(1)}, bf16[144,1152]{1,0:T(8,128)(2,1)S(1)}, u32[]{:S(2)}, u32[]{:S(2)}) %collective-permute-start.41) | collective-permute-done | bytes 331808 | tf_op jit(solution)/shard_map/ppermute | solution.py:808
  (252 shorter events, 119.1 us)
Async XLA Ops:
  13.0 37.3 %all-to-all-start = ((bf16[4,304,288]{1,2,0:T(8,128)(2,1)}), bf16[4,304,288]{1,2,0:T(8,128)(2,1)S(1)}, u32[]{:S(2)}, u32[]{:S(2)}) async-start(bf16[4,304,288]{1,2,0:T(8,128)(2,1)} %copy.26), calls=%async_computation | async-start | bytes 1769472 | tf_op jit(solution)/shard_map/all_to_all | solution.py:870
  17.1 132.2 %all-gather.2.cloned.1.call-start = ((), (), s32[]{:S(2)}) async-start(), calls=%async_computation.6 | async-start | bytes 5971968 | tf_op jit(solution)/shard_map/all_gather | solution.py:875
  17.2 25.4 %collective-permute-start.1 = (bf16[1,144,1152]{2,1,0:T(8,128)(2,1)S(1)}, bf16[1,144,1152]{2,1,0:T(8,128)(2,1)S(1)}, u32[]{:S(2)}, u32[]{:S(2)}) collective-permute-start(bf16[1,144,1152]{2,1,0:T(8,128)(2,1)S(1)} %bitcast.50), channel_id=1, source_target_pairs={{0,16},{1,17},{2,18},{3,19},{4,20},{5,21},{6,22},{7,23},{8,24},{9,... | collective-permute-start | bytes 995336 | tf_op jit(solution)/shard_map/ppermute | solution.py:808
  20.1 29.4 %collective-permute-start.2 = (bf16[1,144,1152]{2,1,0:T(8,128)(2,1)S(1)}, bf16[1,144,1152]{2,1,0:T(8,128)(2,1)S(1)}, u32[]{:S(2)}, u32[]{:S(2)}) collective-permute-start(bf16[1,144,1152]{2,1,0:T(8,128)(2,1)S(1)} %bitcast.51), channel_id=1, source_target_pairs={{0,24},{1,25},{2,26},{3,27},{4,28},{5,29},{6,30},{7,31},{8,16},{9,... | collective-permute-start | bytes 995336 | tf_op jit(solution)/shard_map/ppermute | solution.py:808
  20.6 28.9 %collective-permute-start.3 = (bf16[1,144,1152]{2,1,0:T(8,128)(2,1)S(1)}, bf16[1,144,1152]{2,1,0:T(8,128)(2,1)S(1)}, u32[]{:S(2)}, u32[]{:S(2)}) collective-permute-start(bf16[1,144,1152]{2,1,0:T(8,128)(2,1)S(1)} %bitcast.52), channel_id=1, source_target_pairs={{0,4},{1,5},{2,6},{3,7},{4,0},{5,1},{6,2},{7,3},{8,12},{9,13},{10,... | collective-permute-start | bytes 995336 | tf_op jit(solution)/shard_map/ppermute | solution.py:808
  22.1 27.4 %collective-permute-start.4 = (bf16[1,144,1152]{2,1,0:T(8,128)(2,1)S(1)}, bf16[1,144,1152]{2,1,0:T(8,128)(2,1)}, u32[]{:S(2)}, u32[]{:S(2)}) collective-permute-start(bf16[1,144,1152]{2,1,0:T(8,128)(2,1)S(1)} %bitcast.53), channel_id=1, source_target_pairs={{0,2},{1,3},{2,0},{3,1},{4,6},{5,7},{6,4},{7,5},{8,10},{9,11},{10,... | collective-permute-start | bytes 995336 | tf_op jit(solution)/shard_map/ppermute | solution.py:808
  54.1 32.8 %collective-permute-start.11 = (bf16[3,144,1152]{2,1,0:T(8,128)(2,1)S(1)}, bf16[3,144,1152]{2,1,0:T(8,128)(2,1)S(1)}, u32[]{:S(2)}, u32[]{:S(2)}) collective-permute-start(bf16[3,144,1152]{2,1,0:T(8,128)(2,1)S(1)} %constant_dynamic-update-slice_fusion.refs_6_.refs_7_), channel_id=1, source_target_pairs={{0,1},{1,0},{2,3},{3,2},{4,5},{5,4},{6,7},{7,6},{8,9},{9,8},{10,11... | collective-permute-start | bytes 2985992 | tf_op jit(solution)/shard_map/ppermute | solution.py:808
  54.2 32.7 %collective-permute-start.6 = (bf16[3,144,1152]{2,1,0:T(8,128)(2,1)S(1)}, bf16[3,144,1152]{2,1,0:T(8,128)(2,1)}, u32[]{:S(2)}, u32[]{:S(2)}) collective-permute-start(bf16[3,144,1152]{2,1,0:T(8,128)(2,1)S(1)} %constant_dynamic-update-slice_fusion.refs_6_.refs_7_), channel_id=1, source_target_pairs={{0,4},{1,5},{2,6},{3,7},{4,0},{5,1},{6,2},{7,3},{8,12},{9,13},{10,... | collective-permute-start | bytes 2985992 | tf_op jit(solution)/shard_map/ppermute | solution.py:808
  55.7 31.2 %collective-permute-start.7 = (bf16[3,144,1152]{2,1,0:T(8,128)(2,1)S(1)}, bf16[3,144,1152]{2,1,0:T(8,128)(2,1)}, u32[]{:S(2)}, u32[]{:S(2)}) collective-permute-start(bf16[3,144,1152]{2,1,0:T(8,128)(2,1)S(1)} %constant_dynamic-update-slice_fusion.refs_6_.refs_7_), channel_id=1, source_target_pairs={{0,2},{1,3},{2,0},{3,1},{4,6},{5,7},{6,4},{7,5},{8,10},{9,11},{10,... | collective-permute-start | bytes 2985992 | tf_op jit(solution)/shard_map/ppermute | solution.py:808
  56.1 30.8 %collective-permute-start.9 = (bf16[1,144,1152]{2,1,0:T(8,128)(2,1)S(1)}, bf16[1,144,1152]{2,1,0:T(8,128)(2,1)}, u32[]{:S(2)}, u32[]{:S(2)}) collective-permute-start(bf16[1,144,1152]{2,1,0:T(8,128)(2,1)S(1)} %collective-permute-done.3.refs_4_.refs_5_), channel_id=1, source_target_pairs={{0,1},{1,0},{2,3},{3,2},{4,5},{5,4},{6,7},{7,6},{8,9},{9,8},{10,11... | collective-permute-start | bytes 995336 | tf_op jit(solution)/shard_map/ppermute | solution.py:808
  58.9 28.0 %collective-permute-start.10 = (bf16[1,144,1152]{2,1,0:T(8,128)(2,1)}, bf16[1,144,1152]{2,1,0:T(8,128)(2,1)S(1)}, u32[]{:S(2)}, u32[]{:S(2)}) collective-permute-start(bf16[1,144,1152]{2,1,0:T(8,128)(2,1)} %collective-permute-done.4.refs_5_.refs_6_), channel_id=1, source_target_pairs={{0,1},{1,0},{2,3},{3,2},{4,5},{5,4},{6,7},{7,6},{8,9},{9,8},{10,11... | collective-permute-start | bytes 995336 | tf_op jit(solution)/shard_map/ppermute | solution.py:808
  86.9 33.8 %collective-permute-start.12 = (bf16[3,144,1152]{2,1,0:T(8,128)(2,1)}, bf16[3,144,1152]{2,1,0:T(8,128)(2,1)}, u32[]{:S(2)}, u32[]{:S(2)}) collective-permute-start(bf16[3,144,1152]{2,1,0:T(8,128)(2,1)} %collective-permute-done.6.refs_7_.refs_8_), channel_id=1, source_target_pairs={{0,2},{1,3},{2,0},{3,1},{4,6},{5,7},{6,4},{7,5},{8,10},{9,11},{10,... | collective-permute-start | bytes 2985992 | tf_op jit(solution)/shard_map/ppermute | solution.py:808
  87.4 33.4 %collective-permute-start.13 = (bf16[3,144,1152]{2,1,0:T(8,128)(2,1)}, bf16[3,144,1152]{2,1,0:T(8,128)(2,1)}, u32[]{:S(2)}, u32[]{:S(2)}) collective-permute-start(bf16[3,144,1152]{2,1,0:T(8,128)(2,1)} %collective-permute-done.6.refs_7_.refs_8_), channel_id=1, source_target_pairs={{0,1},{1,0},{2,3},{3,2},{4,5},{5,4},{6,7},{7,6},{8,9},{9,8},{10,11... | collective-permute-start | bytes 2985992 | tf_op jit(solution)/shard_map/ppermute | solution.py:808
  87.4 33.4 %collective-permute-start.14 = (bf16[3,144,1152]{2,1,0:T(8,128)(2,1)}, bf16[3,144,1152]{2,1,0:T(8,128)(2,1)}, u32[]{:S(2)}, u32[]{:S(2)}) collective-permute-start(bf16[3,144,1152]{2,1,0:T(8,128)(2,1)} %collective-permute-done.7.refs_8_.refs_9_), channel_id=1, source_target_pairs={{0,1},{1,0},{2,3},{3,2},{4,5},{5,4},{6,7},{7,6},{8,9},{9,8},{10,11... | collective-permute-start | bytes 2985992 | tf_op jit(solution)/shard_map/ppermute | solution.py:808
  97.4 225.6 %reduce-scatter.2.cloned.1.call-start = ((), (), s32[]{:S(2)}) async-start(), calls=%async_computation.7 | async-start | bytes 5971968 | tf_op jit(solution)/shard_map/reduce_scatter | solution.py:1001
  122.0 25.7 %collective-permute-start.18 = (bf16[256,1152]{1,0:T(8,128)(2,1)S(1)}, bf16[256,1152]{1,0:T(8,128)(2,1)S(1)}, u32[]{:S(2)}, u32[]{:S(2)}) collective-permute-start(bf16[256,1152]{1,0:T(8,128)(2,1)S(1)} %fusion.refs_2_.refs_4_), channel_id=1, source_target_pairs={{0,1},{1,0},{2,3},{3,2},{4,5},{5,4},{6,7},{7,6},{8,9},{9,8},{10,11... | collective-permute-start | bytes 1769480 | tf_op jit(solution)/shard_map/ppermute | solution.py:808
  122.1 25.4 %collective-permute-start.21 = (bf16[256,1152]{1,0:T(8,128)(2,1)S(1)}, bf16[256,1152]{1,0:T(8,128)(2,1)S(1)}, u32[]{:S(2)}, u32[]{:S(2)}) collective-permute-start(bf16[256,1152]{1,0:T(8,128)(2,1)S(1)} %fusion.refs_2_.refs_4_), channel_id=1, source_target_pairs={{0,2},{1,3},{2,0},{3,1},{4,6},{5,7},{6,4},{7,5},{8,10},{9,11},{10,... | collective-permute-start | bytes 1769480 | tf_op jit(solution)/shard_map/ppermute | solution.py:808
  242.4 31.6 %collective-permute-start.32 = (bf16[2,144,1152]{2,1,0:T(8,128)(2,1)}, bf16[2,144,1152]{2,1,0:T(8,128)(2,1)S(1)}, u32[]{:S(2)}, u32[]{:S(2)}) collective-permute-start(bf16[2,144,1152]{2,1,0:T(8,128)(2,1)} %get-tuple-element.186), channel_id=1, source_target_pairs={{0,2},{1,3},{2,0},{3,1},{4,6},{5,7},{6,4},{7,5},{8,10},{9,11},{10,... | collective-permute-start | bytes 1990664 | tf_op jit(solution)/shard_map/ppermute | solution.py:808
  243.9 45.3 %collective-permute-start.35 = (bf16[256,1152]{1,0:T(8,128)(2,1)}, bf16[256,1152]{1,0:T(8,128)(2,1)S(1)}, u32[]{:S(2)}, u32[]{:S(2)}) collective-permute-start(bf16[256,1152]{1,0:T(8,128)(2,1)} %get-tuple-element.193), channel_id=1, source_target_pairs={{0,1},{1,0},{2,3},{3,2},{4,5},{5,4},{6,7},{7,6},{8,9},{9,8},{10,11... | collective-permute-start | bytes 1769480 | tf_op jit(solution)/shard_map/ppermute | solution.py:808
  243.9 45.3 %collective-permute-start.36 = (bf16[256,1152]{1,0:T(8,128)(2,1)S(1)}, bf16[256,1152]{1,0:T(8,128)(2,1)S(1)}, u32[]{:S(2)}, u32[]{:S(2)}) collective-permute-start(bf16[256,1152]{1,0:T(8,128)(2,1)S(1)} %copy-done.32), channel_id=1, source_target_pairs={{0,2},{1,3},{2,0},{3,1},{4,6},{5,7},{6,4},{7,5},{8,10},{9,11},{10,... | collective-permute-start | bytes 1769480 | tf_op jit(solution)/shard_map/ppermute | solution.py:808
  279.3 37.8 %collective-permute-start.38 = (bf16[2,144,1152]{2,1,0:T(8,128)(2,1)}, bf16[2,144,1152]{2,1,0:T(8,128)(2,1)S(1)}, u32[]{:S(2)}, u32[]{:S(2)}) collective-permute-start(bf16[2,144,1152]{2,1,0:T(8,128)(2,1)} %get-tuple-element.202), channel_id=1, source_target_pairs={{0,2},{1,3},{2,0},{3,1},{4,6},{5,7},{6,4},{7,5},{8,10},{9,11},{10,... | collective-permute-start | bytes 1990664 | tf_op jit(solution)/shard_map/ppermute | solution.py:808
  296.2 29.1 %all-to-all-start.3 = ((f32[32,16,128]{2,1,0:T(8,128)}), f32[32,16,128]{2,1,0:T(8,128)S(1)}, u32[]{:S(2)}, u32[]{:S(2)}) async-start(f32[32,16,128]{2,1,0:T(8,128)} %bitcast.23), calls=%async_computation.3 | async-start | bytes 524288 | tf_op jit(solution)/shard_map/all_to_all | solution.py:815
  331.1 30.8 %collective-permute-start.41 = (bf16[144,1152]{1,0:T(8,128)(2,1)S(1)}, bf16[144,1152]{1,0:T(8,128)(2,1)S(1)}, u32[]{:S(2)}, u32[]{:S(2)}) collective-permute-start(bf16[144,1152]{1,0:T(8,128)(2,1)S(1)} %copy-done.42), channel_id=1, source_target_pairs={{0,24},{1,25},{2,26},{3,27},{4,28},{5,29},{6,30},{7,31},{8,16},{9,... | collective-permute-start | bytes 995336 | tf_op jit(solution)/shard_map/ppermute | solution.py:808
  332.8 29.1 %collective-permute-start.43 = (bf16[144,1152]{1,0:T(8,128)(2,1)S(1)}, bf16[144,1152]{1,0:T(8,128)(2,1)}, u32[]{:S(2)}, u32[]{:S(2)}) collective-permute-start(bf16[144,1152]{1,0:T(8,128)(2,1)S(1)} %copy-done.44), channel_id=1, source_target_pairs={{0,8},{1,9},{2,10},{3,11},{4,12},{5,13},{6,14},{7,15},{8,0},{9,1},... | collective-permute-start | bytes 995336 | tf_op jit(solution)/shard_map/ppermute | solution.py:808
  (82 other events, 650.4 us)
Sparse Core Ops, SparseCore 0:
  53.0 93.1 all-gather.1
  201.5 109.6 reduce-scatter.1

commit v4 on v3

--- a/solution.py
+++ b/solution.py
@@ -368,7 +368,7 @@
     lengths, tokens, mod = refs[:3]
     block_refs = refs[3 : 3 + blocks]
     hidden, mixed, probs_out, attended, branch, middle, hidden_two, proj = refs[3 + blocks : 11 + blocks]
-    weight, branch_full, sems = refs[11 + blocks :]
+    weight, branch_full, hidden_s, attended_s, sems = refs[11 + blocks :]
     copies = start_blocks(places, block_refs, weight, sems)
     column_parts, row_parts = weight.shape[0], weight.shape[1]
     size = width // HEADS
@@ -378,7 +378,7 @@
         rows = pl.ds(pl.multiple_of(step * chunk, chunk), chunk)
         clip_mod = mod[step * chunk // span]
         unit, _ = stats(tokens[rows, :].astype(F32))
-        hidden[rows, :] = (unit * (1.0 + clip_mod[1:2]) + clip_mod[0:1]).astype(LOW)
+        hidden_s[rows, :] = (unit * (1.0 + clip_mod[1:2]) + clip_mod[0:1]).astype(LOW)
         return carry
 
     lax.fori_loop(0, clips * span // chunk, first_norm, 0)
@@ -395,7 +395,7 @@
             ],
             axis=0,
         )
-        mixed[place] = dot_nn(hidden[...], columns).astype(LOW)
+        mixed[place] = dot_nn(hidden_s[...], columns).astype(LOW)
 
     for clip in range(clips):
         rows = slice(clip * span, (clip + 1) * span)
@@ -416,10 +416,10 @@
             ]
             for head, prob, value in zip(group, probs, values):
                 probs_out[clip, head] = prob
-                attended[rows, head * size : (head + 1) * size] = value.astype(LOW)
+                attended_s[rows, head * size : (head + 1) * size] = value.astype(LOW)
 
     join_proj(packing, weight, proj)
-    branch_full[...] = dot_nn(attended[...], proj[...])
+    branch_full[...] = dot_nn(attended_s[...], proj[...])
 
     def second_norm(step, carry):
         rows = pl.ds(pl.multiple_of(step * chunk, chunk), chunk)
@@ -433,6 +433,8 @@
         return carry
 
     lax.fori_loop(0, clips * span // chunk, second_norm, 0)
+    hidden[...] = hidden_s[...].T
+    attended[...] = attended_s[...].T
 
 
 def norm_back(grad, values, scale_row):
@@ -554,15 +556,12 @@
 
 
 def attn_weight_kernel(packing, distances, *refs):
-    own, far, outs = refs[:4], refs[4:8], refs[8:-3]
-    hidden_t, attended_t, d_pieces = refs[-3:]
+    own, far, outs, d_pieces = refs[:4], refs[4:8], refs[8:-1], refs[-1]
     half, qkv_cols, proj_cols = packing.half, packing.qkv_cols, packing.proj_cols
-    row_count = own[0].shape[0]
+    row_count = own[0].shape[1]
     column_parts = own[2].shape[0]
-    row_parts = own[0].shape[1] // (2 * half)
+    row_parts = own[0].shape[0] // (2 * half)
     for start, group in ((0, own), (row_count, far)):
-        hidden_t[:, start : start + row_count] = group[0][...].T
-        attended_t[:, start : start + row_count] = group[1][...].T
         for place in range(column_parts):
             d_pieces[place, start : start + row_count, :] = columns_of(
                 group[3], slice(None), place, proj_cols
@@ -577,15 +576,19 @@
             d_proj = d_pieces[place]
             for other in range(row_parts // 2):
                 rows = pl.ds(pl.multiple_of((row ^ (2 * other)) * 2 * half, 16), 2 * half)
-                qkv = dot_nn(hidden_t[rows, :], d_qkv)
-                proj = dot_nn(attended_t[rows, :], d_proj)
+                hidden_t, attended_t = (
+                    jnp.concatenate([own[which][rows, :], far[which][rows, :]], axis=1)
+                    for which in range(2)
+                )
+                qkv = dot_nn(hidden_t, d_qkv)
+                proj = dot_nn(attended_t, d_proj)
                 outs[2 * index + other][x_bit] = packing.pack(qkv, proj).astype(LOW)
 
 
 def feed_kernel(chunk, parts, *refs):
-    sources, stacked, outs = refs[0:4], refs[4], refs[5:13]
-    hidden, d_outs, up_weight, down_weight, up_proj, d_activ, activ, d_up, wide, narrow = refs[13:23]
-    in_sems, weight_sems, out_sems = refs[23:]
+    sources, stacked, outs = refs[0:4], refs[4], refs[5:11]
+    hidden, d_outs, up_weight, down_weight, up_proj, d_activ, activ, d_up, wide, narrow = refs[11:21]
+    in_sems, weight_sems, out_sems = refs[21:]
     rows_each = sources[0].shape[0]
     half = stacked.shape[0] // (2 * parts)
     halves = [pl.ds(index * rows_each, rows_each) for index in range(2)]
@@ -637,30 +640,43 @@
     for index, rows in enumerate(halves):
         sent.append(started(activ.at[rows], outs[index], out_sems.at[index]))
         sent.append(started(d_up.at[rows], outs[2 + index], out_sems.at[2 + index]))
-    for which, total in enumerate(
-        (lambda: dot_nn(d_up[...], up_weight[...]), lambda: dot_nt(activ[...], down_weight[...]))
-    ):
-        value = total()
-        wide[which] = value[:rows_each]
-        narrow[which] = value[rows_each:].astype(LOW)
-        sent.append(started(narrow.at[which], outs[5 + 2 * which], out_sems.at[5 + 2 * which]))
-        sent.append(started(wide.at[which], outs[4 + 2 * which], out_sems.at[4 + 2 * which]))
+    value = dot_nn(d_up[...], up_weight[...])
+    narrow[...] = value[rows_each:].astype(LOW)
+    sent.append(started(narrow, outs[5], out_sems.at[5]))
+    wide[...] = value[:rows_each]
+    sent.append(started(wide, outs[4], out_sems.at[4]))
     for copy in sent:
         copy.wait()
 
 
-def feed_weight_kernel(*refs):
-    stacked = refs[16]
+def feed_weight_kernel(parts, *refs):
+    gathered, stacked, results = refs[16], refs[17], refs[18:22]
+    down_weight, sems = refs[22:]
+    half = gathered.shape[0] // (2 * parts)
+    copies = []
+    for part in range(parts):
+        copy = pltpu.make_async_copy(
+            gathered.at[pl.ds((2 * part + 1) * half, half)],
+            down_weight.at[pl.ds(part * half, half)],
+            sems.at[part],
+        )
+        copy.start()
+        copies.append(copy)
     hidden, d_outs, activ, d_up = (
         jnp.concatenate([ref[...] for ref in refs[i : i + 4]], axis=0) for i in (0, 4, 8, 12)
     )
-    parts, half = stacked.shape[0], stacked.shape[1] // 2
     for side, (left, right) in enumerate(((d_up, hidden), (d_outs, activ))):
         total = dot_tn(left, right).astype(LOW)
         for part in range(parts):
             stacked[part, side * half : (side + 1) * half, :] = total[
                 part * half : (part + 1) * half
             ]
+    for copy in copies:
+        copy.wait()
+    total = dot_nt(activ, down_weight[...])
+    rows = results[0].shape[0]
+    for index, result in enumerate(results):
+        result[...] = total[index * rows : (index + 1) * rows].astype(result.dtype)
 
 
 def modulation_kernel(conds, ada, part_out, ordered):
@@ -697,32 +713,6 @@
             send[part, sub : 2 * sub, pair * sub : (pair + 1) * sub] = down_t[:, start : start + sub]
 
 
-def sum_kernel(*refs):
-    total = refs[0][...].astype(F32)
-    for ref in refs[1:-1]:
-        total += ref[...].astype(F32)
-    refs[-1][...] = total.astype(refs[-1].dtype)
-
-
-def split_sum_kernel(kept, got, stay, leave):
-    total = kept[...].astype(F32) + got[...].astype(F32)
-    stay[...] = total[0]
-    leave[...] = total[1].astype(LOW)
-
-
-def feed_total_kernel(*refs):
-    total = refs[0][...].astype(F32)
-    for ref in refs[1:-1]:
-        total += ref[...].astype(F32)
-    out = refs[-1]
-    parts, sides, half, height = out.shape
-    for part in range(parts):
-        for side in range(sides):
-            out[part, side] = total[
-                side * half : (side + 1) * half, part * height : (part + 1) * height
-            ].astype(LOW)
-
-
 def feed_finish_kernel(back, up_grad, down_grad_t):
     parts, _, sub, height = back.shape
     pairs = height // sub
@@ -744,21 +734,6 @@
         rows = slice(side * packing.half, (side + 1) * packing.half)
         qkv_grad[rows, :] = packing.qkv_of(total, side)
         proj_grad_t[:, rows] = packing.proj_of(total, side).T
-
-
-def out_finish_kernel(sizes, *refs):
-    clips, span, chunk = sizes
-    first, second, third, middle, cotangent, mod, result, d_gate = refs
-    zero_row = jnp.zeros((1, middle.shape[1]), F32)
-    for clip in range(clips):
-
-        def step_rows(step, carry, clip=clip):
-            rows = pl.ds(pl.multiple_of(clip * span + step * chunk, chunk), chunk)
-            value = first[rows, :] + second[rows, :].astype(F32) + third[rows, :].astype(F32)
-            result[rows, :] = (middle[rows, :] + mod[clip, 5:6, :] * value).astype(LOW)
-            return carry + jnp.sum(cotangent[rows, :].astype(F32) * value, 0, keepdims=True)
-
-        d_gate[clip] = lax.fori_loop(0, span // chunk, step_rows, zero_row)
 
 
 VMEM_SPEC = pl.BlockSpec(memory_space=pltpu.VMEM)
@@ -801,7 +776,11 @@
         return results
 
     def sum_low(self, *arrays):
-        return self.call(sum_kernel, shape_of(arrays[0].shape), arrays, "sum_low")
+        total = after(arrays[0], self.token).astype(F32)
+        for array in arrays[1:]:
+            total += array.astype(F32)
+        self.token = total.astype(LOW)
+        return self.token
 
 
 def swap(value, mask, count):
@@ -922,10 +901,10 @@
     hidden, mixed, probs, attended, branch, middle, hidden_two, proj_full = line.call(
         functools.partial(attn_forward_kernel, sizes, packing, places),
         (
-            shape_of(full),
+            shape_of((width, row_count)),
             shape_of((column_parts, row_count, qkv_cols)),
             shape_of((clips, HEADS, span, span)),
-            shape_of(full),
+            shape_of((width, row_count)),
             shape_of(full),
             shape_of(full, F32),
             shape_of(full),
@@ -937,6 +916,8 @@
         (
             weight_scratch,
             pltpu.VMEM(full, F32),
+            pltpu.VMEM(full, LOW),
+            pltpu.VMEM(full, LOW),
             weight_sems,
         ),
         tied=2,
@@ -954,17 +935,17 @@
         pltpu.VMEM(pair_hidden, F32),
         pltpu.VMEM(pair_hidden, LOW),
         pltpu.VMEM(pair_hidden, LOW),
-        pltpu.VMEM((2,) + full, F32),
-        pltpu.VMEM((2,) + full, LOW),
+        pltpu.VMEM(full, F32),
+        pltpu.VMEM(full, LOW),
         pltpu.SemaphoreType.DMA((2, 2)),
         pltpu.SemaphoreType.DMA((column_parts, 2)),
-        pltpu.SemaphoreType.DMA((8,)),
+        pltpu.SemaphoreType.DMA((6,)),
     )
 
     def feed_call(index, name):
         return line.call(
             functools.partial(feed_kernel, 32, column_parts),
-            [shape_of((row_count, hidden_part))] * 4 + [shape_of(full, F32), shape_of(full)] * 2,
+            [shape_of((row_count, hidden_part))] * 4 + [shape_of(full, F32), shape_of(full)],
             (
                 tokens_two[index],
                 tokens_two[index + 1],
@@ -986,20 +967,27 @@
     grad_send = line.sum_low(distant[4], swap(distant[5], 1, count))
     grad_far = swap(grad_send, 2, count)
     grad_parts = (near[4], swap(near[5], 1, count), grad_far)
-    feed_grads = line.call(
-        feed_weight_kernel,
-        shape_of((column_parts, 2 * sub, width)),
+    feed_grads, *partials = line.call(
+        functools.partial(feed_weight_kernel, column_parts),
+        [shape_of((column_parts, 2 * sub, width))]
+        + [shape_of(full, F32), shape_of(full)]
+        + [shape_of(full)] * 2,
         [tokens_two[i] for i in range(4)]
         + [d_outs[i] for i in range(4)]
-        + [*near[0:2], *distant[0:2], *near[2:4], *distant[2:4]],
+        + [*near[0:2], *distant[0:2], *near[2:4], *distant[2:4], feed],
         "feed_weight",
-    ).reshape(2 * sub * column_parts, width)
+        [VMEM_SPEC] * 16 + [ANY_SPEC],
+        (pltpu.VMEM((width, hidden_part), LOW), pltpu.SemaphoreType.DMA((column_parts,))),
+    )
+    feed_grads = feed_grads.reshape(2 * sub * column_parts, width)
     feed_grads, grad_far = lax.optimization_barrier((feed_grads, grad_far))
     grad_parts = grad_parts[:2] + (grad_far,)
     line.token = grad_far
     groups = column_parts // 2
     feed_sum = lax.psum_scatter(feed_grads, "dp", scatter_dimension=0, tiled=True)
 
+    out_send = line.sum_low(partials[2], swap(partials[3], 1, count))
+    out_far = swap(out_send, 2, count)
     d_middle, d_branch, d_attended, d_mod_two = line.call(
         functools.partial(proj_backward_kernel, sizes),
         (
@@ -1019,9 +1007,6 @@
     )
     own_side = (hidden, attended, d_mixed, d_branch)
     far_side = [swap(array, 1, count) for array in own_side]
-    out_send = line.sum_low(distant[6], swap(distant[7], 1, count))
-    out_far = swap(out_send, 2, count)
-
     attn_grads, first = {}, {}
     for distances in (range(groups - 1, groups // 2 - 1, -1), range(groups // 2 - 1, -1, -1)):
         grads = line.call(
@@ -1029,15 +1014,19 @@
             [shape_of((2, height // 2, packing.width))] * (2 * len(distances)),
             (*own_side, *far_side),
             "attn_weight",
-            scratch=(
-                pltpu.VMEM((width, 2 * row_count), LOW),
-                pltpu.VMEM((width, 2 * row_count), LOW),
-                pltpu.VMEM((column_parts, 2 * row_count, proj_cols), LOW),
-            ),
+            scratch=(pltpu.VMEM((column_parts, 2 * row_count, proj_cols), LOW),),
         )
         for index, distance in enumerate(distances):
             attn_grads[distance] = grads[2 * index]
             first[distance] = swap(grads[2 * index + 1], y_mask, count)
+        if not len(distances) < len(first):
+            ffn_out = after(partials[0], line.token) + swap(partials[1], 1, count).astype(F32)
+            ffn_out += out_far.astype(F32)
+            result = (middle + gate_two * ffn_out).astype(LOW).reshape(inputs.shape)
+            d_gate_two = jnp.sum(
+                (cotangent.astype(F32) * ffn_out).reshape(clips, 1, span, width), axis=2
+            )
+            line.token = d_gate_two
     input_grad, d_mod_one = line.call(
         functools.partial(qkv_backward_kernel, sizes, packing, places),
         (shape_of(full), shape_of((clips, 2, width), F32)),
@@ -1046,65 +1035,51 @@
         [VMEM_SPEC] * 4 + [ANY_SPEC] * len(blocks),
         (weight_scratch, pltpu.VMEM(full, F32), weight_sems),
     )
-    block_shape = (height // 2, packing.width)
     stay, second, attn_z = {}, {}, {}
 
     def split_sum(index):
-        stay[index], leave = line.call(
-            split_sum_kernel,
-            (shape_of(block_shape, F32), shape_of(block_shape)),
-            (attn_grads[index], first[index]),
-            "split_sum",
-        )
+        kept = after(attn_grads[index], line.token)
+        stay[index] = kept[0].astype(F32) + first[index][0].astype(F32)
+        leave = (kept[1].astype(F32) + first[index][1].astype(F32)).astype(LOW)
+        line.token = leave
         second[index] = swap(leave, x_mask, count)
 
     def attn_sum(index):
         summed = line.sum_low(stay[index], second[index])
         attn_z[index] = swap(summed, z_masks[index - 1], count)
 
-    split_sum(3)
-    split_sum(2)
-    attn_sum(3)
-    attn_sum(2)
-    result, d_gate_two = line.call(
-        functools.partial(out_finish_kernel, (clips, span, 32)),
-        (shape_of(full), shape_of((clips, 1, width), F32)),
-        (near[6], swap(near[7], 1, count), out_far, middle, cotangent, mod),
-        "out_finish",
-    )
-    result = result.reshape(inputs.shape)
     d_mod = jnp.concatenate([d_mod_one, d_mod_two, d_gate_two], axis=1)
-    split_sum(1)
-    split_sum(0)
-    attn_sum(1)
-    back = line.call(
-        feed_total_kernel,
-        shape_of((row_parts, 2, sub, height)),
-        (feed_sum,),
-        "feed_total",
-    )
-    back = lax.all_to_all(back, "fsdp", 0, 0, tiled=True)
-    up_grad, down_grad_t = line.call(
-        feed_finish_kernel,
-        (shape_of(up_weight.shape, F32), shape_of(down_weight.shape[::-1], F32)),
-        (back,),
-        "feed_finish",
-    )
-    down_grad = down_grad_t.T
-    qkv_grad, proj_grad_t = line.call(
-        functools.partial(attn_finish_kernel, packing),
-        (shape_of((height, qkv_cols), F32), shape_of((proj_cols, height), F32)),
-        (stay[0], second[0], attn_z[3], attn_z[2], attn_z[1]),
-        "attn_finish",
-    )
-    proj_grad = proj_grad_t.T
-
     mod_send = d_mod.reshape(clips, column_parts, ada_cols).transpose(1, 0, 2)
     mod_send = jnp.broadcast_to(
         mod_send.reshape(column_parts, 1, clips * ada_cols),
         (column_parts, row_parts, clips * ada_cols),
     ).reshape(count, clips * ada_cols)
     d_mod_all = padded_exchange(mod_send, count).reshape(count * clips, ada_cols)
+    split_sum(3)
+    line.token, d_mod_all = lax.optimization_barrier((line.token, d_mod_all))
+    for index in (2, 1):
+        split_sum(index)
+        attn_sum(index + 1)
+    back = feed_sum.reshape(2, sub, row_parts, height).transpose(2, 0, 1, 3)
+    line.token, back = lax.optimization_barrier((line.token, back))
+    back = lax.all_to_all(back, "fsdp", 0, 0, tiled=True)
+    split_sum(0)
+    attn_sum(1)
+    qkv_grad, proj_grad_t = line.call(
+        functools.partial(attn_finish_kernel, packing),
+        (shape_of((height, qkv_cols), F32), shape_of((proj_cols, height), F32)),
+        (stay[0], second[0], attn_z[3], attn_z[2], attn_z[1]),
+        "attn_finish",
+    )
+    proj_grad = proj_grad_t.T
+    up_grad, down_grad_t = line.call(
+        feed_finish_kernel,
+        (shape_of(up_weight.shape, F32), shape_of(down_weight.shape[::-1], F32)),
+        (back,),
+        "feed_finish",
+    )
+    down_grad = down_grad_t.T
+
     ada_grad = lax.dot_general(
         cond_all.astype(F32),
         d_mod_all,

time: 378 us -> 362 us (0.958)
  the two profiles are of different devices: /device:TPU:12 before, /device:TPU:0 now
where the time goes in v4:
time: 362 us; the launch traced here: 357 us
  Pallas kernels  118 us (33%)
  waiting for transfers between devices  90.5 us (25%)
  starting transfers between devices  67.8 us (19%)
  local copies, waits for them, and re-layouts  24.8 us (7%)
  blocking collectives  24.3 us (7%)
  between operations  15 us (4%)
  other arithmetic  14.2 us (4%)
    pallas_call x13, Pallas kernels, call(): pl.pallas_call(kernel, out_shape=shapes, in_specs=specs or [VMEM_SPEC] *...  118 us
    ppermute x44, waiting for transfers between devices, swap(): return lax.ppermute(value, AXES, [(i, i ^ mask) for i in range(count)])  72.6 us
    ppermute x44, starting transfers between devices, swap(): return lax.ppermute(value, AXES, [(i, i ^ mask) for i in range(count)])  42.7 us
    all_to_all x1, blocking collectives, fast_body(): conds = lax.all_to_all(conds, 'dp', 0, 0, tiled=True)  24.3 us
    all_to_all x2, starting transfers between devices, padded_exchange(): got = lax.all_to_all(rows, AXES, 0, 0, tiled=True)  16.8 us
    all_to_all x2, waiting for transfers between devices, padded_exchange(): got = lax.all_to_all(rows, AXES, 0, 0, tiled=True)  14.3 us
    unnamed x107, local copies, waits for them, and re-layouts  12.7 us
  transfers between devices with their start and end apart: 50, of which 18 were waited for; matrix products, arithmetic and copies ran while one was open for 7% of the time, Pallas kernels for 28%

profile of v4, /device:TPU:0, one launch (start us, length us, event | category | flops | bytes accessed | tf_op | source)
XLA Modules:
  0.0 356.7 jit_solution(10412121395724239787)
XLA Ops:
  7.2 3.6 %prepare.1 = (bf16[144,1152]{1,0:T(8,128)(2,1)}, bf16[4,304,288]{2,1,0:T(8,128)(2,1)}) custom-call(s32[2]{0:T(128)} %refs_0_.2, s32[2]{0:T(128)} %refs_1_.1, bf16[1000,1152]{1,0:T(8,128)(2,1)} %refs_2_.1, bf16[101,1152]{1,0:T(8,128)(2,1)} %refs_3_.1, bf16[288,432]{1,0:T(8,128)(2,1)} %refs_4_.1, bf16[144,288]{1,0:T(8,128)(2,1)} %bitcast.91, ...), custom_call_target="tpu_custom_call" | custom-call | flops 1000 | bytes 100 | tf_op jit(solution)/shard_map/prepare/pallas_call | solution.py:765
  13.0 4.4 %all-to-all-start = ((bf16[4,304,288]{1,2,0:T(8,128)(2,1)}), bf16[4,304,288]{1,2,0:T(8,128)(2,1)S(1)}, u32[]{:S(2)}, u32[]{:S(2)}) async-start(bf16[4,304,288]{1,2,0:T(8,128)(2,1)} %copy.28), calls=%async_computation | async-start | bytes 1769472 | tf_op jit(solution)/shard_map/all_to_all | solution.py:849
  25.9 8.7 %collective-permute-done = bf16[1,144,1152]{2,1,0:T(8,128)(2,1)S(1)} collective-permute-done((bf16[1,144,1152]{2,1,0:T(8,128)(2,1)S(1)}, bf16[1,144,1152]{2,1,0:T(8,128)(2,1)S(1)}, u32[]{:S(2)}, u32[]{:S(2)}) %collective-permute-start) | collective-permute-done | bytes 331808 | tf_op jit(solution)/shard_map/ppermute | solution.py:787
  34.7 10.9 %collective-permute-done.1 = bf16[1,144,1152]{2,1,0:T(8,128)(2,1)S(1)} collective-permute-done((bf16[1,144,1152]{2,1,0:T(8,128)(2,1)S(1)}, bf16[1,144,1152]{2,1,0:T(8,128)(2,1)S(1)}, u32[]{:S(2)}, u32[]{:S(2)}) %collective-permute-start.1) | collective-permute-done | bytes 331808 | tf_op jit(solution)/shard_map/ppermute | solution.py:787
  58.8 24.3 %all_to_all.25.conds = bf16[8,16,384]{2,1,0:T(8,128)(2,1)} all-to-all(bf16[8,16,384]{2,1,0:T(8,128)(2,1)S(1)} %broadcast_in_dim.20), channel_id=1, replica_groups=mesh['dp'=8,'fsdp'=4] {'dp'}, dimensions={0} | all-to-all | bytes 196608 | tf_op jit(solution)/shard_map/all_to_all | solution.py:860
  89.9 8.8 %all-to-all-start.2 = ((f32[32,16,128]{2,1,0:T(8,128)}), f32[32,16,128]{2,1,0:T(8,128)S(1)}, u32[]{:S(2)}, u32[]{:S(2)}) async-start(f32[32,16,128]{2,1,0:T(8,128)} %bitcast.84), calls=%async_computation.2 | async-start | bytes 524288 | tf_op jit(solution)/shard_map/all_to_all | solution.py:794
  100.9 14.3 %all-to-all-done.2 = f32[32,16,128]{2,1,0:T(8,128)S(1)} async-done(((f32[32,16,128]{2,1,0:T(8,128)}), f32[32,16,128]{2,1,0:T(8,128)S(1)}, u32[]{:S(2)}, u32[]{:S(2)}) %all-to-all-start.2) | async-done | bytes 262176 | tf_op jit(solution)/shard_map/all_to_all | solution.py:794
  121.6 21.7 %attn_forward.1 = (bf16[1152,256]{1,0:T(8,128)(2,1)}, bf16[8,256,432]{2,1,0:T(8,128)(2,1)}, bf16[2,16,128,128]{3,2,1,0:T(8,128)(2,1)}, bf16[1152,256]{1,0:T(8,12...) custom-call(s32[2]{0:T(128)} %refs_0_.3, ...), custom_call_target="tpu_custom_call" | custom-call | flops 1000 | bytes 100 | tf_op jit(solution)/shard_map/attn_forward/pallas_call | solution.py:765
  145.6 3.7 %all-gather.2.cloned.1.call-done.refs_4_.refs_16_ = bf16[2304,1152]{1,0:T(8,128)(2,1)} async-done(((bf16[288,1152]{1,0:T(8,128)(2,1)}), bf16[2304,1152]{1,0:T(8,128)(2,1)}) %all-gather.2.cloned.1.call-update) | async-done | bytes 5308432 | tf_op jit(solution)/shard_map/all_gather | solution.py:854
  149.2 11.8 %feed_near.1 = (bf16[256,1152]{1,0:T(8,128)(2,1)}, bf16[256,1152]{1,0:T(8,128)(2,1)}, bf16[256,1152]{1,0:T(8,128)(2,1)}, bf16[256,1152]{1,0:T(8,128)(2,1)}, f32[...) custom-call(bf16[256,1152]{1,0:T(8,128)(2,1)} %get-tuple-element.140.refs_0_, bf16[256,1152]{1,0:T(8,128)(2,1)} %copy-done.16, ...), custom_call_target="tpu_custom_call" | custom-call | flops 1000 | bytes 100 | tf_op jit(solution)/shard_map/feed_near/pallas_call | solution.py:765
  164.0 11.9 %feed_distant.1 = (bf16[256,1152]{1,0:T(8,128)(2,1)}, bf16[256,1152]{1,0:T(8,128)(2,1)}, bf16[256,1152]{1,0:T(8,128)(2,1)}, bf16[256,1152]{1,0:T(8,128)(2,1)}, f...) custom-call(bf16[256,1152]{1,0:T(8,128)(2,1)} %copy-done.17, bf16[256,1152]{1,0:T(8,128)(2,1)} %copy-done.19, ...), custom_call_target="tpu_custom_call" | custom-call | flops 1000 | bytes 100 | tf_op jit(solution)/shard_map/feed_distant/pallas_call | solution.py:765
  181.1 15.9 %feed_weight.1 = (bf16[8,288,1152]{2,1,0:T(8,128)(2,1)}, f32[256,1152]{1,0:T(8,128)}, bf16[256,1152]{1,0:T(8,128)(2,1)}, bf16[256,1152]{1,0:T(8,128)(2,1)}, bf16[256,1152]{1,0:T(8,128)(2,1)}) custom-call(bf16[256,1152]{1,0:T(8,128)(2,1)} %get-tuple-element.140.refs_0_, bf16[256,1152]{1,0:T(8,128)(2,1)} %copy-done.16, bf16[256,1152]{1,0:T(8,128)(2,1)} %copy-done.17, ...), custom_call_target="tpu_custom_call" | custom-call | flops 1000 | bytes 100 | tf_op jit(solution)/shard_map/feed_weight/pallas_call | solution.py:765
  202.1 8.0 %proj_backward.1 = (f32[256,1152]{1,0:T(8,128)}, bf16[256,1152]{1,0:T(8,128)(2,1)}, bf16[256,1152]{1,0:T(8,128)(2,1)}, f32[2,3,1152]{2,1,0:T(4,128)}) custom-call(bf16[256,1152]{1,0:T(8,128)(2,1)} %bitcast.68, f32[2,6,1152]{2,1,0:T(8,128)} %copy-done.32, f32[256,1152]{1,0:T(8,128)} %get-tuple-element.129.refs_2_, ...), custom_call_target="tpu_custom_call" | custom-call | flops 1000 | bytes 100 | tf_op jit(solution)/shard_map/proj_backward/pallas_call | solution.py:765
  210.1 10.4 %attn_backward.1.refs_2_.refs_3_ = bf16[8,256,512]{2,1,0:T(8,128)(2,1)} custom-call(bf16[8,256,432]{2,1,0:T(8,128)(2,1)} %get-tuple-element.160.refs_0_, bf16[2,16,128,128]{3,2,1,0:T(8,128)(2,1)} %get-tuple-element.161.refs_1_, bf16[256,1152]{1,0:T(8,128)(2,1)} %get-tuple-element.162.refs_2_), custom_call_target="tpu_custom_call" | custom-call | flops 1000 | bytes 100 | tf_op jit(solution)/shard_map/attn_backward/pallas_call | solution.py:765
  221.6 4.4 %collective-permute-done.27.refs_4_ = bf16[1152,256]{1,0:T(8,128)(2,1)S(1)} collective-permute-done((bf16[1152,256]{1,0:T(8,128)(2,1)S(1)}, bf16[1152,256]{1,0:T(8,128)(2,1)S(1)}, u32[]{:S(2)}, u32[]{:S(2)}) %collective-permute-start.27) | collective-permute-done | bytes 589856 | tf_op jit(solution)/shard_map/ppermute | solution.py:787
  230.2 7.1 %attn_weight.2 = (bf16[2,144,1152]{2,1,0:T(8,128)(2,1)}, bf16[2,144,1152]{2,1,0:T(8,128)(2,1)}, bf16[2,144,1152]{2,1,0:T(8,128)(2,1)}, bf16[2,144,1152]{2,1,0:T(8,128)(2,1)}) custom-call(bf16[1152,256]{1,0:T(8,128)(2,1)} %get-tuple-element.169.refs_0_, bf16[1152,256]{1,0:T(8,128)(2,1)} %get-tuple-element.164.refs_1_, ...), custom_call_target="tpu_custom_call" | custom-call | flops 1000 | bytes 100 | tf_op jit(solution)/shard_map/attn_weight/pallas_call | solution.py:765
  243.3 7.0 %attn_weight.3 = (bf16[2,144,1152]{2,1,0:T(8,128)(2,1)}, bf16[2,144,1152]{2,1,0:T(8,128)(2,1)}, bf16[2,144,1152]{2,1,0:T(8,128)(2,1)}, bf16[2,144,1152]{2,1,0:T(8,128)(2,1)}) custom-call(bf16[1152,256]{1,0:T(8,128)(2,1)} %get-tuple-element.169.refs_0_, bf16[1152,256]{1,0:T(8,128)(2,1)} %get-tuple-element.164.refs_1_, ...), custom_call_target="tpu_custom_call" | custom-call | flops 1000 | bytes 100 | tf_op jit(solution)/shard_map/attn_weight/pallas_call | solution.py:765
  250.3 13.1 %qkv_backward.1 = (bf16[256,1152]{1,0:T(8,128)(2,1)}, f32[2,2,1152]{2,1,0:T(2,128)}) custom-call(bf16[256,1152]{1,0:T(8,128)(2,1)} %bitcast.73, f32[2,6,1152]{2,1,0:T(8,128)} %copy-done.32, f32[256,1152]{1,0:T(8,128)} %get-tuple-element.172.refs_2_, bf16[8,256,512]{2,1,0:T(8,128)(2,1)} %attn_backward.1.refs_2_.refs_3_, bf16[1,144,1152]{2,1,0:T(8,128)(2,1)} %bitcast.75, ...), custom_call_target="tpu_custom_call" | custom-call | flops 1000 | bytes 100 | tf_op jit(solution)/shard_map/qkv_backward/pallas_call | solution.py:765
  267.4 8.0 %all-to-all-start.3 = ((f32[32,16,128]{2,1,0:T(8,128)}), f32[32,16,128]{2,1,0:T(8,128)S(1)}, u32[]{:S(2)}, u32[]{:S(2)}) async-start(f32[32,16,128]{2,1,0:T(8,128)} %bitcast.33), calls=%async_computation.3 | async-start | bytes 524288 | tf_op jit(solution)/shard_map/all_to_all | solution.py:794
  279.0 22.5 %collective-permute-done.34 = bf16[2,144,1152]{2,1,0:T(8,128)(2,1)} collective-permute-done((bf16[2,144,1152]{2,1,0:T(8,128)(2,1)}, bf16[2,144,1152]{2,1,0:T(8,128)(2,1)}, u32[]{:S(2)}, u32[]{:S(2)}) %collective-permute-start.34) | collective-permute-done | bytes 663584 | tf_op jit(solution)/shard_map/ppermute | solution.py:787
  311.0 5.5 %collective-permute-start.42 = (bf16[144,1152]{1,0:T(8,128)(2,1)}, bf16[144,1152]{1,0:T(8,128)(2,1)}, u32[]{:S(2)}, u32[]{:S(2)}) collective-permute-start(bf16[144,1152]{1,0:T(8,128)(2,1)} %add_convert_fusion.2), channel_id=1, source_target_pairs={{0,16},{1,17},{2,18},{3,19},{4,20},{5,21},{6,22},{7,23},{8,24},{9,... | collective-permute-start | bytes 995336 | tf_op jit(solution)/shard_map/ppermute | solution.py:787
  319.8 3.6 %all-to-all-start.4 = ((bf16[4,2,144,288]{3,2,1,0:T(8,128)(2,1)}), bf16[4,2,144,288]{3,2,1,0:T(8,128)(2,1)S(1)}, u32[]{:S(2)}, u32[]{:S(2)}) async-start(bf16[4,2,144,288]{3,2,1,0:T(8,128)(2,1)} %bitcast.70), calls=%async_computation.5 | async-start | bytes 1769472 | tf_op jit(solution)/shard_map/all_to_all | solution.py:1065
  331.2 7.3 %collective-permute-done.42.refs_3_ = bf16[144,1152]{1,0:T(8,128)(2,1)} collective-permute-done((bf16[144,1152]{1,0:T(8,128)(2,1)}, bf16[144,1152]{1,0:T(8,128)(2,1)}, u32[]{:S(2)}, u32[]{:S(2)}) %collective-permute-start.42) | collective-permute-done | bytes 331808 | tf_op jit(solution)/shard_map/ppermute | solution.py:787
  338.4 4.7 %collective-permute-done.43.refs_4_ = bf16[144,1152]{1,0:T(8,128)(2,1)} collective-permute-done((bf16[144,1152]{1,0:T(8,128)(2,1)}, bf16[144,1152]{1,0:T(8,128)(2,1)}, u32[]{:S(2)}, u32[]{:S(2)}) %collective-permute-start.43) | collective-permute-done | bytes 331808 | tf_op jit(solution)/shard_map/ppermute | solution.py:787
  (241 shorter events, 100.3 us)
Async XLA Ops:
  13.0 33.4 %all-to-all-start = ((bf16[4,304,288]{1,2,0:T(8,128)(2,1)}), bf16[4,304,288]{1,2,0:T(8,128)(2,1)S(1)}, u32[]{:S(2)}, u32[]{:S(2)}) async-start(bf16[4,304,288]{1,2,0:T(8,128)(2,1)} %copy.28), calls=%async_computation | async-start | bytes 1769472 | tf_op jit(solution)/shard_map/all_to_all | solution.py:849
  17.3 131.9 %all-gather.2.cloned.1.call-start = ((), (), s32[]{:S(2)}) async-start(), calls=%async_computation.6 | async-start | bytes 5971968 | tf_op jit(solution)/shard_map/all_gather | solution.py:854
  50.3 32.8 %collective-permute-start.11 = (bf16[3,144,1152]{2,1,0:T(8,128)(2,1)S(1)}, bf16[3,144,1152]{2,1,0:T(8,128)(2,1)S(1)}, u32[]{:S(2)}, u32[]{:S(2)}) collective-permute-start(bf16[3,144,1152]{2,1,0:T(8,128)(2,1)S(1)} %constant_dynamic-update-slice_fusion.refs_6_.refs_7_), channel_id=1, source_target_pairs={{0,1},{1,0},{2,3},{3,2},{4,5},{5,4},{6,7},{7,6},{8,9},{9,8},{10,11... | collective-permute-start | bytes 2985992 | tf_op jit(solution)/shard_map/ppermute | solution.py:787
  50.4 32.7 %collective-permute-start.6 = (bf16[3,144,1152]{2,1,0:T(8,128)(2,1)S(1)}, bf16[3,144,1152]{2,1,0:T(8,128)(2,1)}, u32[]{:S(2)}, u32[]{:S(2)}) collective-permute-start(bf16[3,144,1152]{2,1,0:T(8,128)(2,1)S(1)} %constant_dynamic-update-slice_fusion.refs_6_.refs_7_), channel_id=1, source_target_pairs={{0,4},{1,5},{2,6},{3,7},{4,0},{5,1},{6,2},{7,3},{8,12},{9,13},{10,... | collective-permute-start | bytes 2985992 | tf_op jit(solution)/shard_map/ppermute | solution.py:787
  51.9 31.2 %collective-permute-start.7 = (bf16[3,144,1152]{2,1,0:T(8,128)(2,1)S(1)}, bf16[3,144,1152]{2,1,0:T(8,128)(2,1)}, u32[]{:S(2)}, u32[]{:S(2)}) collective-permute-start(bf16[3,144,1152]{2,1,0:T(8,128)(2,1)S(1)} %constant_dynamic-update-slice_fusion.refs_6_.refs_7_), channel_id=1, source_target_pairs={{0,2},{1,3},{2,0},{3,1},{4,6},{5,7},{6,4},{7,5},{8,10},{9,11},{10,... | collective-permute-start | bytes 2985992 | tf_op jit(solution)/shard_map/ppermute | solution.py:787
  53.8 29.3 %collective-permute-start.9 = (bf16[1,144,1152]{2,1,0:T(8,128)(2,1)S(1)}, bf16[1,144,1152]{2,1,0:T(8,128)(2,1)}, u32[]{:S(2)}, u32[]{:S(2)}) collective-permute-start(bf16[1,144,1152]{2,1,0:T(8,128)(2,1)S(1)} %collective-permute-done.3.refs_4_.refs_5_), channel_id=1, source_target_pairs={{0,1},{1,0},{2,3},{3,2},{4,5},{5,4},{6,7},{7,6},{8,9},{9,8},{10,11... | collective-permute-start | bytes 995336 | tf_op jit(solution)/shard_map/ppermute | solution.py:787
  56.6 26.5 %collective-permute-start.10 = (bf16[1,144,1152]{2,1,0:T(8,128)(2,1)}, bf16[1,144,1152]{2,1,0:T(8,128)(2,1)S(1)}, u32[]{:S(2)}, u32[]{:S(2)}) collective-permute-start(bf16[1,144,1152]{2,1,0:T(8,128)(2,1)} %collective-permute-done.4.refs_5_.refs_6_), channel_id=1, source_target_pairs={{0,1},{1,0},{2,3},{3,2},{4,5},{5,4},{6,7},{7,6},{8,9},{9,8},{10,11... | collective-permute-start | bytes 995336 | tf_op jit(solution)/shard_map/ppermute | solution.py:787
  83.1 33.9 %collective-permute-start.12 = (bf16[3,144,1152]{2,1,0:T(8,128)(2,1)}, bf16[3,144,1152]{2,1,0:T(8,128)(2,1)}, u32[]{:S(2)}, u32[]{:S(2)}) collective-permute-start(bf16[3,144,1152]{2,1,0:T(8,128)(2,1)} %collective-permute-done.6.refs_7_.refs_8_), channel_id=1, source_target_pairs={{0,2},{1,3},{2,0},{3,1},{4,6},{5,7},{6,4},{7,5},{8,10},{9,11},{10,... | collective-permute-start | bytes 2985992 | tf_op jit(solution)/shard_map/ppermute | solution.py:787
  85.0 32.0 %collective-permute-start.13 = (bf16[3,144,1152]{2,1,0:T(8,128)(2,1)}, bf16[3,144,1152]{2,1,0:T(8,128)(2,1)}, u32[]{:S(2)}, u32[]{:S(2)}) collective-permute-start(bf16[3,144,1152]{2,1,0:T(8,128)(2,1)} %collective-permute-done.6.refs_7_.refs_8_), channel_id=1, source_target_pairs={{0,1},{1,0},{2,3},{3,2},{4,5},{5,4},{6,7},{7,6},{8,9},{9,8},{10,11... | collective-permute-start | bytes 2985992 | tf_op jit(solution)/shard_map/ppermute | solution.py:787
  85.0 32.0 %collective-permute-start.14 = (bf16[3,144,1152]{2,1,0:T(8,128)(2,1)}, bf16[3,144,1152]{2,1,0:T(8,128)(2,1)}, u32[]{:S(2)}, u32[]{:S(2)}) collective-permute-start(bf16[3,144,1152]{2,1,0:T(8,128)(2,1)} %collective-permute-done.7.refs_8_.refs_9_), channel_id=1, source_target_pairs={{0,1},{1,0},{2,3},{3,2},{4,5},{5,4},{6,7},{7,6},{8,9},{9,8},{10,11... | collective-permute-start | bytes 2985992 | tf_op jit(solution)/shard_map/ppermute | solution.py:787
  98.7 217.7 %reduce-scatter.2.cloned.1.call-start = ((), (), s32[]{:S(2)}) async-start(), calls=%async_computation.7 | async-start | bytes 5971968 | tf_op jit(solution)/shard_map/reduce_scatter | solution.py:987
  118.3 27.1 %collective-permute-start.19 = (bf16[256,1152]{1,0:T(8,128)(2,1)S(1)}, bf16[256,1152]{1,0:T(8,128)(2,1)S(1)}, u32[]{:S(2)}, u32[]{:S(2)}) collective-permute-start(bf16[256,1152]{1,0:T(8,128)(2,1)S(1)} %fusion.refs_2_.refs_4_), channel_id=1, source_target_pairs={{0,1},{1,0},{2,3},{3,2},{4,5},{5,4},{6,7},{7,6},{8,9},{9,8},{10,11... | collective-permute-start | bytes 1769480 | tf_op jit(solution)/shard_map/ppermute | solution.py:787
  118.4 26.8 %collective-permute-start.21 = (bf16[256,1152]{1,0:T(8,128)(2,1)S(1)}, bf16[256,1152]{1,0:T(8,128)(2,1)S(1)}, u32[]{:S(2)}, u32[]{:S(2)}) collective-permute-start(bf16[256,1152]{1,0:T(8,128)(2,1)S(1)} %fusion.refs_2_.refs_4_), channel_id=1, source_target_pairs={{0,2},{1,3},{2,0},{3,1},{4,6},{5,7},{6,4},{7,5},{8,10},{9,11},{10,... | collective-permute-start | bytes 1769480 | tf_op jit(solution)/shard_map/ppermute | solution.py:787
  237.3 38.1 %collective-permute-start.33 = (bf16[2,144,1152]{2,1,0:T(8,128)(2,1)}, bf16[2,144,1152]{2,1,0:T(8,128)(2,1)}, u32[]{:S(2)}, u32[]{:S(2)}) collective-permute-start(bf16[2,144,1152]{2,1,0:T(8,128)(2,1)} %get-tuple-element.176), channel_id=1, source_target_pairs={{0,2},{1,3},{2,0},{3,1},{4,6},{5,7},{6,4},{7,5},{8,10},{9,11},{10,... | collective-permute-start | bytes 1990664 | tf_op jit(solution)/shard_map/ppermute | solution.py:787
  237.8 40.7 %collective-permute-start.35 = (bf16[2,144,1152]{2,1,0:T(8,128)(2,1)}, bf16[2,144,1152]{2,1,0:T(8,128)(2,1)S(1)}, u32[]{:S(2)}, u32[]{:S(2)}) collective-permute-start(bf16[2,144,1152]{2,1,0:T(8,128)(2,1)} %get-tuple-element.181), channel_id=1, source_target_pairs={{0,2},{1,3},{2,0},{3,1},{4,6},{5,7},{6,4},{7,5},{8,10},{9,11},{10,... | collective-permute-start | bytes 1990664 | tf_op jit(solution)/shard_map/ppermute | solution.py:787
  264.2 43.2 %collective-permute-start.37 = (bf16[2,144,1152]{2,1,0:T(8,128)(2,1)}, bf16[2,144,1152]{2,1,0:T(8,128)(2,1)}, u32[]{:S(2)}, u32[]{:S(2)}) collective-permute-start(bf16[2,144,1152]{2,1,0:T(8,128)(2,1)} %get-tuple-element.184), channel_id=1, source_target_pairs={{0,2},{1,3},{2,0},{3,1},{4,6},{5,7},{6,4},{7,5},{8,10},{9,11},{10,... | collective-permute-start | bytes 1990664 | tf_op jit(solution)/shard_map/ppermute | solution.py:787
  264.8 36.7 %collective-permute-start.34 = (bf16[2,144,1152]{2,1,0:T(8,128)(2,1)}, bf16[2,144,1152]{2,1,0:T(8,128)(2,1)}, u32[]{:S(2)}, u32[]{:S(2)}) collective-permute-start(bf16[2,144,1152]{2,1,0:T(8,128)(2,1)} %get-tuple-element.179), channel_id=1, source_target_pairs={{0,2},{1,3},{2,0},{3,1},{4,6},{5,7},{6,4},{7,5},{8,10},{9,11},{10,... | collective-permute-start | bytes 1990664 | tf_op jit(solution)/shard_map/ppermute | solution.py:787
  267.4 52.4 %all-to-all-start.3 = ((f32[32,16,128]{2,1,0:T(8,128)}), f32[32,16,128]{2,1,0:T(8,128)S(1)}, u32[]{:S(2)}, u32[]{:S(2)}) async-start(f32[32,16,128]{2,1,0:T(8,128)} %bitcast.33), calls=%async_computation.3 | async-start | bytes 524288 | tf_op jit(solution)/shard_map/all_to_all | solution.py:794
  276.7 28.5 %collective-permute-start.36 = (bf16[144,1152]{1,0:T(8,128)(2,1)S(1)}, bf16[144,1152]{1,0:T(8,128)(2,1)S(1)}, u32[]{:S(2)}, u32[]{:S(2)}) collective-permute-start(bf16[144,1152]{1,0:T(8,128)(2,1)S(1)} %get-tuple-element.202), channel_id=1, source_target_pairs={{0,4},{1,5},{2,6},{3,7},{4,0},{5,1},{6,2},{7,3},{8,12},{9,13},{10,... | collective-permute-start | bytes 995336 | tf_op jit(solution)/shard_map/ppermute | solution.py:787
  278.7 31.4 %collective-permute-start.41 = (bf16[144,1152]{1,0:T(8,128)(2,1)S(1)}, bf16[144,1152]{1,0:T(8,128)(2,1)S(1)}, u32[]{:S(2)}, u32[]{:S(2)}) collective-permute-start(bf16[144,1152]{1,0:T(8,128)(2,1)S(1)} %get-tuple-element.196), channel_id=1, source_target_pairs={{0,4},{1,5},{2,6},{3,7},{4,0},{5,1},{6,2},{7,3},{8,12},{9,13},{10,... | collective-permute-start | bytes 995336 | tf_op jit(solution)/shard_map/ppermute | solution.py:787
  303.7 27.5 %collective-permute-start.39 = (bf16[144,1152]{1,0:T(8,128)(2,1)}, bf16[144,1152]{1,0:T(8,128)(2,1)}, u32[]{:S(2)}, u32[]{:S(2)}) collective-permute-start(bf16[144,1152]{1,0:T(8,128)(2,1)} %get-tuple-element.199), channel_id=1, source_target_pairs={{0,4},{1,5},{2,6},{3,7},{4,0},{5,1},{6,2},{7,3},{8,12},{9,13},{10,... | collective-permute-start | bytes 995336 | tf_op jit(solution)/shard_map/ppermute | solution.py:787
  306.0 32.5 %collective-permute-start.40 = (bf16[144,1152]{1,0:T(8,128)(2,1)}, bf16[144,1152]{1,0:T(8,128)(2,1)}, u32[]{:S(2)}, u32[]{:S(2)}) collective-permute-start(bf16[144,1152]{1,0:T(8,128)(2,1)} %add_convert_fusion.6), channel_id=1, source_target_pairs={{0,24},{1,25},{2,26},{3,27},{4,28},{5,29},{6,30},{7,31},{8,16},{9,... | collective-permute-start | bytes 995336 | tf_op jit(solution)/shard_map/ppermute | solution.py:787
  311.0 27.5 %collective-permute-start.42 = (bf16[144,1152]{1,0:T(8,128)(2,1)}, bf16[144,1152]{1,0:T(8,128)(2,1)}, u32[]{:S(2)}, u32[]{:S(2)}) collective-permute-start(bf16[144,1152]{1,0:T(8,128)(2,1)} %add_convert_fusion.2), channel_id=1, source_target_pairs={{0,16},{1,17},{2,18},{3,19},{4,20},{5,21},{6,22},{7,23},{8,24},{9,... | collective-permute-start | bytes 995336 | tf_op jit(solution)/shard_map/ppermute | solution.py:787
  319.8 26.1 %all-to-all-start.4 = ((bf16[4,2,144,288]{3,2,1,0:T(8,128)(2,1)}), bf16[4,2,144,288]{3,2,1,0:T(8,128)(2,1)S(1)}, u32[]{:S(2)}, u32[]{:S(2)}) async-start(bf16[4,2,144,288]{3,2,1,0:T(8,128)(2,1)} %bitcast.70), calls=%async_computation.5 | async-start | bytes 1769472 | tf_op jit(solution)/shard_map/all_to_all | solution.py:1065
  (75 other events, 697.8 us)
Sparse Core Ops, SparseCore 0:
  49.2 99.9 all-gather.1
  197.2 112.8 reduce-scatter.1

commit v5 on v4

--- a/solution.py
+++ b/solution.py
@@ -1057,14 +1057,22 @@
     d_mod_all = padded_exchange(mod_send, count).reshape(count * clips, ada_cols)
     split_sum(3)
     line.token, d_mod_all = lax.optimization_barrier((line.token, d_mod_all))
-    for index in (2, 1):
-        split_sum(index)
-        attn_sum(index + 1)
+    split_sum(2)
+    attn_sum(3)
+    attn_sum(2)
+    split_sum(1)
     back = feed_sum.reshape(2, sub, row_parts, height).transpose(2, 0, 1, 3)
     line.token, back = lax.optimization_barrier((line.token, back))
     back = lax.all_to_all(back, "fsdp", 0, 0, tiled=True)
     split_sum(0)
     attn_sum(1)
+    up_grad, down_grad_t = line.call(
+        feed_finish_kernel,
+        (shape_of(up_weight.shape, F32), shape_of(down_weight.shape[::-1], F32)),
+        (back,),
+        "feed_finish",
+    )
+    down_grad = down_grad_t.T
     qkv_grad, proj_grad_t = line.call(
         functools.partial(attn_finish_kernel, packing),
         (shape_of((height, qkv_cols), F32), shape_of((proj_cols, height), F32)),
@@ -1072,13 +1080,6 @@
         "attn_finish",
     )
     proj_grad = proj_grad_t.T
-    up_grad, down_grad_t = line.call(
-        feed_finish_kernel,
-        (shape_of(up_weight.shape, F32), shape_of(down_weight.shape[::-1], F32)),
-        (back,),
-        "feed_finish",
-    )
-    down_grad = down_grad_t.T
 
     ada_grad = lax.dot_general(
         cond_all.astype(F32),

time: 362 us -> 356 us (0.983)
  starting transfers between devices: 67.8 us -> 62.6 us
    ppermute x44, waiting for transfers between devices: 72.6 us -> 65.3 us  [swap(): return lax.ppermute(value, AXES, [(i, i ^ mask) for i in range(count)])]
    all_to_all x1, waiting for transfers between devices: 0.01 us -> 7.06 us  [fast_body(): back = lax.all_to_all(back, 'fsdp', 0, 0, tiled=True)]
    ppermute x44, starting transfers between devices: 42.7 us -> 37.5 us  [swap(): return lax.ppermute(value, AXES, [(i, i ^ mask) for i in range(count)])]
  transfers between devices with their start and end apart: 50 -> 50, of which waited for: 18 -> 19; matrix products, arithmetic and copies ran while one was open for 7% -> 7% of each run, Pallas kernels for 28% -> 29%
where the time goes in v5:
time: 356 us; the launch traced here: 351 us
  Pallas kernels  119 us (33%)
  waiting for transfers between devices  90.3 us (25%)
  starting transfers between devices  62.6 us (18%)
  local copies, waits for them, and re-layouts  24.9 us (7%)
  blocking collectives  24.3 us (7%)
  between operations  15 us (4%)
  other arithmetic  14.3 us (4%)
    pallas_call x13, Pallas kernels, call(): pl.pallas_call(kernel, out_shape=shapes, in_specs=specs or [VMEM_SPEC] *...  119 us
    ppermute x44, waiting for transfers between devices, swap(): return lax.ppermute(value, AXES, [(i, i ^ mask) for i in range(count)])  65.3 us
    ppermute x44, starting transfers between devices, swap(): return lax.ppermute(value, AXES, [(i, i ^ mask) for i in range(count)])  37.5 us
    all_to_all x1, blocking collectives, fast_body(): conds = lax.all_to_all(conds, 'dp', 0, 0, tiled=True)  24.3 us
    all_to_all x2, starting transfers between devices, padded_exchange(): got = lax.all_to_all(rows, AXES, 0, 0, tiled=True)  16.8 us
    all_to_all x2, waiting for transfers between devices, padded_exchange(): got = lax.all_to_all(rows, AXES, 0, 0, tiled=True)  14.3 us
    unnamed x107, local copies, waits for them, and re-layouts  12.7 us
  transfers between devices with their start and end apart: 50, of which 19 were waited for; matrix products, arithmetic and copies ran while one was open for 7% of the time, Pallas kernels for 29%

profile of v5, /device:TPU:0, one launch (start us, length us, event | category | flops | bytes accessed | tf_op | source)
XLA Modules:
  0.0 351.5 jit_solution(6228247901353347292)
XLA Ops:
  7.2 3.6 %prepare.1 = (bf16[144,1152]{1,0:T(8,128)(2,1)}, bf16[4,304,288]{2,1,0:T(8,128)(2,1)}) custom-call(s32[2]{0:T(128)} %refs_0_.2, s32[2]{0:T(128)} %refs_1_.1, bf16[1000,1152]{1,0:T(8,128)(2,1)} %refs_2_.1, bf16[101,1152]{1,0:T(8,128)(2,1)} %refs_3_.1, bf16[288,432]{1,0:T(8,128)(2,1)} %refs_4_.1, bf16[144,288]{1,0:T(8,128)(2,1)} %bitcast.91, ...), custom_call_target="tpu_custom_call" | custom-call | flops 1000 | bytes 100 | tf_op jit(solution)/shard_map/prepare/pallas_call | solution.py:765
  13.0 4.4 %all-to-all-start = ((bf16[4,304,288]{1,2,0:T(8,128)(2,1)}), bf16[4,304,288]{1,2,0:T(8,128)(2,1)S(1)}, u32[]{:S(2)}, u32[]{:S(2)}) async-start(bf16[4,304,288]{1,2,0:T(8,128)(2,1)} %copy.28), calls=%async_computation | async-start | bytes 1769472 | tf_op jit(solution)/shard_map/all_to_all | solution.py:849
  25.9 8.7 %collective-permute-done = bf16[1,144,1152]{2,1,0:T(8,128)(2,1)S(1)} collective-permute-done((bf16[1,144,1152]{2,1,0:T(8,128)(2,1)S(1)}, bf16[1,144,1152]{2,1,0:T(8,128)(2,1)S(1)}, u32[]{:S(2)}, u32[]{:S(2)}) %collective-permute-start) | collective-permute-done | bytes 331808 | tf_op jit(solution)/shard_map/ppermute | solution.py:787
  34.7 10.9 %collective-permute-done.1 = bf16[1,144,1152]{2,1,0:T(8,128)(2,1)S(1)} collective-permute-done((bf16[1,144,1152]{2,1,0:T(8,128)(2,1)S(1)}, bf16[1,144,1152]{2,1,0:T(8,128)(2,1)S(1)}, u32[]{:S(2)}, u32[]{:S(2)}) %collective-permute-start.1) | collective-permute-done | bytes 331808 | tf_op jit(solution)/shard_map/ppermute | solution.py:787
  58.8 24.3 %all_to_all.25.conds = bf16[8,16,384]{2,1,0:T(8,128)(2,1)} all-to-all(bf16[8,16,384]{2,1,0:T(8,128)(2,1)S(1)} %broadcast_in_dim.20), channel_id=1, replica_groups=mesh['dp'=8,'fsdp'=4] {'dp'}, dimensions={0} | all-to-all | bytes 196608 | tf_op jit(solution)/shard_map/all_to_all | solution.py:860
  89.9 8.8 %all-to-all-start.2 = ((f32[32,16,128]{2,1,0:T(8,128)}), f32[32,16,128]{2,1,0:T(8,128)S(1)}, u32[]{:S(2)}, u32[]{:S(2)}) async-start(f32[32,16,128]{2,1,0:T(8,128)} %bitcast.84), calls=%async_computation.2 | async-start | bytes 524288 | tf_op jit(solution)/shard_map/all_to_all | solution.py:794
  100.9 14.3 %all-to-all-done.2 = f32[32,16,128]{2,1,0:T(8,128)S(1)} async-done(((f32[32,16,128]{2,1,0:T(8,128)}), f32[32,16,128]{2,1,0:T(8,128)S(1)}, u32[]{:S(2)}, u32[]{:S(2)}) %all-to-all-start.2) | async-done | bytes 262176 | tf_op jit(solution)/shard_map/all_to_all | solution.py:794
  121.6 21.7 %attn_forward.1 = (bf16[1152,256]{1,0:T(8,128)(2,1)}, bf16[8,256,432]{2,1,0:T(8,128)(2,1)}, bf16[2,16,128,128]{3,2,1,0:T(8,128)(2,1)}, bf16[1152,256]{1,0:T(8,12...) custom-call(s32[2]{0:T(128)} %refs_0_.3, ...), custom_call_target="tpu_custom_call" | custom-call | flops 1000 | bytes 100 | tf_op jit(solution)/shard_map/attn_forward/pallas_call | solution.py:765
  145.6 3.7 %all-gather.2.cloned.1.call-done.refs_4_.refs_16_ = bf16[2304,1152]{1,0:T(8,128)(2,1)} async-done(((bf16[288,1152]{1,0:T(8,128)(2,1)}), bf16[2304,1152]{1,0:T(8,128)(2,1)}) %all-gather.2.cloned.1.call-update) | async-done | bytes 5308432 | tf_op jit(solution)/shard_map/all_gather | solution.py:854
  149.2 11.8 %feed_near.1 = (bf16[256,1152]{1,0:T(8,128)(2,1)}, bf16[256,1152]{1,0:T(8,128)(2,1)}, bf16[256,1152]{1,0:T(8,128)(2,1)}, bf16[256,1152]{1,0:T(8,128)(2,1)}, f32[...) custom-call(bf16[256,1152]{1,0:T(8,128)(2,1)} %get-tuple-element.140.refs_0_, bf16[256,1152]{1,0:T(8,128)(2,1)} %copy-done.16, ...), custom_call_target="tpu_custom_call" | custom-call | flops 1000 | bytes 100 | tf_op jit(solution)/shard_map/feed_near/pallas_call | solution.py:765
  164.0 11.9 %feed_distant.1 = (bf16[256,1152]{1,0:T(8,128)(2,1)}, bf16[256,1152]{1,0:T(8,128)(2,1)}, bf16[256,1152]{1,0:T(8,128)(2,1)}, bf16[256,1152]{1,0:T(8,128)(2,1)}, f...) custom-call(bf16[256,1152]{1,0:T(8,128)(2,1)} %copy-done.17, bf16[256,1152]{1,0:T(8,128)(2,1)} %copy-done.19, ...), custom_call_target="tpu_custom_call" | custom-call | flops 1000 | bytes 100 | tf_op jit(solution)/shard_map/feed_distant/pallas_call | solution.py:765
  181.1 15.9 %feed_weight.1 = (bf16[8,288,1152]{2,1,0:T(8,128)(2,1)}, f32[256,1152]{1,0:T(8,128)}, bf16[256,1152]{1,0:T(8,128)(2,1)}, bf16[256,1152]{1,0:T(8,128)(2,1)}, bf16[256,1152]{1,0:T(8,128)(2,1)}) custom-call(bf16[256,1152]{1,0:T(8,128)(2,1)} %get-tuple-element.140.refs_0_, bf16[256,1152]{1,0:T(8,128)(2,1)} %copy-done.16, bf16[256,1152]{1,0:T(8,128)(2,1)} %copy-done.17, ...), custom_call_target="tpu_custom_call" | custom-call | flops 1000 | bytes 100 | tf_op jit(solution)/shard_map/feed_weight/pallas_call | solution.py:765
  202.1 8.0 %proj_backward.1 = (f32[256,1152]{1,0:T(8,128)}, bf16[256,1152]{1,0:T(8,128)(2,1)}, bf16[256,1152]{1,0:T(8,128)(2,1)}, f32[2,3,1152]{2,1,0:T(4,128)}) custom-call(bf16[256,1152]{1,0:T(8,128)(2,1)} %bitcast.68, f32[2,6,1152]{2,1,0:T(8,128)} %copy-done.32, f32[256,1152]{1,0:T(8,128)} %get-tuple-element.129.refs_2_, ...), custom_call_target="tpu_custom_call" | custom-call | flops 1000 | bytes 100 | tf_op jit(solution)/shard_map/proj_backward/pallas_call | solution.py:765
  210.1 10.4 %attn_backward.1.refs_2_.refs_3_ = bf16[8,256,512]{2,1,0:T(8,128)(2,1)} custom-call(bf16[8,256,432]{2,1,0:T(8,128)(2,1)} %get-tuple-element.160.refs_0_, bf16[2,16,128,128]{3,2,1,0:T(8,128)(2,1)} %get-tuple-element.161.refs_1_, bf16[256,1152]{1,0:T(8,128)(2,1)} %get-tuple-element.162.refs_2_), custom_call_target="tpu_custom_call" | custom-call | flops 1000 | bytes 100 | tf_op jit(solution)/shard_map/attn_backward/pallas_call | solution.py:765
  221.6 4.4 %collective-permute-done.27.refs_4_ = bf16[1152,256]{1,0:T(8,128)(2,1)S(1)} collective-permute-done((bf16[1152,256]{1,0:T(8,128)(2,1)S(1)}, bf16[1152,256]{1,0:T(8,128)(2,1)S(1)}, u32[]{:S(2)}, u32[]{:S(2)}) %collective-permute-start.27) | collective-permute-done | bytes 589856 | tf_op jit(solution)/shard_map/ppermute | solution.py:787
  230.2 7.2 %attn_weight.2 = (bf16[2,144,1152]{2,1,0:T(8,128)(2,1)}, bf16[2,144,1152]{2,1,0:T(8,128)(2,1)}, bf16[2,144,1152]{2,1,0:T(8,128)(2,1)}, bf16[2,144,1152]{2,1,0:T(8,128)(2,1)}) custom-call(bf16[1152,256]{1,0:T(8,128)(2,1)} %get-tuple-element.169.refs_0_, bf16[1152,256]{1,0:T(8,128)(2,1)} %get-tuple-element.164.refs_1_, ...), custom_call_target="tpu_custom_call" | custom-call | flops 1000 | bytes 100 | tf_op jit(solution)/shard_map/attn_weight/pallas_call | solution.py:765
  243.3 7.0 %attn_weight.3 = (bf16[2,144,1152]{2,1,0:T(8,128)(2,1)}, bf16[2,144,1152]{2,1,0:T(8,128)(2,1)}, bf16[2,144,1152]{2,1,0:T(8,128)(2,1)}, bf16[2,144,1152]{2,1,0:T(8,128)(2,1)}) custom-call(bf16[1152,256]{1,0:T(8,128)(2,1)} %get-tuple-element.169.refs_0_, bf16[1152,256]{1,0:T(8,128)(2,1)} %get-tuple-element.164.refs_1_, ...), custom_call_target="tpu_custom_call" | custom-call | flops 1000 | bytes 100 | tf_op jit(solution)/shard_map/attn_weight/pallas_call | solution.py:765
  250.3 13.1 %qkv_backward.1 = (bf16[256,1152]{1,0:T(8,128)(2,1)}, f32[2,2,1152]{2,1,0:T(2,128)}) custom-call(bf16[256,1152]{1,0:T(8,128)(2,1)} %bitcast.73, f32[2,6,1152]{2,1,0:T(8,128)} %copy-done.32, f32[256,1152]{1,0:T(8,128)} %get-tuple-element.172.refs_2_, bf16[8,256,512]{2,1,0:T(8,128)(2,1)} %attn_backward.1.refs_2_.refs_3_, bf16[1,144,1152]{2,1,0:T(8,128)(2,1)} %bitcast.75, ...), custom_call_target="tpu_custom_call" | custom-call | flops 1000 | bytes 100 | tf_op jit(solution)/shard_map/qkv_backward/pallas_call | solution.py:765
  267.4 8.0 %all-to-all-start.3 = ((f32[32,16,128]{2,1,0:T(8,128)}), f32[32,16,128]{2,1,0:T(8,128)S(1)}, u32[]{:S(2)}, u32[]{:S(2)}) async-start(f32[32,16,128]{2,1,0:T(8,128)} %bitcast.33), calls=%async_computation.3 | async-start | bytes 524288 | tf_op jit(solution)/shard_map/all_to_all | solution.py:794
  279.0 16.6 %collective-permute-done.36 = bf16[144,1152]{1,0:T(8,128)(2,1)S(1)} collective-permute-done((bf16[144,1152]{1,0:T(8,128)(2,1)S(1)}, bf16[144,1152]{1,0:T(8,128)(2,1)S(1)}, u32[]{:S(2)}, u32[]{:S(2)}) %collective-permute-start.36) | collective-permute-done | bytes 331808 | tf_op jit(solution)/shard_map/ppermute | solution.py:787
  296.4 6.4 %collective-permute-done.37 = bf16[144,1152]{1,0:T(8,128)(2,1)S(1)} collective-permute-done((bf16[144,1152]{1,0:T(8,128)(2,1)S(1)}, bf16[144,1152]{1,0:T(8,128)(2,1)S(1)}, u32[]{:S(2)}, u32[]{:S(2)}) %collective-permute-start.37) | collective-permute-done | bytes 331808 | tf_op jit(solution)/shard_map/ppermute | solution.py:787
  317.3 3.6 %all-to-all-start.4 = ((bf16[4,2,144,288]{3,2,1,0:T(8,128)(2,1)}), bf16[4,2,144,288]{3,2,1,0:T(8,128)(2,1)S(1)}, u32[]{:S(2)}, u32[]{:S(2)}) async-start(bf16[4,2,144,288]{3,2,1,0:T(8,128)(2,1)} %bitcast.70), calls=%async_computation.5 | async-start | bytes 1769472 | tf_op jit(solution)/shard_map/all_to_all | solution.py:1066
  326.5 7.1 %all-to-all-done.4.back = bf16[4,2,144,288]{3,2,1,0:T(8,128)(2,1)S(1)} async-done(((bf16[4,2,144,288]{3,2,1,0:T(8,128)(2,1)}), bf16[4,2,144,288]{3,2,1,0:T(8,128)(2,1)S(1)}, u32[]{:S(2)}, u32[]{:S(2)}) %all-to-all-start.4) | async-done | bytes 663584 | tf_op jit(solution)/shard_map/all_to_all | solution.py:1066
  337.3 4.3 %collective-permute-done.43.refs_4_ = bf16[144,1152]{1,0:T(8,128)(2,1)} collective-permute-done((bf16[144,1152]{1,0:T(8,128)(2,1)}, bf16[144,1152]{1,0:T(8,128)(2,1)}, u32[]{:S(2)}, u32[]{:S(2)}) %collective-permute-start.43) | collective-permute-done | bytes 331808 | tf_op jit(solution)/shard_map/ppermute | solution.py:787
  (241 shorter events, 100.6 us)
Async XLA Ops:
  13.0 33.4 %all-to-all-start = ((bf16[4,304,288]{1,2,0:T(8,128)(2,1)}), bf16[4,304,288]{1,2,0:T(8,128)(2,1)S(1)}, u32[]{:S(2)}, u32[]{:S(2)}) async-start(bf16[4,304,288]{1,2,0:T(8,128)(2,1)} %copy.28), calls=%async_computation | async-start | bytes 1769472 | tf_op jit(solution)/shard_map/all_to_all | solution.py:849
  17.3 131.9 %all-gather.2.cloned.1.call-start = ((), (), s32[]{:S(2)}) async-start(), calls=%async_computation.6 | async-start | bytes 5971968 | tf_op jit(solution)/shard_map/all_gather | solution.py:854
  19.8 25.8 %collective-permute-start.1 = (bf16[1,144,1152]{2,1,0:T(8,128)(2,1)S(1)}, bf16[1,144,1152]{2,1,0:T(8,128)(2,1)S(1)}, u32[]{:S(2)}, u32[]{:S(2)}) collective-permute-start(bf16[1,144,1152]{2,1,0:T(8,128)(2,1)S(1)} %bitcast.77), channel_id=1, source_target_pairs={{0,16},{1,17},{2,18},{3,19},{4,20},{5,21},{6,22},{7,23},{8,24},{9,... | collective-permute-start | bytes 995336 | tf_op jit(solution)/shard_map/ppermute | solution.py:787
  50.3 32.8 %collective-permute-start.11 = (bf16[3,144,1152]{2,1,0:T(8,128)(2,1)S(1)}, bf16[3,144,1152]{2,1,0:T(8,128)(2,1)S(1)}, u32[]{:S(2)}, u32[]{:S(2)}) collective-permute-start(bf16[3,144,1152]{2,1,0:T(8,128)(2,1)S(1)} %constant_dynamic-update-slice_fusion.refs_6_.refs_7_), channel_id=1, source_target_pairs={{0,1},{1,0},{2,3},{3,2},{4,5},{5,4},{6,7},{7,6},{8,9},{9,8},{10,11... | collective-permute-start | bytes 2985992 | tf_op jit(solution)/shard_map/ppermute | solution.py:787
  50.4 32.7 %collective-permute-start.6 = (bf16[3,144,1152]{2,1,0:T(8,128)(2,1)S(1)}, bf16[3,144,1152]{2,1,0:T(8,128)(2,1)}, u32[]{:S(2)}, u32[]{:S(2)}) collective-permute-start(bf16[3,144,1152]{2,1,0:T(8,128)(2,1)S(1)} %constant_dynamic-update-slice_fusion.refs_6_.refs_7_), channel_id=1, source_target_pairs={{0,4},{1,5},{2,6},{3,7},{4,0},{5,1},{6,2},{7,3},{8,12},{9,13},{10,... | collective-permute-start | bytes 2985992 | tf_op jit(solution)/shard_map/ppermute | solution.py:787
  51.9 31.2 %collective-permute-start.7 = (bf16[3,144,1152]{2,1,0:T(8,128)(2,1)S(1)}, bf16[3,144,1152]{2,1,0:T(8,128)(2,1)}, u32[]{:S(2)}, u32[]{:S(2)}) collective-permute-start(bf16[3,144,1152]{2,1,0:T(8,128)(2,1)S(1)} %constant_dynamic-update-slice_fusion.refs_6_.refs_7_), channel_id=1, source_target_pairs={{0,2},{1,3},{2,0},{3,1},{4,6},{5,7},{6,4},{7,5},{8,10},{9,11},{10,... | collective-permute-start | bytes 2985992 | tf_op jit(solution)/shard_map/ppermute | solution.py:787
  53.8 29.3 %collective-permute-start.9 = (bf16[1,144,1152]{2,1,0:T(8,128)(2,1)S(1)}, bf16[1,144,1152]{2,1,0:T(8,128)(2,1)}, u32[]{:S(2)}, u32[]{:S(2)}) collective-permute-start(bf16[1,144,1152]{2,1,0:T(8,128)(2,1)S(1)} %collective-permute-done.3.refs_4_.refs_5_), channel_id=1, source_target_pairs={{0,1},{1,0},{2,3},{3,2},{4,5},{5,4},{6,7},{7,6},{8,9},{9,8},{10,11... | collective-permute-start | bytes 995336 | tf_op jit(solution)/shard_map/ppermute | solution.py:787
  56.6 26.5 %collective-permute-start.10 = (bf16[1,144,1152]{2,1,0:T(8,128)(2,1)}, bf16[1,144,1152]{2,1,0:T(8,128)(2,1)S(1)}, u32[]{:S(2)}, u32[]{:S(2)}) collective-permute-start(bf16[1,144,1152]{2,1,0:T(8,128)(2,1)} %collective-permute-done.4.refs_5_.refs_6_), channel_id=1, source_target_pairs={{0,1},{1,0},{2,3},{3,2},{4,5},{5,4},{6,7},{7,6},{8,9},{9,8},{10,11... | collective-permute-start | bytes 995336 | tf_op jit(solution)/shard_map/ppermute | solution.py:787
  83.1 33.9 %collective-permute-start.12 = (bf16[3,144,1152]{2,1,0:T(8,128)(2,1)}, bf16[3,144,1152]{2,1,0:T(8,128)(2,1)}, u32[]{:S(2)}, u32[]{:S(2)}) collective-permute-start(bf16[3,144,1152]{2,1,0:T(8,128)(2,1)} %collective-permute-done.6.refs_7_.refs_8_), channel_id=1, source_target_pairs={{0,2},{1,3},{2,0},{3,1},{4,6},{5,7},{6,4},{7,5},{8,10},{9,11},{10,... | collective-permute-start | bytes 2985992 | tf_op jit(solution)/shard_map/ppermute | solution.py:787
  85.0 32.0 %collective-permute-start.13 = (bf16[3,144,1152]{2,1,0:T(8,128)(2,1)}, bf16[3,144,1152]{2,1,0:T(8,128)(2,1)}, u32[]{:S(2)}, u32[]{:S(2)}) collective-permute-start(bf16[3,144,1152]{2,1,0:T(8,128)(2,1)} %collective-permute-done.6.refs_7_.refs_8_), channel_id=1, source_target_pairs={{0,1},{1,0},{2,3},{3,2},{4,5},{5,4},{6,7},{7,6},{8,9},{9,8},{10,11... | collective-permute-start | bytes 2985992 | tf_op jit(solution)/shard_map/ppermute | solution.py:787
  85.0 32.0 %collective-permute-start.14 = (bf16[3,144,1152]{2,1,0:T(8,128)(2,1)}, bf16[3,144,1152]{2,1,0:T(8,128)(2,1)}, u32[]{:S(2)}, u32[]{:S(2)}) collective-permute-start(bf16[3,144,1152]{2,1,0:T(8,128)(2,1)} %collective-permute-done.7.refs_8_.refs_9_), channel_id=1, source_target_pairs={{0,1},{1,0},{2,3},{3,2},{4,5},{5,4},{6,7},{7,6},{8,9},{9,8},{10,11... | collective-permute-start | bytes 2985992 | tf_op jit(solution)/shard_map/ppermute | solution.py:787
  89.9 25.3 %all-to-all-start.2 = ((f32[32,16,128]{2,1,0:T(8,128)}), f32[32,16,128]{2,1,0:T(8,128)S(1)}, u32[]{:S(2)}, u32[]{:S(2)}) async-start(f32[32,16,128]{2,1,0:T(8,128)} %bitcast.84), calls=%async_computation.2 | async-start | bytes 524288 | tf_op jit(solution)/shard_map/all_to_all | solution.py:794
  98.7 215.2 %reduce-scatter.2.cloned.1.call-start = ((), (), s32[]{:S(2)}) async-start(), calls=%async_computation.7 | async-start | bytes 5971968 | tf_op jit(solution)/shard_map/reduce_scatter | solution.py:987
  118.3 27.1 %collective-permute-start.19 = (bf16[256,1152]{1,0:T(8,128)(2,1)S(1)}, bf16[256,1152]{1,0:T(8,128)(2,1)S(1)}, u32[]{:S(2)}, u32[]{:S(2)}) collective-permute-start(bf16[256,1152]{1,0:T(8,128)(2,1)S(1)} %fusion.refs_2_.refs_4_), channel_id=1, source_target_pairs={{0,1},{1,0},{2,3},{3,2},{4,5},{5,4},{6,7},{7,6},{8,9},{9,8},{10,11... | collective-permute-start | bytes 1769480 | tf_op jit(solution)/shard_map/ppermute | solution.py:787
  118.4 26.8 %collective-permute-start.21 = (bf16[256,1152]{1,0:T(8,128)(2,1)S(1)}, bf16[256,1152]{1,0:T(8,128)(2,1)S(1)}, u32[]{:S(2)}, u32[]{:S(2)}) collective-permute-start(bf16[256,1152]{1,0:T(8,128)(2,1)S(1)} %fusion.refs_2_.refs_4_), channel_id=1, source_target_pairs={{0,2},{1,3},{2,0},{3,1},{4,6},{5,7},{6,4},{7,5},{8,10},{9,11},{10,... | collective-permute-start | bytes 1769480 | tf_op jit(solution)/shard_map/ppermute | solution.py:787
  237.3 38.1 %collective-permute-start.33 = (bf16[2,144,1152]{2,1,0:T(8,128)(2,1)}, bf16[2,144,1152]{2,1,0:T(8,128)(2,1)}, u32[]{:S(2)}, u32[]{:S(2)}) collective-permute-start(bf16[2,144,1152]{2,1,0:T(8,128)(2,1)} %get-tuple-element.176), channel_id=1, source_target_pairs={{0,2},{1,3},{2,0},{3,1},{4,6},{5,7},{6,4},{7,5},{8,10},{9,11},{10,... | collective-permute-start | bytes 1990664 | tf_op jit(solution)/shard_map/ppermute | solution.py:787
  237.9 40.6 %collective-permute-start.35 = (bf16[2,144,1152]{2,1,0:T(8,128)(2,1)}, bf16[2,144,1152]{2,1,0:T(8,128)(2,1)S(1)}, u32[]{:S(2)}, u32[]{:S(2)}) collective-permute-start(bf16[2,144,1152]{2,1,0:T(8,128)(2,1)} %get-tuple-element.181), channel_id=1, source_target_pairs={{0,2},{1,3},{2,0},{3,1},{4,6},{5,7},{6,4},{7,5},{8,10},{9,11},{10,... | collective-permute-start | bytes 1990664 | tf_op jit(solution)/shard_map/ppermute | solution.py:787
  264.1 39.4 %collective-permute-start.38 = (bf16[2,144,1152]{2,1,0:T(8,128)(2,1)}, bf16[2,144,1152]{2,1,0:T(8,128)(2,1)}, u32[]{:S(2)}, u32[]{:S(2)}) collective-permute-start(bf16[2,144,1152]{2,1,0:T(8,128)(2,1)} %get-tuple-element.185), channel_id=1, source_target_pairs={{0,2},{1,3},{2,0},{3,1},{4,6},{5,7},{6,4},{7,5},{8,10},{9,11},{10,... | collective-permute-start | bytes 1990664 | tf_op jit(solution)/shard_map/ppermute | solution.py:787
  264.8 42.1 %collective-permute-start.34 = (bf16[2,144,1152]{2,1,0:T(8,128)(2,1)}, bf16[2,144,1152]{2,1,0:T(8,128)(2,1)}, u32[]{:S(2)}, u32[]{:S(2)}) collective-permute-start(bf16[2,144,1152]{2,1,0:T(8,128)(2,1)} %get-tuple-element.179), channel_id=1, source_target_pairs={{0,2},{1,3},{2,0},{3,1},{4,6},{5,7},{6,4},{7,5},{8,10},{9,11},{10,... | collective-permute-start | bytes 1990664 | tf_op jit(solution)/shard_map/ppermute | solution.py:787
  267.4 49.9 %all-to-all-start.3 = ((f32[32,16,128]{2,1,0:T(8,128)}), f32[32,16,128]{2,1,0:T(8,128)S(1)}, u32[]{:S(2)}, u32[]{:S(2)}) async-start(f32[32,16,128]{2,1,0:T(8,128)} %bitcast.33), calls=%async_computation.3 | async-start | bytes 524288 | tf_op jit(solution)/shard_map/all_to_all | solution.py:794
  278.7 24.1 %collective-permute-start.37 = (bf16[144,1152]{1,0:T(8,128)(2,1)S(1)}, bf16[144,1152]{1,0:T(8,128)(2,1)S(1)}, u32[]{:S(2)}, u32[]{:S(2)}) collective-permute-start(bf16[144,1152]{1,0:T(8,128)(2,1)S(1)} %get-tuple-element.199), channel_id=1, source_target_pairs={{0,4},{1,5},{2,6},{3,7},{4,0},{5,1},{6,2},{7,3},{8,12},{9,13},{10,... | collective-permute-start | bytes 995336 | tf_op jit(solution)/shard_map/ppermute | solution.py:787
  309.1 28.2 %collective-permute-start.40 = (bf16[144,1152]{1,0:T(8,128)(2,1)}, bf16[144,1152]{1,0:T(8,128)(2,1)}, u32[]{:S(2)}, u32[]{:S(2)}) collective-permute-start(bf16[144,1152]{1,0:T(8,128)(2,1)} %get-tuple-element.195), channel_id=1, source_target_pairs={{0,4},{1,5},{2,6},{3,7},{4,0},{5,1},{6,2},{7,3},{8,12},{9,13},{10,... | collective-permute-start | bytes 995336 | tf_op jit(solution)/shard_map/ppermute | solution.py:787
  310.0 27.2 %collective-permute-start.42 = (bf16[144,1152]{1,0:T(8,128)(2,1)}, bf16[144,1152]{1,0:T(8,128)(2,1)}, u32[]{:S(2)}, u32[]{:S(2)}) collective-permute-start(bf16[144,1152]{1,0:T(8,128)(2,1)} %add_convert_fusion.5), channel_id=1, source_target_pairs={{0,16},{1,17},{2,18},{3,19},{4,20},{5,21},{6,22},{7,23},{8,24},{9,... | collective-permute-start | bytes 995336 | tf_op jit(solution)/shard_map/ppermute | solution.py:787
  312.2 25.0 %collective-permute-start.41 = (bf16[144,1152]{1,0:T(8,128)(2,1)}, bf16[144,1152]{1,0:T(8,128)(2,1)}, u32[]{:S(2)}, u32[]{:S(2)}) collective-permute-start(bf16[144,1152]{1,0:T(8,128)(2,1)} %add_convert_fusion.6), channel_id=1, source_target_pairs={{0,24},{1,25},{2,26},{3,27},{4,28},{5,29},{6,30},{7,31},{8,16},{9,... | collective-permute-start | bytes 995336 | tf_op jit(solution)/shard_map/ppermute | solution.py:787
  (75 other events, 677.1 us)
Sparse Core Ops, SparseCore 0:
  49.2 99.9 all-gather.1
  197.2 112.7 reduce-scatter.1

commit v6 on v5

--- a/solution.py
+++ b/solution.py
@@ -679,6 +679,12 @@
         result[...] = total[index * rows : (index + 1) * rows].astype(result.dtype)
 
 
+def join_rows_kernel(pieces, out):
+    height = pieces.shape[2]
+    for part in range(pieces.shape[0]):
+        out[:, part * height : (part + 1) * height] = pieces[part, 0 : out.shape[0], :]
+
+
 def modulation_kernel(conds, ada, part_out, ordered):
     groups, rows, _ = ordered.shape
     for group in range(groups):
@@ -848,8 +854,7 @@
     own_x, own_y = swap(own, x_mask, count), swap(own, y_mask, count)
     both_got = lax.all_to_all(both_send, "fsdp", 0, 0, tiled=True)
     *far, own_x, own_y, both_got = gate(*far, own_x, own_y, both_got)
-    own_feed = both_got[:, : 2 * sub].reshape(row_parts, 2, sub, height)
-    own_feed = own_feed.transpose(1, 2, 0, 3).reshape(2 * sub, width)
+    own_feed = line.call(join_rows_kernel, shape_of((2 * sub, width)), (both_got,), "join_rows")
     conds = both_got[:, 2 * sub : 2 * sub + clips].reshape(row_parts * clips, height)
     feed = lax.all_gather(own_feed, "dp", axis=0, tiled=True)
 
@@ -944,7 +949,7 @@
 
     def feed_call(index, name):
         return line.call(
-            functools.partial(feed_kernel, 32, column_parts),
+            functools.partial(feed_kernel, 16, column_parts),
             [shape_of((row_count, hidden_part))] * 4 + [shape_of(full, F32), shape_of(full)],
             (
                 tokens_two[index],
@@ -980,7 +985,8 @@
         (pltpu.VMEM((width, hidden_part), LOW), pltpu.SemaphoreType.DMA((column_parts,))),
     )
     feed_grads = feed_grads.reshape(2 * sub * column_parts, width)
-    feed_grads, grad_far = lax.optimization_barrier((feed_grads, grad_far))
+    far_side = [swap(array, 1, count) for array in (hidden, attended)]
+    feed_grads, grad_far, *far_side = lax.optimization_barrier((feed_grads, grad_far, *far_side))
     grad_parts = grad_parts[:2] + (grad_far,)
     line.token = grad_far
     groups = column_parts // 2
@@ -1006,7 +1012,7 @@
         "attn_backward",
     )
     own_side = (hidden, attended, d_mixed, d_branch)
-    far_side = [swap(array, 1, count) for array in own_side]
+    far_side += [swap(array, 1, count) for array in own_side[2:]]
     attn_grads, first = {}, {}
     for distances in (range(groups - 1, groups // 2 - 1, -1), range(groups // 2 - 1, -1, -1)):
         grads = line.call(

time: 356 us -> 351 us (0.986)
  waiting for transfers between devices: 90.3 us -> 86.6 us
    ppermute x44, waiting for transfers between devices: 65.3 us -> 60.1 us  [swap(): return lax.ppermute(value, AXES, [(i, i ^ mask) for i in range(count)])]
    pallas_call x13 -> x14, Pallas kernels: 119 us -> 121 us  [call(): pl.pallas_call(kernel, out_shape=shapes, in_specs=specs or [VMEM_SPEC] *...]
    unnamed x107 -> x95, local copies, waits for them, and re-layouts: 12.7 us -> 11 us
  transfers between devices with their start and end apart: 50 -> 50, of which waited for: 19 -> 17; matrix products, arithmetic and copies ran while one was open for 7% -> 7% of each run, Pallas kernels for 29% -> 29%
where the time goes in v6:
time: 351 us; the launch traced here: 347 us
  Pallas kernels  121 us (34%)
  waiting for transfers between devices  86.6 us (25%)
  starting transfers between devices  62.8 us (18%)
  blocking collectives  24.3 us (7%)
  local copies, waits for them, and re-layouts  21.8 us (6%)
  between operations  15 us (4%)
  other arithmetic  13.5 us (4%)
    pallas_call x14, Pallas kernels, call(): pl.pallas_call(kernel, out_shape=shapes, in_specs=specs or [VMEM_SPEC] *...  121 us
    ppermute x44, waiting for transfers between devices, swap(): return lax.ppermute(value, AXES, [(i, i ^ mask) for i in range(count)])  60.1 us
    ppermute x44, starting transfers between devices, swap(): return lax.ppermute(value, AXES, [(i, i ^ mask) for i in range(count)])  39.1 us
    all_to_all x1, blocking collectives, fast_body(): conds = lax.all_to_all(conds, 'dp', 0, 0, tiled=True)  24.3 us
    all_to_all x2, starting transfers between devices, padded_exchange(): got = lax.all_to_all(rows, AXES, 0, 0, tiled=True)  15.4 us
    all_to_all x2, waiting for transfers between devices, padded_exchange(): got = lax.all_to_all(rows, AXES, 0, 0, tiled=True)  15 us
    unnamed x95, local copies, waits for them, and re-layouts  11 us
  transfers between devices with their start and end apart: 50, of which 17 were waited for; matrix products, arithmetic and copies ran while one was open for 7% of the time, Pallas kernels for 29%

profile of v6, /device:TPU:0, one launch (start us, length us, event | category | flops | bytes accessed | tf_op | source)
XLA Modules:
  0.0 346.5 jit_solution(17895334566217381798)
XLA Ops:
  7.2 3.6 %prepare.1 = (bf16[144,1152]{1,0:T(8,128)(2,1)}, bf16[4,304,288]{2,1,0:T(8,128)(2,1)}) custom-call(s32[2]{0:T(128)} %refs_0_.2, s32[2]{0:T(128)} %refs_1_.1, bf16[1000,1152]{1,0:T(8,128)(2,1)} %refs_2_.1, bf16[101,1152]{1,0:T(8,128)(2,1)} %refs_3_.1, bf16[288,432]{1,0:T(8,128)(2,1)} %refs_4_.1, bf16[144,288]{1,0:T(8,128)(2,1)} %bitcast.87, ...), custom_call_target="tpu_custom_call" | custom-call | flops 1000 | bytes 100 | tf_op jit(solution)/shard_map/prepare/pallas_call | solution.py:771
  13.0 4.4 %all-to-all-start = ((bf16[4,304,288]{1,2,0:T(8,128)(2,1)}), bf16[4,304,288]{1,2,0:T(8,128)(2,1)S(1)}, u32[]{:S(2)}, u32[]{:S(2)}) async-start(bf16[4,304,288]{1,2,0:T(8,128)(2,1)} %copy.26), calls=%async_computation | async-start | bytes 1769472 | tf_op jit(solution)/shard_map/all_to_all | solution.py:855
  25.9 8.7 %collective-permute-done = bf16[1,144,1152]{2,1,0:T(8,128)(2,1)S(1)} collective-permute-done((bf16[1,144,1152]{2,1,0:T(8,128)(2,1)S(1)}, bf16[1,144,1152]{2,1,0:T(8,128)(2,1)S(1)}, u32[]{:S(2)}, u32[]{:S(2)}) %collective-permute-start) | collective-permute-done | bytes 331808 | tf_op jit(solution)/shard_map/ppermute | solution.py:793
  34.7 10.9 %collective-permute-done.1 = bf16[1,144,1152]{2,1,0:T(8,128)(2,1)S(1)} collective-permute-done((bf16[1,144,1152]{2,1,0:T(8,128)(2,1)S(1)}, bf16[1,144,1152]{2,1,0:T(8,128)(2,1)S(1)}, u32[]{:S(2)}, u32[]{:S(2)}) %collective-permute-start.1) | collective-permute-done | bytes 331808 | tf_op jit(solution)/shard_map/ppermute | solution.py:793
  57.9 24.3 %all_to_all.25.conds = bf16[8,16,384]{2,1,0:T(8,128)(2,1)} all-to-all(bf16[8,16,384]{2,1,0:T(8,128)(2,1)S(1)} %broadcast_in_dim.20), channel_id=1, replica_groups=mesh['dp'=8,'fsdp'=4] {'dp'}, dimensions={0} | all-to-all | bytes 196608 | tf_op jit(solution)/shard_map/all_to_all | solution.py:865
  89.0 8.9 %all-to-all-start.2 = ((f32[32,16,128]{2,1,0:T(8,128)}), f32[32,16,128]{2,1,0:T(8,128)S(1)}, u32[]{:S(2)}, u32[]{:S(2)}) async-start(f32[32,16,128]{2,1,0:T(8,128)} %bitcast.80), calls=%async_computation.2 | async-start | bytes 524288 | tf_op jit(solution)/shard_map/all_to_all | solution.py:800
  100.1 15.0 %all-to-all-done.2 = f32[32,16,128]{2,1,0:T(8,128)S(1)} async-done(((f32[32,16,128]{2,1,0:T(8,128)}), f32[32,16,128]{2,1,0:T(8,128)S(1)}, u32[]{:S(2)}, u32[]{:S(2)}) %all-to-all-start.2) | async-done | bytes 262176 | tf_op jit(solution)/shard_map/all_to_all | solution.py:800
  120.6 21.7 %attn_forward.1 = (bf16[1152,256]{1,0:T(8,128)(2,1)}, bf16[8,256,432]{2,1,0:T(8,128)(2,1)}, bf16[2,16,128,128]{3,2,1,0:T(8,128)(2,1)}, bf16[1152,256]{1,0:T(8,12...) custom-call(s32[2]{0:T(128)} %refs_0_.3, ...), custom_call_target="tpu_custom_call" | custom-call | flops 1000 | bytes 100 | tf_op jit(solution)/shard_map/attn_forward/pallas_call | solution.py:771
  144.7 4.9 %all-gather.2.cloned.1.call-done.refs_4_.refs_16_ = bf16[2304,1152]{1,0:T(8,128)(2,1)} async-done(((bf16[288,1152]{1,0:T(8,128)(2,1)}), bf16[2304,1152]{1,0:T(8,128)(2,1)}) %all-gather.2.cloned.1.call-update) | async-done | bytes 5308432 | tf_op jit(solution)/shard_map/all_gather | solution.py:859
  149.5 11.8 %feed_near.1 = (bf16[256,1152]{1,0:T(8,128)(2,1)}, bf16[256,1152]{1,0:T(8,128)(2,1)}, bf16[256,1152]{1,0:T(8,128)(2,1)}, bf16[256,1152]{1,0:T(8,128)(2,1)}, f32[...) custom-call(bf16[256,1152]{1,0:T(8,128)(2,1)} %get-tuple-element.144.refs_0_, bf16[256,1152]{1,0:T(8,128)(2,1)} %copy-done.16, ...), custom_call_target="tpu_custom_call" | custom-call | flops 1000 | bytes 100 | tf_op jit(solution)/shard_map/feed_near/pallas_call | solution.py:771
  164.4 12.0 %feed_distant.1 = (bf16[256,1152]{1,0:T(8,128)(2,1)}, bf16[256,1152]{1,0:T(8,128)(2,1)}, bf16[256,1152]{1,0:T(8,128)(2,1)}, bf16[256,1152]{1,0:T(8,128)(2,1)}, f...) custom-call(bf16[256,1152]{1,0:T(8,128)(2,1)} %copy-done.17, bf16[256,1152]{1,0:T(8,128)(2,1)} %copy-done.19, ...), custom_call_target="tpu_custom_call" | custom-call | flops 1000 | bytes 100 | tf_op jit(solution)/shard_map/feed_distant/pallas_call | solution.py:771
  181.6 15.9 %feed_weight.1 = (bf16[8,288,1152]{2,1,0:T(8,128)(2,1)}, f32[256,1152]{1,0:T(8,128)}, bf16[256,1152]{1,0:T(8,128)(2,1)}, bf16[256,1152]{1,0:T(8,128)(2,1)}, bf16[256,1152]{1,0:T(8,128)(2,1)}) custom-call(bf16[256,1152]{1,0:T(8,128)(2,1)} %get-tuple-element.144.refs_0_, bf16[256,1152]{1,0:T(8,128)(2,1)} %copy-done.16, bf16[256,1152]{1,0:T(8,128)(2,1)} %copy-done.17, ...), custom_call_target="tpu_custom_call" | custom-call | flops 1000 | bytes 100 | tf_op jit(solution)/shard_map/feed_weight/pallas_call | solution.py:771
  203.0 8.0 %proj_backward.1 = (f32[256,1152]{1,0:T(8,128)}, bf16[256,1152]{1,0:T(8,128)(2,1)}, bf16[256,1152]{1,0:T(8,128)(2,1)}, f32[2,3,1152]{2,1,0:T(4,128)}) custom-call(bf16[256,1152]{1,0:T(8,128)(2,1)} %bitcast.65, f32[2,6,1152]{2,1,0:T(8,128)} %copy-done.32, f32[256,1152]{1,0:T(8,128)} %get-tuple-element.133.refs_2_, ...), custom_call_target="tpu_custom_call" | custom-call | flops 1000 | bytes 100 | tf_op jit(solution)/shard_map/proj_backward/pallas_call | solution.py:771
  211.0 10.4 %attn_backward.1.refs_2_.refs_3_ = bf16[8,256,512]{2,1,0:T(8,128)(2,1)} custom-call(bf16[8,256,432]{2,1,0:T(8,128)(2,1)} %get-tuple-element.165.refs_0_, bf16[2,16,128,128]{3,2,1,0:T(8,128)(2,1)} %get-tuple-element.166.refs_1_, bf16[256,1152]{1,0:T(8,128)(2,1)} %get-tuple-element.167.refs_2_), custom_call_target="tpu_custom_call" | custom-call | flops 1000 | bytes 100 | tf_op jit(solution)/shard_map/attn_backward/pallas_call | solution.py:771
  222.5 4.4 %collective-permute-done.30.refs_7_ = bf16[256,1152]{1,0:T(8,128)(2,1)S(1)} collective-permute-done((bf16[256,1152]{1,0:T(8,128)(2,1)S(1)}, bf16[256,1152]{1,0:T(8,128)(2,1)S(1)}, u32[]{:S(2)}, u32[]{:S(2)}) %collective-permute-start.30) | collective-permute-done | bytes 589856 | tf_op jit(solution)/shard_map/ppermute | solution.py:793
  229.1 7.1 %attn_weight.2 = (bf16[2,144,1152]{2,1,0:T(8,128)(2,1)}, bf16[2,144,1152]{2,1,0:T(8,128)(2,1)}, bf16[2,144,1152]{2,1,0:T(8,128)(2,1)}, bf16[2,144,1152]{2,1,0:T(8,128)(2,1)}) custom-call(bf16[1152,256]{1,0:T(8,128)(2,1)} %get-tuple-element.175.refs_0_, bf16[1152,256]{1,0:T(8,128)(2,1)} %get-tuple-element.155.refs_1_, ...), custom_call_target="tpu_custom_call" | custom-call | flops 1000 | bytes 100 | tf_op jit(solution)/shard_map/attn_weight/pallas_call | solution.py:771
  239.2 7.0 %attn_weight.3 = (bf16[2,144,1152]{2,1,0:T(8,128)(2,1)}, bf16[2,144,1152]{2,1,0:T(8,128)(2,1)}, bf16[2,144,1152]{2,1,0:T(8,128)(2,1)}, bf16[2,144,1152]{2,1,0:T(8,128)(2,1)}) custom-call(bf16[1152,256]{1,0:T(8,128)(2,1)} %get-tuple-element.175.refs_0_, bf16[1152,256]{1,0:T(8,128)(2,1)} %get-tuple-element.155.refs_1_, ...), custom_call_target="tpu_custom_call" | custom-call | flops 1000 | bytes 100 | tf_op jit(solution)/shard_map/attn_weight/pallas_call | solution.py:771
  246.2 13.1 %qkv_backward.1 = (bf16[256,1152]{1,0:T(8,128)(2,1)}, f32[2,2,1152]{2,1,0:T(2,128)}) custom-call(bf16[256,1152]{1,0:T(8,128)(2,1)} %bitcast.69, f32[2,6,1152]{2,1,0:T(8,128)} %copy-done.32, f32[256,1152]{1,0:T(8,128)} %get-tuple-element.178.refs_2_, bf16[8,256,512]{2,1,0:T(8,128)(2,1)} %attn_backward.1.refs_2_.refs_3_, bf16[1,144,1152]{2,1,0:T(8,128)(2,1)} %bitcast.71, ...), custom_call_target="tpu_custom_call" | custom-call | flops 1000 | bytes 100 | tf_op jit(solution)/shard_map/qkv_backward/pallas_call | solution.py:771
  263.3 6.5 %all-to-all-start.3 = ((f32[32,16,128]{2,1,0:T(8,128)}), f32[32,16,128]{2,1,0:T(8,128)S(1)}, u32[]{:S(2)}, u32[]{:S(2)}) async-start(f32[32,16,128]{2,1,0:T(8,128)} %bitcast.30), calls=%async_computation.3 | async-start | bytes 524288 | tf_op jit(solution)/shard_map/all_to_all | solution.py:800
  273.4 12.7 %collective-permute-done.36 = bf16[144,1152]{1,0:T(8,128)(2,1)S(1)} collective-permute-done((bf16[144,1152]{1,0:T(8,128)(2,1)S(1)}, bf16[144,1152]{1,0:T(8,128)(2,1)S(1)}, u32[]{:S(2)}, u32[]{:S(2)}) %collective-permute-start.36) | collective-permute-done | bytes 331808 | tf_op jit(solution)/shard_map/ppermute | solution.py:793
  286.9 10.2 %collective-permute-done.37 = bf16[144,1152]{1,0:T(8,128)(2,1)S(1)} collective-permute-done((bf16[144,1152]{1,0:T(8,128)(2,1)S(1)}, bf16[144,1152]{1,0:T(8,128)(2,1)S(1)}, u32[]{:S(2)}, u32[]{:S(2)}) %collective-permute-start.37) | collective-permute-done | bytes 331808 | tf_op jit(solution)/shard_map/ppermute | solution.py:793
  312.6 3.6 %all-to-all-start.4 = ((bf16[4,2,144,288]{3,2,1,0:T(8,128)(2,1)}), bf16[4,2,144,288]{3,2,1,0:T(8,128)(2,1)S(1)}, u32[]{:S(2)}, u32[]{:S(2)}) async-start(bf16[4,2,144,288]{3,2,1,0:T(8,128)(2,1)} %bitcast.67), calls=%async_computation.5 | async-start | bytes 1769472 | tf_op jit(solution)/shard_map/all_to_all | solution.py:1072
  322.4 6.5 %all-to-all-done.4.back = bf16[4,2,144,288]{3,2,1,0:T(8,128)(2,1)S(1)} async-done(((bf16[4,2,144,288]{3,2,1,0:T(8,128)(2,1)}), bf16[4,2,144,288]{3,2,1,0:T(8,128)(2,1)S(1)}, u32[]{:S(2)}, u32[]{:S(2)}) %all-to-all-start.4) | async-done | bytes 663584 | tf_op jit(solution)/shard_map/all_to_all | solution.py:1072
  332.6 4.1 %collective-permute-done.43.refs_4_ = bf16[144,1152]{1,0:T(8,128)(2,1)} collective-permute-done((bf16[144,1152]{1,0:T(8,128)(2,1)}, bf16[144,1152]{1,0:T(8,128)(2,1)}, u32[]{:S(2)}, u32[]{:S(2)}) %collective-permute-start.43) | collective-permute-done | bytes 331808 | tf_op jit(solution)/shard_map/ppermute | solution.py:793
  (227 shorter events, 95.8 us)
Async XLA Ops:
  13.0 32.6 %all-to-all-start = ((bf16[4,304,288]{1,2,0:T(8,128)(2,1)}), bf16[4,304,288]{1,2,0:T(8,128)(2,1)S(1)}, u32[]{:S(2)}, u32[]{:S(2)}) async-start(bf16[4,304,288]{1,2,0:T(8,128)(2,1)} %copy.26), calls=%async_computation | async-start | bytes 1769472 | tf_op jit(solution)/shard_map/all_to_all | solution.py:855
  17.3 132.2 %all-gather.2.cloned.1.call-start = ((), (), s32[]{:S(2)}) async-start(), calls=%async_computation.6 | async-start | bytes 5971968 | tf_op jit(solution)/shard_map/all_gather | solution.py:859
  19.8 25.8 %collective-permute-start.1 = (bf16[1,144,1152]{2,1,0:T(8,128)(2,1)S(1)}, bf16[1,144,1152]{2,1,0:T(8,128)(2,1)S(1)}, u32[]{:S(2)}, u32[]{:S(2)}) collective-permute-start(bf16[1,144,1152]{2,1,0:T(8,128)(2,1)S(1)} %bitcast.73), channel_id=1, source_target_pairs={{0,16},{1,17},{2,18},{3,19},{4,20},{5,21},{6,22},{7,23},{8,24},{9,... | collective-permute-start | bytes 995336 | tf_op jit(solution)/shard_map/ppermute | solution.py:793
  49.4 32.8 %collective-permute-start.11 = (bf16[3,144,1152]{2,1,0:T(8,128)(2,1)S(1)}, bf16[3,144,1152]{2,1,0:T(8,128)(2,1)S(1)}, u32[]{:S(2)}, u32[]{:S(2)}) collective-permute-start(bf16[3,144,1152]{2,1,0:T(8,128)(2,1)S(1)} %constant_dynamic-update-slice_fusion.refs_6_.refs_7_), channel_id=1, source_target_pairs={{0,1},{1,0},{2,3},{3,2},{4,5},{5,4},{6,7},{7,6},{8,9},{9,8},{10,11... | collective-permute-start | bytes 2985992 | tf_op jit(solution)/shard_map/ppermute | solution.py:793
  49.5 32.7 %collective-permute-start.6 = (bf16[3,144,1152]{2,1,0:T(8,128)(2,1)S(1)}, bf16[3,144,1152]{2,1,0:T(8,128)(2,1)}, u32[]{:S(2)}, u32[]{:S(2)}) collective-permute-start(bf16[3,144,1152]{2,1,0:T(8,128)(2,1)S(1)} %constant_dynamic-update-slice_fusion.refs_6_.refs_7_), channel_id=1, source_target_pairs={{0,4},{1,5},{2,6},{3,7},{4,0},{5,1},{6,2},{7,3},{8,12},{9,13},{10,... | collective-permute-start | bytes 2985992 | tf_op jit(solution)/shard_map/ppermute | solution.py:793
  51.0 31.2 %collective-permute-start.7 = (bf16[3,144,1152]{2,1,0:T(8,128)(2,1)S(1)}, bf16[3,144,1152]{2,1,0:T(8,128)(2,1)}, u32[]{:S(2)}, u32[]{:S(2)}) collective-permute-start(bf16[3,144,1152]{2,1,0:T(8,128)(2,1)S(1)} %constant_dynamic-update-slice_fusion.refs_6_.refs_7_), channel_id=1, source_target_pairs={{0,2},{1,3},{2,0},{3,1},{4,6},{5,7},{6,4},{7,5},{8,10},{9,11},{10,... | collective-permute-start | bytes 2985992 | tf_op jit(solution)/shard_map/ppermute | solution.py:793
  52.9 29.3 %collective-permute-start.9 = (bf16[1,144,1152]{2,1,0:T(8,128)(2,1)S(1)}, bf16[1,144,1152]{2,1,0:T(8,128)(2,1)}, u32[]{:S(2)}, u32[]{:S(2)}) collective-permute-start(bf16[1,144,1152]{2,1,0:T(8,128)(2,1)S(1)} %collective-permute-done.3.refs_4_.refs_5_), channel_id=1, source_target_pairs={{0,1},{1,0},{2,3},{3,2},{4,5},{5,4},{6,7},{7,6},{8,9},{9,8},{10,11... | collective-permute-start | bytes 995336 | tf_op jit(solution)/shard_map/ppermute | solution.py:793
  55.7 26.5 %collective-permute-start.10 = (bf16[1,144,1152]{2,1,0:T(8,128)(2,1)}, bf16[1,144,1152]{2,1,0:T(8,128)(2,1)S(1)}, u32[]{:S(2)}, u32[]{:S(2)}) collective-permute-start(bf16[1,144,1152]{2,1,0:T(8,128)(2,1)} %collective-permute-done.4.refs_5_.refs_6_), channel_id=1, source_target_pairs={{0,1},{1,0},{2,3},{3,2},{4,5},{5,4},{6,7},{7,6},{8,9},{9,8},{10,11... | collective-permute-start | bytes 995336 | tf_op jit(solution)/shard_map/ppermute | solution.py:793
  82.2 33.9 %collective-permute-start.12 = (bf16[3,144,1152]{2,1,0:T(8,128)(2,1)}, bf16[3,144,1152]{2,1,0:T(8,128)(2,1)}, u32[]{:S(2)}, u32[]{:S(2)}) collective-permute-start(bf16[3,144,1152]{2,1,0:T(8,128)(2,1)} %collective-permute-done.6.refs_7_.refs_8_), channel_id=1, source_target_pairs={{0,2},{1,3},{2,0},{3,1},{4,6},{5,7},{6,4},{7,5},{8,10},{9,11},{10,... | collective-permute-start | bytes 2985992 | tf_op jit(solution)/shard_map/ppermute | solution.py:793
  84.2 32.0 %collective-permute-start.13 = (bf16[3,144,1152]{2,1,0:T(8,128)(2,1)}, bf16[3,144,1152]{2,1,0:T(8,128)(2,1)}, u32[]{:S(2)}, u32[]{:S(2)}) collective-permute-start(bf16[3,144,1152]{2,1,0:T(8,128)(2,1)} %collective-permute-done.6.refs_7_.refs_8_), channel_id=1, source_target_pairs={{0,1},{1,0},{2,3},{3,2},{4,5},{5,4},{6,7},{7,6},{8,9},{9,8},{10,11... | collective-permute-start | bytes 2985992 | tf_op jit(solution)/shard_map/ppermute | solution.py:793
  84.2 32.0 %collective-permute-start.14 = (bf16[3,144,1152]{2,1,0:T(8,128)(2,1)}, bf16[3,144,1152]{2,1,0:T(8,128)(2,1)}, u32[]{:S(2)}, u32[]{:S(2)}) collective-permute-start(bf16[3,144,1152]{2,1,0:T(8,128)(2,1)} %collective-permute-done.7.refs_8_.refs_9_), channel_id=1, source_target_pairs={{0,1},{1,0},{2,3},{3,2},{4,5},{5,4},{6,7},{7,6},{8,9},{9,8},{10,11... | collective-permute-start | bytes 2985992 | tf_op jit(solution)/shard_map/ppermute | solution.py:793
  89.0 26.1 %all-to-all-start.2 = ((f32[32,16,128]{2,1,0:T(8,128)}), f32[32,16,128]{2,1,0:T(8,128)S(1)}, u32[]{:S(2)}, u32[]{:S(2)}) async-start(f32[32,16,128]{2,1,0:T(8,128)} %bitcast.80), calls=%async_computation.2 | async-start | bytes 524288 | tf_op jit(solution)/shard_map/all_to_all | solution.py:800
  97.9 211.3 %reduce-scatter.2.cloned.1.call-start = ((), (), s32[]{:S(2)}) async-start(), calls=%async_computation.7 | async-start | bytes 5971968 | tf_op jit(solution)/shard_map/reduce_scatter | solution.py:993
  117.4 27.0 %collective-permute-start.19 = (bf16[256,1152]{1,0:T(8,128)(2,1)S(1)}, bf16[256,1152]{1,0:T(8,128)(2,1)S(1)}, u32[]{:S(2)}, u32[]{:S(2)}) collective-permute-start(bf16[256,1152]{1,0:T(8,128)(2,1)S(1)} %fusion.refs_2_.refs_4_), channel_id=1, source_target_pairs={{0,1},{1,0},{2,3},{3,2},{4,5},{5,4},{6,7},{7,6},{8,9},{9,8},{10,11... | collective-permute-start | bytes 1769480 | tf_op jit(solution)/shard_map/ppermute | solution.py:793
  117.5 26.8 %collective-permute-start.21 = (bf16[256,1152]{1,0:T(8,128)(2,1)S(1)}, bf16[256,1152]{1,0:T(8,128)(2,1)S(1)}, u32[]{:S(2)}, u32[]{:S(2)}) collective-permute-start(bf16[256,1152]{1,0:T(8,128)(2,1)S(1)} %fusion.refs_2_.refs_4_), channel_id=1, source_target_pairs={{0,2},{1,3},{2,0},{3,1},{4,6},{5,7},{6,4},{7,5},{8,10},{9,11},{10,... | collective-permute-start | bytes 1769480 | tf_op jit(solution)/shard_map/ppermute | solution.py:793
  236.2 33.6 %collective-permute-start.33 = (bf16[2,144,1152]{2,1,0:T(8,128)(2,1)}, bf16[2,144,1152]{2,1,0:T(8,128)(2,1)}, u32[]{:S(2)}, u32[]{:S(2)}) collective-permute-start(bf16[2,144,1152]{2,1,0:T(8,128)(2,1)} %get-tuple-element.182), channel_id=1, source_target_pairs={{0,2},{1,3},{2,0},{3,1},{4,6},{5,7},{6,4},{7,5},{8,10},{9,11},{10,... | collective-permute-start | bytes 1990664 | tf_op jit(solution)/shard_map/ppermute | solution.py:793
  236.8 36.1 %collective-permute-start.35 = (bf16[2,144,1152]{2,1,0:T(8,128)(2,1)}, bf16[2,144,1152]{2,1,0:T(8,128)(2,1)S(1)}, u32[]{:S(2)}, u32[]{:S(2)}) collective-permute-start(bf16[2,144,1152]{2,1,0:T(8,128)(2,1)} %get-tuple-element.187), channel_id=1, source_target_pairs={{0,2},{1,3},{2,0},{3,1},{4,6},{5,7},{6,4},{7,5},{8,10},{9,11},{10,... | collective-permute-start | bytes 1990664 | tf_op jit(solution)/shard_map/ppermute | solution.py:793
  260.1 37.9 %collective-permute-start.38 = (bf16[2,144,1152]{2,1,0:T(8,128)(2,1)}, bf16[2,144,1152]{2,1,0:T(8,128)(2,1)}, u32[]{:S(2)}, u32[]{:S(2)}) collective-permute-start(bf16[2,144,1152]{2,1,0:T(8,128)(2,1)} %get-tuple-element.191), channel_id=1, source_target_pairs={{0,2},{1,3},{2,0},{3,1},{4,6},{5,7},{6,4},{7,5},{8,10},{9,11},{10,... | collective-permute-start | bytes 1990664 | tf_op jit(solution)/shard_map/ppermute | solution.py:793
  260.8 40.5 %collective-permute-start.34 = (bf16[2,144,1152]{2,1,0:T(8,128)(2,1)}, bf16[2,144,1152]{2,1,0:T(8,128)(2,1)}, u32[]{:S(2)}, u32[]{:S(2)}) collective-permute-start(bf16[2,144,1152]{2,1,0:T(8,128)(2,1)} %get-tuple-element.185), channel_id=1, source_target_pairs={{0,2},{1,3},{2,0},{3,1},{4,6},{5,7},{6,4},{7,5},{8,10},{9,11},{10,... | collective-permute-start | bytes 1990664 | tf_op jit(solution)/shard_map/ppermute | solution.py:793
  263.3 49.3 %all-to-all-start.3 = ((f32[32,16,128]{2,1,0:T(8,128)}), f32[32,16,128]{2,1,0:T(8,128)S(1)}, u32[]{:S(2)}, u32[]{:S(2)}) async-start(f32[32,16,128]{2,1,0:T(8,128)} %bitcast.30), calls=%async_computation.3 | async-start | bytes 524288 | tf_op jit(solution)/shard_map/all_to_all | solution.py:800
  273.1 24.1 %collective-permute-start.37 = (bf16[144,1152]{1,0:T(8,128)(2,1)S(1)}, bf16[144,1152]{1,0:T(8,128)(2,1)S(1)}, u32[]{:S(2)}, u32[]{:S(2)}) collective-permute-start(bf16[144,1152]{1,0:T(8,128)(2,1)S(1)} %get-tuple-element.205), channel_id=1, source_target_pairs={{0,4},{1,5},{2,6},{3,7},{4,0},{5,1},{6,2},{7,3},{8,12},{9,13},{10,... | collective-permute-start | bytes 995336 | tf_op jit(solution)/shard_map/ppermute | solution.py:793
  303.5 29.1 %collective-permute-start.40 = (bf16[144,1152]{1,0:T(8,128)(2,1)}, bf16[144,1152]{1,0:T(8,128)(2,1)}, u32[]{:S(2)}, u32[]{:S(2)}) collective-permute-start(bf16[144,1152]{1,0:T(8,128)(2,1)} %get-tuple-element.201), channel_id=1, source_target_pairs={{0,4},{1,5},{2,6},{3,7},{4,0},{5,1},{6,2},{7,3},{8,12},{9,13},{10,... | collective-permute-start | bytes 995336 | tf_op jit(solution)/shard_map/ppermute | solution.py:793
  304.4 28.1 %collective-permute-start.42 = (bf16[144,1152]{1,0:T(8,128)(2,1)}, bf16[144,1152]{1,0:T(8,128)(2,1)}, u32[]{:S(2)}, u32[]{:S(2)}) collective-permute-start(bf16[144,1152]{1,0:T(8,128)(2,1)} %add_convert_fusion.5), channel_id=1, source_target_pairs={{0,16},{1,17},{2,18},{3,19},{4,20},{5,21},{6,22},{7,23},{8,24},{9,... | collective-permute-start | bytes 995336 | tf_op jit(solution)/shard_map/ppermute | solution.py:793
  307.9 24.7 %collective-permute-start.41 = (bf16[144,1152]{1,0:T(8,128)(2,1)}, bf16[144,1152]{1,0:T(8,128)(2,1)}, u32[]{:S(2)}, u32[]{:S(2)}) collective-permute-start(bf16[144,1152]{1,0:T(8,128)(2,1)} %add_convert_fusion.6), channel_id=1, source_target_pairs={{0,24},{1,25},{2,26},{3,27},{4,28},{5,29},{6,30},{7,31},{8,16},{9,... | collective-permute-start | bytes 995336 | tf_op jit(solution)/shard_map/ppermute | solution.py:793
  (69 other events, 684.4 us)
Sparse Core Ops, SparseCore 0:
  49.4 100.0 all-gather.1
  197.8 110.4 reduce-scatter.1

commit v7 on v6

--- a/solution.py
+++ b/solution.py
@@ -717,6 +717,15 @@
         for pair in range(pairs):
             start = (pair * row_parts + part) * sub
             send[part, sub : 2 * sub, pair * sub : (pair + 1) * sub] = down_t[:, start : start + sub]
+
+
+def cut_rows_kernel(total, out):
+    parts, sides, half, height = out.shape
+    for part in range(parts):
+        for side in range(sides):
+            out[part, side] = total[
+                side * half : (side + 1) * half, part * height : (part + 1) * height
+            ]
 
 
 def feed_finish_kernel(back, up_grad, down_grad_t):
@@ -1067,7 +1076,9 @@
     attn_sum(3)
     attn_sum(2)
     split_sum(1)
-    back = feed_sum.reshape(2, sub, row_parts, height).transpose(2, 0, 1, 3)
+    back = line.call(
+        cut_rows_kernel, shape_of((row_parts, 2, sub, height)), (feed_sum,), "cut_rows"
+    )
     line.token, back = lax.optimization_barrier((line.token, back))
     back = lax.all_to_all(back, "fsdp", 0, 0, tiled=True)
     split_sum(0)

time: 351 us -> 351 us (level)
    pallas_call x14 -> x15, Pallas kernels: 121 us -> 123 us  [call(): pl.pallas_call(kernel, out_shape=shapes, in_specs=specs or [VMEM_SPEC] *...]
  transfers between devices with their start and end apart: 50 -> 50, of which waited for: 17 -> 17; matrix products, arithmetic and copies ran while one was open for 7% -> 6% of each run, Pallas kernels for 29% -> 30%
where the time goes in v7:
time: 351 us; the launch traced here: 347 us
  Pallas kernels  123 us (35%)
  waiting for transfers between devices  87.7 us (25%)
  starting transfers between devices  62.8 us (18%)
  blocking collectives  24.3 us (7%)
  local copies, waits for them, and re-layouts  18.5 us (5%)
  between operations  15 us (4%)
  other arithmetic  13.5 us (4%)
    pallas_call x15, Pallas kernels, call(): pl.pallas_call(kernel, out_shape=shapes, in_specs=specs or [VMEM_SPEC] *...  123 us
    ppermute x44, waiting for transfers between devices, swap(): return lax.ppermute(value, AXES, [(i, i ^ mask) for i in range(count)])  61.2 us
    ppermute x44, starting transfers between devices, swap(): return lax.ppermute(value, AXES, [(i, i ^ mask) for i in range(count)])  39.1 us
    all_to_all x1, blocking collectives, fast_body(): conds = lax.all_to_all(conds, 'dp', 0, 0, tiled=True)  24.3 us
    all_to_all x2, starting transfers between devices, padded_exchange(): got = lax.all_to_all(rows, AXES, 0, 0, tiled=True)  15.4 us
    all_to_all x2, waiting for transfers between devices, padded_exchange(): got = lax.all_to_all(rows, AXES, 0, 0, tiled=True)  15 us
    unnamed x95, local copies, waits for them, and re-layouts  11 us
  transfers between devices with their start and end apart: 50, of which 17 were waited for; matrix products, arithmetic and copies ran while one was open for 6% of the time, Pallas kernels for 30%

profile of v7, /device:TPU:0, one launch (start us, length us, event | category | flops | bytes accessed | tf_op | source)
XLA Modules:
  0.0 346.5 jit_solution(17896302882499605711)
XLA Ops:
  7.2 3.6 %prepare.1 = (bf16[144,1152]{1,0:T(8,128)(2,1)}, bf16[4,304,288]{2,1,0:T(8,128)(2,1)}) custom-call(s32[2]{0:T(128)} %refs_0_.2, s32[2]{0:T(128)} %refs_1_.1, bf16[1000,1152]{1,0:T(8,128)(2,1)} %refs_2_.1, bf16[101,1152]{1,0:T(8,128)(2,1)} %refs_3_.1, bf16[288,432]{1,0:T(8,128)(2,1)} %refs_4_.1, bf16[144,288]{1,0:T(8,128)(2,1)} %bitcast.83, ...), custom_call_target="tpu_custom_call" | custom-call | flops 1000 | bytes 100 | tf_op jit(solution)/shard_map/prepare/pallas_call | solution.py:780
  13.0 4.4 %all-to-all-start = ((bf16[4,304,288]{1,2,0:T(8,128)(2,1)}), bf16[4,304,288]{1,2,0:T(8,128)(2,1)S(1)}, u32[]{:S(2)}, u32[]{:S(2)}) async-start(bf16[4,304,288]{1,2,0:T(8,128)(2,1)} %copy.24), calls=%async_computation | async-start | bytes 1769472 | tf_op jit(solution)/shard_map/all_to_all | solution.py:864
  25.9 8.7 %collective-permute-done = bf16[1,144,1152]{2,1,0:T(8,128)(2,1)S(1)} collective-permute-done((bf16[1,144,1152]{2,1,0:T(8,128)(2,1)S(1)}, bf16[1,144,1152]{2,1,0:T(8,128)(2,1)S(1)}, u32[]{:S(2)}, u32[]{:S(2)}) %collective-permute-start) | collective-permute-done | bytes 331808 | tf_op jit(solution)/shard_map/ppermute | solution.py:802
  34.7 10.9 %collective-permute-done.1 = bf16[1,144,1152]{2,1,0:T(8,128)(2,1)S(1)} collective-permute-done((bf16[1,144,1152]{2,1,0:T(8,128)(2,1)S(1)}, bf16[1,144,1152]{2,1,0:T(8,128)(2,1)S(1)}, u32[]{:S(2)}, u32[]{:S(2)}) %collective-permute-start.1) | collective-permute-done | bytes 331808 | tf_op jit(solution)/shard_map/ppermute | solution.py:802
  57.9 24.3 %all_to_all.25.conds = bf16[8,16,384]{2,1,0:T(8,128)(2,1)} all-to-all(bf16[8,16,384]{2,1,0:T(8,128)(2,1)S(1)} %broadcast_in_dim.20), channel_id=1, replica_groups=mesh['dp'=8,'fsdp'=4] {'dp'}, dimensions={0} | all-to-all | bytes 196608 | tf_op jit(solution)/shard_map/all_to_all | solution.py:874
  89.0 8.9 %all-to-all-start.2 = ((f32[32,16,128]{2,1,0:T(8,128)}), f32[32,16,128]{2,1,0:T(8,128)S(1)}, u32[]{:S(2)}, u32[]{:S(2)}) async-start(f32[32,16,128]{2,1,0:T(8,128)} %bitcast.76), calls=%async_computation.2 | async-start | bytes 524288 | tf_op jit(solution)/shard_map/all_to_all | solution.py:809
  100.1 15.0 %all-to-all-done.2 = f32[32,16,128]{2,1,0:T(8,128)S(1)} async-done(((f32[32,16,128]{2,1,0:T(8,128)}), f32[32,16,128]{2,1,0:T(8,128)S(1)}, u32[]{:S(2)}, u32[]{:S(2)}) %all-to-all-start.2) | async-done | bytes 262176 | tf_op jit(solution)/shard_map/all_to_all | solution.py:809
  120.6 21.7 %attn_forward.1 = (bf16[1152,256]{1,0:T(8,128)(2,1)}, bf16[8,256,432]{2,1,0:T(8,128)(2,1)}, bf16[2,16,128,128]{3,2,1,0:T(8,128)(2,1)}, bf16[1152,256]{1,0:T(8,12...) custom-call(s32[2]{0:T(128)} %refs_0_.3, ...), custom_call_target="tpu_custom_call" | custom-call | flops 1000 | bytes 100 | tf_op jit(solution)/shard_map/attn_forward/pallas_call | solution.py:780
  144.7 4.9 %all-gather.2.cloned.1.call-done.refs_4_.refs_16_ = bf16[2304,1152]{1,0:T(8,128)(2,1)} async-done(((bf16[288,1152]{1,0:T(8,128)(2,1)}), bf16[2304,1152]{1,0:T(8,128)(2,1)}) %all-gather.2.cloned.1.call-update) | async-done | bytes 5308432 | tf_op jit(solution)/shard_map/all_gather | solution.py:868
  149.5 11.8 %feed_near.1 = (bf16[256,1152]{1,0:T(8,128)(2,1)}, bf16[256,1152]{1,0:T(8,128)(2,1)}, bf16[256,1152]{1,0:T(8,128)(2,1)}, bf16[256,1152]{1,0:T(8,128)(2,1)}, f32[...) custom-call(bf16[256,1152]{1,0:T(8,128)(2,1)} %get-tuple-element.144.refs_0_, bf16[256,1152]{1,0:T(8,128)(2,1)} %copy-done.16, ...), custom_call_target="tpu_custom_call" | custom-call | flops 1000 | bytes 100 | tf_op jit(solution)/shard_map/feed_near/pallas_call | solution.py:780
  164.4 12.0 %feed_distant.1 = (bf16[256,1152]{1,0:T(8,128)(2,1)}, bf16[256,1152]{1,0:T(8,128)(2,1)}, bf16[256,1152]{1,0:T(8,128)(2,1)}, bf16[256,1152]{1,0:T(8,128)(2,1)}, f...) custom-call(bf16[256,1152]{1,0:T(8,128)(2,1)} %copy-done.17, bf16[256,1152]{1,0:T(8,128)(2,1)} %copy-done.19, ...), custom_call_target="tpu_custom_call" | custom-call | flops 1000 | bytes 100 | tf_op jit(solution)/shard_map/feed_distant/pallas_call | solution.py:780
  181.6 15.9 %feed_weight.1 = (bf16[8,288,1152]{2,1,0:T(8,128)(2,1)}, f32[256,1152]{1,0:T(8,128)}, bf16[256,1152]{1,0:T(8,128)(2,1)}, bf16[256,1152]{1,0:T(8,128)(2,1)}, bf16[256,1152]{1,0:T(8,128)(2,1)}) custom-call(bf16[256,1152]{1,0:T(8,128)(2,1)} %get-tuple-element.144.refs_0_, bf16[256,1152]{1,0:T(8,128)(2,1)} %copy-done.16, bf16[256,1152]{1,0:T(8,128)(2,1)} %copy-done.17, ...), custom_call_target="tpu_custom_call" | custom-call | flops 1000 | bytes 100 | tf_op jit(solution)/shard_map/feed_weight/pallas_call | solution.py:780
  203.0 8.0 %proj_backward.1 = (f32[256,1152]{1,0:T(8,128)}, bf16[256,1152]{1,0:T(8,128)(2,1)}, bf16[256,1152]{1,0:T(8,128)(2,1)}, f32[2,3,1152]{2,1,0:T(4,128)}) custom-call(bf16[256,1152]{1,0:T(8,128)(2,1)} %bitcast.62, f32[2,6,1152]{2,1,0:T(8,128)} %copy-done.32, f32[256,1152]{1,0:T(8,128)} %get-tuple-element.133.refs_2_, ...), custom_call_target="tpu_custom_call" | custom-call | flops 1000 | bytes 100 | tf_op jit(solution)/shard_map/proj_backward/pallas_call | solution.py:780
  211.0 10.4 %attn_backward.1.refs_2_.refs_3_ = bf16[8,256,512]{2,1,0:T(8,128)(2,1)} custom-call(bf16[8,256,432]{2,1,0:T(8,128)(2,1)} %get-tuple-element.165.refs_0_, bf16[2,16,128,128]{3,2,1,0:T(8,128)(2,1)} %get-tuple-element.166.refs_1_, bf16[256,1152]{1,0:T(8,128)(2,1)} %get-tuple-element.167.refs_2_), custom_call_target="tpu_custom_call" | custom-call | flops 1000 | bytes 100 | tf_op jit(solution)/shard_map/attn_backward/pallas_call | solution.py:780
  222.5 4.4 %collective-permute-done.30.refs_7_ = bf16[256,1152]{1,0:T(8,128)(2,1)S(1)} collective-permute-done((bf16[256,1152]{1,0:T(8,128)(2,1)S(1)}, bf16[256,1152]{1,0:T(8,128)(2,1)S(1)}, u32[]{:S(2)}, u32[]{:S(2)}) %collective-permute-start.30) | collective-permute-done | bytes 589856 | tf_op jit(solution)/shard_map/ppermute | solution.py:802
  229.1 7.1 %attn_weight.2 = (bf16[2,144,1152]{2,1,0:T(8,128)(2,1)}, bf16[2,144,1152]{2,1,0:T(8,128)(2,1)}, bf16[2,144,1152]{2,1,0:T(8,128)(2,1)}, bf16[2,144,1152]{2,1,0:T(8,128)(2,1)}) custom-call(bf16[1152,256]{1,0:T(8,128)(2,1)} %get-tuple-element.175.refs_0_, bf16[1152,256]{1,0:T(8,128)(2,1)} %get-tuple-element.155.refs_1_, ...), custom_call_target="tpu_custom_call" | custom-call | flops 1000 | bytes 100 | tf_op jit(solution)/shard_map/attn_weight/pallas_call | solution.py:780
  239.2 7.0 %attn_weight.3 = (bf16[2,144,1152]{2,1,0:T(8,128)(2,1)}, bf16[2,144,1152]{2,1,0:T(8,128)(2,1)}, bf16[2,144,1152]{2,1,0:T(8,128)(2,1)}, bf16[2,144,1152]{2,1,0:T(8,128)(2,1)}) custom-call(bf16[1152,256]{1,0:T(8,128)(2,1)} %get-tuple-element.175.refs_0_, bf16[1152,256]{1,0:T(8,128)(2,1)} %get-tuple-element.155.refs_1_, ...), custom_call_target="tpu_custom_call" | custom-call | flops 1000 | bytes 100 | tf_op jit(solution)/shard_map/attn_weight/pallas_call | solution.py:780
  246.2 13.1 %qkv_backward.1 = (bf16[256,1152]{1,0:T(8,128)(2,1)}, f32[2,2,1152]{2,1,0:T(2,128)}) custom-call(bf16[256,1152]{1,0:T(8,128)(2,1)} %bitcast.65, f32[2,6,1152]{2,1,0:T(8,128)} %copy-done.32, f32[256,1152]{1,0:T(8,128)} %get-tuple-element.178.refs_2_, bf16[8,256,512]{2,1,0:T(8,128)(2,1)} %attn_backward.1.refs_2_.refs_3_, bf16[1,144,1152]{2,1,0:T(8,128)(2,1)} %bitcast.67, ...), custom_call_target="tpu_custom_call" | custom-call | flops 1000 | bytes 100 | tf_op jit(solution)/shard_map/qkv_backward/pallas_call | solution.py:780
  263.3 6.5 %all-to-all-start.3 = ((f32[32,16,128]{2,1,0:T(8,128)}), f32[32,16,128]{2,1,0:T(8,128)S(1)}, u32[]{:S(2)}, u32[]{:S(2)}) async-start(f32[32,16,128]{2,1,0:T(8,128)} %bitcast.29), calls=%async_computation.3 | async-start | bytes 524288 | tf_op jit(solution)/shard_map/all_to_all | solution.py:809
  273.4 12.7 %collective-permute-done.36 = bf16[144,1152]{1,0:T(8,128)(2,1)S(1)} collective-permute-done((bf16[144,1152]{1,0:T(8,128)(2,1)S(1)}, bf16[144,1152]{1,0:T(8,128)(2,1)S(1)}, u32[]{:S(2)}, u32[]{:S(2)}) %collective-permute-start.36) | collective-permute-done | bytes 331808 | tf_op jit(solution)/shard_map/ppermute | solution.py:802
  286.9 10.2 %collective-permute-done.37 = bf16[144,1152]{1,0:T(8,128)(2,1)S(1)} collective-permute-done((bf16[144,1152]{1,0:T(8,128)(2,1)S(1)}, bf16[144,1152]{1,0:T(8,128)(2,1)S(1)}, u32[]{:S(2)}, u32[]{:S(2)}) %collective-permute-start.37) | collective-permute-done | bytes 331808 | tf_op jit(solution)/shard_map/ppermute | solution.py:802
  311.5 3.6 %all-to-all-start.4 = ((bf16[4,2,144,288]{3,2,1,0:T(8,128)(2,1)}), bf16[4,2,144,288]{3,2,1,0:T(8,128)(2,1)S(1)}, u32[]{:S(2)}, u32[]{:S(2)}) async-start(bf16[4,2,144,288]{3,2,1,0:T(8,128)(2,1)} %cut_rows.1), calls=%async_computation.5 | async-start | bytes 1769472 | tf_op jit(solution)/shard_map/all_to_all | solution.py:1083
  321.3 6.5 %all-to-all-done.4.back = bf16[4,2,144,288]{3,2,1,0:T(8,128)(2,1)S(1)} async-done(((bf16[4,2,144,288]{3,2,1,0:T(8,128)(2,1)}), bf16[4,2,144,288]{3,2,1,0:T(8,128)(2,1)S(1)}, u32[]{:S(2)}, u32[]{:S(2)}) %all-to-all-start.4) | async-done | bytes 663584 | tf_op jit(solution)/shard_map/all_to_all | solution.py:1083
  331.5 5.2 %collective-permute-done.43.refs_4_ = bf16[144,1152]{1,0:T(8,128)(2,1)} collective-permute-done((bf16[144,1152]{1,0:T(8,128)(2,1)}, bf16[144,1152]{1,0:T(8,128)(2,1)}, u32[]{:S(2)}, u32[]{:S(2)}) %collective-permute-start.43) | collective-permute-done | bytes 331808 | tf_op jit(solution)/shard_map/ppermute | solution.py:802
  (226 shorter events, 94.7 us)
Async XLA Ops:
  13.0 32.6 %all-to-all-start = ((bf16[4,304,288]{1,2,0:T(8,128)(2,1)}), bf16[4,304,288]{1,2,0:T(8,128)(2,1)S(1)}, u32[]{:S(2)}, u32[]{:S(2)}) async-start(bf16[4,304,288]{1,2,0:T(8,128)(2,1)} %copy.24), calls=%async_computation | async-start | bytes 1769472 | tf_op jit(solution)/shard_map/all_to_all | solution.py:864
  17.3 132.2 %all-gather.2.cloned.1.call-start = ((), (), s32[]{:S(2)}) async-start(), calls=%async_computation.6 | async-start | bytes 5971968 | tf_op jit(solution)/shard_map/all_gather | solution.py:868
  19.8 25.8 %collective-permute-start.1 = (bf16[1,144,1152]{2,1,0:T(8,128)(2,1)S(1)}, bf16[1,144,1152]{2,1,0:T(8,128)(2,1)S(1)}, u32[]{:S(2)}, u32[]{:S(2)}) collective-permute-start(bf16[1,144,1152]{2,1,0:T(8,128)(2,1)S(1)} %bitcast.69), channel_id=1, source_target_pairs={{0,16},{1,17},{2,18},{3,19},{4,20},{5,21},{6,22},{7,23},{8,24},{9,... | collective-permute-start | bytes 995336 | tf_op jit(solution)/shard_map/ppermute | solution.py:802
  49.4 32.8 %collective-permute-start.11 = (bf16[3,144,1152]{2,1,0:T(8,128)(2,1)S(1)}, bf16[3,144,1152]{2,1,0:T(8,128)(2,1)S(1)}, u32[]{:S(2)}, u32[]{:S(2)}) collective-permute-start(bf16[3,144,1152]{2,1,0:T(8,128)(2,1)S(1)} %constant_dynamic-update-slice_fusion.refs_6_.refs_7_), channel_id=1, source_target_pairs={{0,1},{1,0},{2,3},{3,2},{4,5},{5,4},{6,7},{7,6},{8,9},{9,8},{10,11... | collective-permute-start | bytes 2985992 | tf_op jit(solution)/shard_map/ppermute | solution.py:802
  49.5 32.7 %collective-permute-start.6 = (bf16[3,144,1152]{2,1,0:T(8,128)(2,1)S(1)}, bf16[3,144,1152]{2,1,0:T(8,128)(2,1)}, u32[]{:S(2)}, u32[]{:S(2)}) collective-permute-start(bf16[3,144,1152]{2,1,0:T(8,128)(2,1)S(1)} %constant_dynamic-update-slice_fusion.refs_6_.refs_7_), channel_id=1, source_target_pairs={{0,4},{1,5},{2,6},{3,7},{4,0},{5,1},{6,2},{7,3},{8,12},{9,13},{10,... | collective-permute-start | bytes 2985992 | tf_op jit(solution)/shard_map/ppermute | solution.py:802
  51.0 31.2 %collective-permute-start.7 = (bf16[3,144,1152]{2,1,0:T(8,128)(2,1)S(1)}, bf16[3,144,1152]{2,1,0:T(8,128)(2,1)}, u32[]{:S(2)}, u32[]{:S(2)}) collective-permute-start(bf16[3,144,1152]{2,1,0:T(8,128)(2,1)S(1)} %constant_dynamic-update-slice_fusion.refs_6_.refs_7_), channel_id=1, source_target_pairs={{0,2},{1,3},{2,0},{3,1},{4,6},{5,7},{6,4},{7,5},{8,10},{9,11},{10,... | collective-permute-start | bytes 2985992 | tf_op jit(solution)/shard_map/ppermute | solution.py:802
  52.9 29.3 %collective-permute-start.9 = (bf16[1,144,1152]{2,1,0:T(8,128)(2,1)S(1)}, bf16[1,144,1152]{2,1,0:T(8,128)(2,1)}, u32[]{:S(2)}, u32[]{:S(2)}) collective-permute-start(bf16[1,144,1152]{2,1,0:T(8,128)(2,1)S(1)} %collective-permute-done.3.refs_4_.refs_5_), channel_id=1, source_target_pairs={{0,1},{1,0},{2,3},{3,2},{4,5},{5,4},{6,7},{7,6},{8,9},{9,8},{10,11... | collective-permute-start | bytes 995336 | tf_op jit(solution)/shard_map/ppermute | solution.py:802
  55.7 26.5 %collective-permute-start.10 = (bf16[1,144,1152]{2,1,0:T(8,128)(2,1)}, bf16[1,144,1152]{2,1,0:T(8,128)(2,1)S(1)}, u32[]{:S(2)}, u32[]{:S(2)}) collective-permute-start(bf16[1,144,1152]{2,1,0:T(8,128)(2,1)} %collective-permute-done.4.refs_5_.refs_6_), channel_id=1, source_target_pairs={{0,1},{1,0},{2,3},{3,2},{4,5},{5,4},{6,7},{7,6},{8,9},{9,8},{10,11... | collective-permute-start | bytes 995336 | tf_op jit(solution)/shard_map/ppermute | solution.py:802
  82.2 33.9 %collective-permute-start.12 = (bf16[3,144,1152]{2,1,0:T(8,128)(2,1)}, bf16[3,144,1152]{2,1,0:T(8,128)(2,1)}, u32[]{:S(2)}, u32[]{:S(2)}) collective-permute-start(bf16[3,144,1152]{2,1,0:T(8,128)(2,1)} %collective-permute-done.6.refs_7_.refs_8_), channel_id=1, source_target_pairs={{0,2},{1,3},{2,0},{3,1},{4,6},{5,7},{6,4},{7,5},{8,10},{9,11},{10,... | collective-permute-start | bytes 2985992 | tf_op jit(solution)/shard_map/ppermute | solution.py:802
  84.2 32.0 %collective-permute-start.13 = (bf16[3,144,1152]{2,1,0:T(8,128)(2,1)}, bf16[3,144,1152]{2,1,0:T(8,128)(2,1)}, u32[]{:S(2)}, u32[]{:S(2)}) collective-permute-start(bf16[3,144,1152]{2,1,0:T(8,128)(2,1)} %collective-permute-done.6.refs_7_.refs_8_), channel_id=1, source_target_pairs={{0,1},{1,0},{2,3},{3,2},{4,5},{5,4},{6,7},{7,6},{8,9},{9,8},{10,11... | collective-permute-start | bytes 2985992 | tf_op jit(solution)/shard_map/ppermute | solution.py:802
  84.2 32.0 %collective-permute-start.14 = (bf16[3,144,1152]{2,1,0:T(8,128)(2,1)}, bf16[3,144,1152]{2,1,0:T(8,128)(2,1)}, u32[]{:S(2)}, u32[]{:S(2)}) collective-permute-start(bf16[3,144,1152]{2,1,0:T(8,128)(2,1)} %collective-permute-done.7.refs_8_.refs_9_), channel_id=1, source_target_pairs={{0,1},{1,0},{2,3},{3,2},{4,5},{5,4},{6,7},{7,6},{8,9},{9,8},{10,11... | collective-permute-start | bytes 2985992 | tf_op jit(solution)/shard_map/ppermute | solution.py:802
  89.0 26.1 %all-to-all-start.2 = ((f32[32,16,128]{2,1,0:T(8,128)}), f32[32,16,128]{2,1,0:T(8,128)S(1)}, u32[]{:S(2)}, u32[]{:S(2)}) async-start(f32[32,16,128]{2,1,0:T(8,128)} %bitcast.76), calls=%async_computation.2 | async-start | bytes 524288 | tf_op jit(solution)/shard_map/all_to_all | solution.py:809
  97.9 211.3 %reduce-scatter.2.cloned.1.call-start = ((), (), s32[]{:S(2)}) async-start(), calls=%async_computation.7 | async-start | bytes 5971968 | tf_op jit(solution)/shard_map/reduce_scatter | solution.py:1002
  117.4 27.0 %collective-permute-start.19 = (bf16[256,1152]{1,0:T(8,128)(2,1)S(1)}, bf16[256,1152]{1,0:T(8,128)(2,1)S(1)}, u32[]{:S(2)}, u32[]{:S(2)}) collective-permute-start(bf16[256,1152]{1,0:T(8,128)(2,1)S(1)} %fusion.refs_2_.refs_4_), channel_id=1, source_target_pairs={{0,1},{1,0},{2,3},{3,2},{4,5},{5,4},{6,7},{7,6},{8,9},{9,8},{10,11... | collective-permute-start | bytes 1769480 | tf_op jit(solution)/shard_map/ppermute | solution.py:802
  117.5 26.8 %collective-permute-start.21 = (bf16[256,1152]{1,0:T(8,128)(2,1)S(1)}, bf16[256,1152]{1,0:T(8,128)(2,1)S(1)}, u32[]{:S(2)}, u32[]{:S(2)}) collective-permute-start(bf16[256,1152]{1,0:T(8,128)(2,1)S(1)} %fusion.refs_2_.refs_4_), channel_id=1, source_target_pairs={{0,2},{1,3},{2,0},{3,1},{4,6},{5,7},{6,4},{7,5},{8,10},{9,11},{10,... | collective-permute-start | bytes 1769480 | tf_op jit(solution)/shard_map/ppermute | solution.py:802
  236.2 33.6 %collective-permute-start.33 = (bf16[2,144,1152]{2,1,0:T(8,128)(2,1)}, bf16[2,144,1152]{2,1,0:T(8,128)(2,1)}, u32[]{:S(2)}, u32[]{:S(2)}) collective-permute-start(bf16[2,144,1152]{2,1,0:T(8,128)(2,1)} %get-tuple-element.182), channel_id=1, source_target_pairs={{0,2},{1,3},{2,0},{3,1},{4,6},{5,7},{6,4},{7,5},{8,10},{9,11},{10,... | collective-permute-start | bytes 1990664 | tf_op jit(solution)/shard_map/ppermute | solution.py:802
  236.8 36.1 %collective-permute-start.35 = (bf16[2,144,1152]{2,1,0:T(8,128)(2,1)}, bf16[2,144,1152]{2,1,0:T(8,128)(2,1)S(1)}, u32[]{:S(2)}, u32[]{:S(2)}) collective-permute-start(bf16[2,144,1152]{2,1,0:T(8,128)(2,1)} %get-tuple-element.188), channel_id=1, source_target_pairs={{0,2},{1,3},{2,0},{3,1},{4,6},{5,7},{6,4},{7,5},{8,10},{9,11},{10,... | collective-permute-start | bytes 1990664 | tf_op jit(solution)/shard_map/ppermute | solution.py:802
  260.1 37.9 %collective-permute-start.38 = (bf16[2,144,1152]{2,1,0:T(8,128)(2,1)}, bf16[2,144,1152]{2,1,0:T(8,128)(2,1)}, u32[]{:S(2)}, u32[]{:S(2)}) collective-permute-start(bf16[2,144,1152]{2,1,0:T(8,128)(2,1)} %get-tuple-element.192), channel_id=1, source_target_pairs={{0,2},{1,3},{2,0},{3,1},{4,6},{5,7},{6,4},{7,5},{8,10},{9,11},{10,... | collective-permute-start | bytes 1990664 | tf_op jit(solution)/shard_map/ppermute | solution.py:802
  260.8 40.5 %collective-permute-start.34 = (bf16[2,144,1152]{2,1,0:T(8,128)(2,1)}, bf16[2,144,1152]{2,1,0:T(8,128)(2,1)}, u32[]{:S(2)}, u32[]{:S(2)}) collective-permute-start(bf16[2,144,1152]{2,1,0:T(8,128)(2,1)} %get-tuple-element.185), channel_id=1, source_target_pairs={{0,2},{1,3},{2,0},{3,1},{4,6},{5,7},{6,4},{7,5},{8,10},{9,11},{10,... | collective-permute-start | bytes 1990664 | tf_op jit(solution)/shard_map/ppermute | solution.py:802
  263.3 48.2 %all-to-all-start.3 = ((f32[32,16,128]{2,1,0:T(8,128)}), f32[32,16,128]{2,1,0:T(8,128)S(1)}, u32[]{:S(2)}, u32[]{:S(2)}) async-start(f32[32,16,128]{2,1,0:T(8,128)} %bitcast.29), calls=%async_computation.3 | async-start | bytes 524288 | tf_op jit(solution)/shard_map/all_to_all | solution.py:809
  273.1 24.1 %collective-permute-start.37 = (bf16[144,1152]{1,0:T(8,128)(2,1)S(1)}, bf16[144,1152]{1,0:T(8,128)(2,1)S(1)}, u32[]{:S(2)}, u32[]{:S(2)}) collective-permute-start(bf16[144,1152]{1,0:T(8,128)(2,1)S(1)} %get-tuple-element.205), channel_id=1, source_target_pairs={{0,4},{1,5},{2,6},{3,7},{4,0},{5,1},{6,2},{7,3},{8,12},{9,13},{10,... | collective-permute-start | bytes 995336 | tf_op jit(solution)/shard_map/ppermute | solution.py:802
  303.5 28.0 %collective-permute-start.40 = (bf16[144,1152]{1,0:T(8,128)(2,1)}, bf16[144,1152]{1,0:T(8,128)(2,1)}, u32[]{:S(2)}, u32[]{:S(2)}) collective-permute-start(bf16[144,1152]{1,0:T(8,128)(2,1)} %get-tuple-element.201), channel_id=1, source_target_pairs={{0,4},{1,5},{2,6},{3,7},{4,0},{5,1},{6,2},{7,3},{8,12},{9,13},{10,... | collective-permute-start | bytes 995336 | tf_op jit(solution)/shard_map/ppermute | solution.py:802
  304.4 27.0 %collective-permute-start.42 = (bf16[144,1152]{1,0:T(8,128)(2,1)}, bf16[144,1152]{1,0:T(8,128)(2,1)}, u32[]{:S(2)}, u32[]{:S(2)}) collective-permute-start(bf16[144,1152]{1,0:T(8,128)(2,1)} %add_convert_fusion.5), channel_id=1, source_target_pairs={{0,16},{1,17},{2,18},{3,19},{4,20},{5,21},{6,22},{7,23},{8,24},{9,... | collective-permute-start | bytes 995336 | tf_op jit(solution)/shard_map/ppermute | solution.py:802
  307.9 23.6 %collective-permute-start.41 = (bf16[144,1152]{1,0:T(8,128)(2,1)}, bf16[144,1152]{1,0:T(8,128)(2,1)}, u32[]{:S(2)}, u32[]{:S(2)}) collective-permute-start(bf16[144,1152]{1,0:T(8,128)(2,1)} %add_convert_fusion.6), channel_id=1, source_target_pairs={{0,24},{1,25},{2,26},{3,27},{4,28},{5,29},{6,30},{7,31},{8,16},{9,... | collective-permute-start | bytes 995336 | tf_op jit(solution)/shard_map/ppermute | solution.py:802
  (69 other events, 684.4 us)
Sparse Core Ops, SparseCore 0:
  49.4 100.0 all-gather.1
  197.8 110.4 reduce-scatter.1
